TPU v7x, 256 devices: a whole 4x4x8 slice. The times are simulated.
256 devices in a mesh: dp: 16 (over y_lo, z), seq: 16 (over x, y_hi, core).
Axes of the slice: x: 4, y: 4 (y_hi: 2, y_lo: 2; y = y_hi * 2 + y_lo), z: 8, core: 2. Of those that a mesh axis runs over, the one named last changes fastest.
Arguments:
- q_in: bfloat16 [16, 2048, 1024], P('dp', 'seq'), may hold values from -6 to 6
- k_in: bfloat16 [16, 2048, 512], P('dp', 'seq'), may hold values from -6 to 6
- v_in: bfloat16 [16, 2048, 512], P('dp', 'seq'), may hold values from -6 to 6
- q_gain: float32 [128], replicated, may hold values from 0.7 to 5
- k_gain: float32 [128], replicated, may hold values from 0.7 to 5
- seg_ids: int32 [16, 2048], P('dp'), may hold values from 0 to 3, never falling along the last dimension, each value on 1 to 1536 neighbouring positions
- teacher: bfloat16 [16, 7168, 2048], P('dp', 'seq'), may hold values from -6 to 6
- mapping: bfloat16 [7168, 1024], P('seq'), may hold values from -0.0625 to 0.0625
Outputs:
- dq_in: bfloat16 [16, 2048, 1024], P('dp', 'seq')
- dk_in: bfloat16 [16, 2048, 512], P('dp', 'seq')
- dv_in: bfloat16 [16, 2048, 512], P('dp', 'seq')
- q_gain_grad: float32 [128], replicated
- key_gain_gradient: float32 [128], replicated
Inputs may be any that keep to these rules, and one draw needn't show every extreme that they name: `seg_ids`: segment numbers never fall along a sequence; each of the 4 documents has 1 to 1536 tokens, one exactly 1536.
All inputs are finite; a program needn't handle non-finite values.
Results may differ from a plain program's by a relative error of at most 0.035.
The roundings to bfloat16 on the way count: a program that leaves them out, or rounds other values in their place, can miss the bound.
Values may be sent and summed in bfloat16 or wider, within the bound.
No kernel may reach another device: no remote copies, remote signals or barrier semaphores. Data moves between devices by JAX's collectives and lax.ppermute only.
A program may use at most 64 MiB of HBM per device.

v0:
```python
import math

import jax
import jax.numpy as jnp
from jax import lax
from jax.sharding import PartitionSpec as P

epsilon = 1e-06


def apply_norm_scale(value_rows):
    scale_rows = lax.rsqrt(jnp.mean(value_rows * value_rows, axis=-1, keepdims=True) + epsilon)
    return (value_rows * scale_rows, scale_rows)


def norm_backward(grad_hat, unit, scale_rows, gain):
    grad_unit = grad_hat * gain
    return scale_rows * (grad_unit - unit * jnp.mean(grad_unit * unit, axis=-1, keepdims=True))


def on_device(q_in, k_in, v_in, q_gain, k_gain, seg_ids, teacher, mapping):
    tok_rows = q_in.shape[1]
    head_size = q_gain.shape[0]
    q_heads = q_in.shape[2] // head_size
    kv_heads = k_in.shape[2] // head_size
    heads_per_group = q_heads // kv_heads
    seq_count = lax.axis_size("seq")
    seq_length = tok_rows * seq_count
    factor = head_size ** (-0.5)
    seq_place = lax.axis_index("seq")
    start_row = seq_place * tok_rows
    teacher_slab = teacher[0]
    target_outputs = lax.psum_scatter(
        lax.dot_general(
            teacher_slab, mapping, (((0,), (0,)), ((), ())), preferred_element_type=jnp.float32
        ).astype(jnp.bfloat16),
        "seq",
        scatter_dimension=0,
        tiled=True,
    ).astype(jnp.float32)
    query_unit_rows, query_norm_scale = apply_norm_scale(
        q_in[0].astype(jnp.float32).reshape(tok_rows, kv_heads, heads_per_group, head_size)
    )
    key_unit_rows, key_norm_scale = apply_norm_scale(
        k_in[0].astype(jnp.float32).reshape(tok_rows, kv_heads, head_size)
    )
    q_hat = (query_unit_rows * q_gain).astype(jnp.bfloat16)
    k_hat = (key_unit_rows * k_gain).astype(jnp.bfloat16).reshape(tok_rows, kv_heads * head_size)
    value_rows = v_in[0]
    segs_all = seg_ids[0]
    my_segs = lax.dynamic_slice_in_dim(segs_all, start_row, tok_rows, 0)
    my_pos = start_row + jnp.arange(tok_rows, dtype=jnp.int32)
    target_row_block = target_outputs.reshape(tok_rows, kv_heads, heads_per_group, head_size)

    def allowed_keys(row_count):
        key_pos = jnp.arange(row_count, dtype=jnp.int32)
        return (key_pos[None, :] <= my_pos[:, None]) & (segs_all[None, :] == my_segs[:, None])

    def block_scores(key_block):
        key_heads = key_block.reshape(key_block.shape[0], kv_heads, head_size)
        return (
            jnp.einsum("tjgd,sjd->jgts", q_hat, key_heads, preferred_element_type=jnp.float32)
            * factor
        )

    stat_shape = (kv_heads, heads_per_group, tok_rows)
    key_block = lax.all_gather(k_hat, "seq", axis=0, tiled=True)
    row_max = jnp.full(stat_shape, -1e30, jnp.float32)
    allowed = allowed_keys(key_block.shape[0])[None, None]
    scores = block_scores(key_block)
    max_next = jnp.maximum(row_max, jnp.max(jnp.where(allowed, scores, -1e30), axis=-1))
    fresh = jnp.sum(jnp.where(allowed, jnp.exp(scores - max_next[..., None]), 0.0), axis=-1)
    log_total = max_next + jnp.log(fresh)

    def block_probs(key_block):
        allowed = allowed_keys(key_block.shape[0])[None, None]
        return jnp.where(allowed, jnp.exp(block_scores(key_block) - log_total[..., None]), 0.0)

    key_block = lax.all_gather(k_hat, "seq", axis=0, tiled=True)
    value_block = lax.all_gather(value_rows, "seq", axis=0, tiled=True)
    probs_low = block_probs(key_block).astype(jnp.bfloat16)
    value_heads = value_block.reshape(value_block.shape[0], kv_heads, head_size)
    outputs = jnp.einsum(
        "jgts,sjd->tjgd", probs_low, value_heads, preferred_element_type=jnp.float32
    )
    errors = outputs - target_row_block
    d_out = errors.astype(jnp.bfloat16)
    row_delta = jnp.transpose(jnp.sum(d_out.astype(jnp.float32) * outputs, axis=-1), (1, 2, 0))
    key_block = lax.all_gather(k_hat, "seq", axis=0, tiled=True)
    value_block = lax.all_gather(value_rows, "seq", axis=0, tiled=True)
    row_count = key_block.shape[0]
    probs = block_probs(key_block)
    probs_low = probs.astype(jnp.bfloat16)
    key_heads = key_block.reshape(row_count, kv_heads, head_size)
    value_heads = value_block.reshape(row_count, kv_heads, head_size)
    d_probs = jnp.einsum("tjgd,sjd->jgts", d_out, value_heads, preferred_element_type=jnp.float32)
    d_scores = (factor * probs * (d_probs - row_delta[..., None])).astype(jnp.bfloat16)
    d_query = jnp.einsum("jgts,sjd->tjgd", d_scores, key_heads, preferred_element_type=jnp.float32)
    key_piece = jnp.einsum(
        "jgts,tjgd->sjd", d_scores, q_hat, preferred_element_type=jnp.float32
    ).reshape(row_count, kv_heads * head_size)
    value_piece = jnp.einsum(
        "jgts,tjgd->sjd", probs_low, d_out, preferred_element_type=jnp.float32
    ).reshape(row_count, kv_heads * head_size)
    key_term = key_piece
    value_term = value_piece
    d_query, key_term, value_term = (d_query, key_term, value_term)
    key_own, value_own = (
        lax.psum_scatter(
            key_term.astype(jnp.bfloat16), "seq", scatter_dimension=0, tiled=True
        ).astype(jnp.float32),
        lax.psum_scatter(
            value_term.astype(jnp.bfloat16), "seq", scatter_dimension=0, tiled=True
        ).astype(jnp.float32),
    )
    d_key = key_own.reshape(tok_rows, kv_heads, head_size)
    dq_rows = norm_backward(d_query, query_unit_rows, query_norm_scale, q_gain)
    dk_rows = norm_backward(d_key, key_unit_rows, key_norm_scale, k_gain)
    q_part = jnp.sum(d_query * query_unit_rows, axis=(0, 1, 2))
    k_part = jnp.sum(d_key * key_unit_rows, axis=(0, 1))
    q_total, k_total = lax.psum((q_part, k_part), ("dp", "seq"))
    doc_count = lax.axis_size("dp")
    q_gain_grad = q_total * (1.0 / math.sqrt(doc_count * seq_length * q_heads))
    key_gain_gradient = k_total * (1.0 / math.sqrt(doc_count * seq_length * kv_heads))
    dq_out = dq_rows.reshape(1, tok_rows, q_heads * head_size).astype(jnp.bfloat16)
    dk_out = dk_rows.reshape(1, tok_rows, kv_heads * head_size).astype(jnp.bfloat16)
    dv_out = value_own.reshape(1, tok_rows, kv_heads * head_size).astype(jnp.bfloat16)
    return (dq_out, dk_out, dv_out, q_gain_grad, key_gain_gradient)


def solution(mesh):
    return jax.shard_map(
        on_device,
        mesh=mesh,
        in_specs=(
            P("dp", "seq", None),
            P("dp", "seq", None),
            P("dp", "seq", None),
            P(),
            P(),
            P("dp", None),
            P("dp", "seq", None),
            P("seq", None),
        ),
        out_specs=(P("dp", "seq", None), P("dp", "seq", None), P("dp", "seq", None), P(), P()),
        check_vma=False,
    )
```

profile of v0, /device:TPU:32, one launch (start us, length us, event | category | flops | bytes accessed | tf_op | source)
XLA Modules:
  0.0 402.3 jit_solution(16938926505897569122)
XLA Ops:
  7.2 0.0 copy-start
  7.2 0.0 all-gather.6.cloned.1.call-start
  7.2 0.7 all-gather.6.cloned.1.call-update
  7.9 0.0 all-gather.4.cloned.1.call-start
  8.0 1.0 copy.61
  9.0 0.7 broadcast_bitcast_fusion
  9.7 0.8 multiply_convert_fusion.2
  10.5 0.0 all-gather.4.cloned.1.call-update
  10.5 0.0 copy-start.5
  10.5 0.0 copy-start.7
  10.5 0.0 reduce-scatter.6.cloned.1.call-start
  10.6 0.0 copy-done
  10.6 5.6 %convolution_convert_fusion = bf16[2048,1024]{1,0:T(8,128)(2,1)} fusion(bf16[448,1024]{1,0:T(8,128)(2,1)} %param.15, bf16[1,448,2048]{2,1,0:T(8,128)(2,1)S(1)} %copy-done), kind=kOutput, calls=%fused_computation.15 | convolution fusion | flops 1881145344 | bytes 6946816 | tf_op jit(solution)/shard_map/dot_general | solution.py:34
  16.2 0.0 copy-start.6
  16.2 0.0 reduce-scatter.6.cloned.1.call-update
  16.2 0.0 reduce-scatter.10.cloned.1.call-start
  16.2 0.0 copy-done.5
  16.3 0.1 copy.60
  16.4 0.0 copy-done.7
  16.4 0.1 multiply_reduce_fusion.3
  16.5 0.3 fusion.10
  16.9 50.0 %all-gather.6.cloned.1.call-done = bf16[1,2048,512]{2,1,0:T(8,128)(2,1)} async-done(((bf16[1,128,512]{2,1,0:T(8,128)(2,1)}), bf16[1,2048,512]{2,1,0:T(8,128)(2,1)}) %all-gather.6.cloned.1.call-update) | async-done | bytes 2097168 | tf_op jit(solution)/shard_map/all_gather | solution.py:90
  66.8 3.9 copy.64
  70.8 52.8 %all-gather.4.cloned.1.call-done = bf16[2048,512]{0,1:T(8,128)(2,1)} async-done(((bf16[128,512]{0,1:T(8,128)(2,1)}), bf16[2048,512]{0,1:T(8,128)(2,1)}) %all-gather.4.cloned.1.call-update) | async-done | bytes 2097168 | tf_op jit(solution)/shard_map/all_gather | solution.py:89
  123.5 0.0 copy-done.6
  123.5 3.2 fusion.2
  126.8 0.0 copy-start.1
  126.8 3.2 copy-done.1
  130.0 1.7 fusion.5
  131.7 0.6 log_add_fusion
  132.3 82.6 %reduce-scatter.6.cloned.1.call-done = bf16[128,1024]{1,0:T(8,128)(2,1)} async-done(((bf16[2048,1024]{1,0:T(8,128)(2,1)}), bf16[128,1024]{1,0:T(8,128)(2,1)}) %reduce-scatter.6.cloned.1.call-update) | async-done | bytes 262160 | tf_op jit(solution)/shard_map/reduce_scatter | solution.py:33
  214.9 1.1 copy.66
  216.0 0.0 copy-start.2
  216.0 0.0 copy-start.4
  216.0 0.0 copy-start.8
  216.0 5.8 %multiply_reduce_fusion.2 = (f32[128,4,2]{0,2,1:T(2,128)S(1)}, bf16[128,4,2,128]{0,3,2,1:T(8,128)(2,1)S(1)}) fusion(f32[128,4,2,128]{0,3,2,1:T(8,128)S(1)} %bitcast.131, bf16[2048,4,128,1]{0,2,3,1:T(8,128)(2,1)} %bitcast.126, f32[4,2048,128,2]{2,1,3,0:T(8,128)} %copy-done.1, f32[4,2,128]{2,1,0:T(2,128)} %log_add_fusion, pred[128,2048]{0,1:T(8,128)(4,1)S(1)} %fusion.10), kind=kOutput, calls=%fused_computation.24 | convolution fusion | flops 545913856 | bytes 11542528 | tf_op jit(solution)/shard_map/jgts,sjd->tjgd/dot_general | solution.py:83
  221.9 0.0 copy-start.11
  221.9 0.5 copy-done.2
  222.4 0.7 copy-done.4
  223.1 0.0 copy-done.8
  223.1 3.3 fusion.1
  226.4 0.0 copy-done.11
  226.4 0.0 copy-start.3
  226.4 2.0 copy-done.3
  228.4 2.8 bitcast_convert_fusion.1
  231.2 3.9 copy.93
  235.1 0.0 reduce-scatter.10.cloned.1.call-update
  235.1 0.2 reduce-scatter.8.cloned.1.call-start
  235.4 0.0 copy-done.9
  235.4 6.7 %bitcast_convert_fusion = bf16[4,128,2048]{2,1,0:T(8,128)(2,1)} fusion(bf16[128,4,2,128]{0,3,2,1:T(8,128)(2,1)} %copy-done.11, f32[4,2048,128,2]{2,1,3,0:T(8,128)} %copy-done.1, f32[4,2,128]{2,1,0:T(2,128)S(1)} %copy-done.9, pred[128,2048]{0,1:T(8,128)(4,1)S(1)} %fusion.10), kind=kOutput, calls=%fused_computation.13 | convolution fusion | flops 546308096 | bytes 11014144 | tf_op jit(solution)/shard_map/jgts,tjgd->sjd/dot_general | solution.py:102
  242.1 4.0 copy.73
  246.1 0.0 reduce-scatter.8.cloned.1.call-update
  246.1 3.9 multiply_reduce_fusion
  250.0 0.2 multiply_convert_fusion
  250.1 0.9 copy.74
  251.0 61.7 %reduce-scatter.10.cloned.1.call-done = bf16[128,512]{1,0:T(8,128)(2,1)} async-done(((bf16[2048,512]{1,0:T(8,128)(2,1)}), bf16[128,512]{1,0:T(8,128)(2,1)}) %reduce-scatter.10.cloned.1.call-update) | async-done | bytes 131088
  312.6 1.0 copy.94
  313.7 0.0 copy-done.10
  313.7 0.1 multiply_reduce_fusion.5
  313.8 0.3 multiply_reduce_fusion.4
  314.1 0.8 copy.75
  314.9 75.7 %all-reduce = (f32[128]{0:T(128)S(1)}, f32[128]{0:T(128)S(1)}) all-reduce(f32[128]{0:T(128)S(1)} %get-tuple-element.25, f32[128]{0:T(128)S(1)} %bitcast_reduce_fusion), channel_id=1, replica_groups=mesh['dp'=16,'seq'=16] {'dp','seq'}, use_global_device_ids=true, to_apply=%region_11.12 | all-reduce | flops 256 | bytes 2048 | tf_op jit(solution)/shard_map/psum | solution.py:121
  390.5 0.5 broadcast_multiply_fusion.2
  391.1 4.7 %reduce-scatter.8.cloned.1.call-done = bf16[128,512]{1,0:T(8,128)(2,1)} async-done(((bf16[2048,512]{1,0:T(8,128)(2,1)}), bf16[128,512]{1,0:T(8,128)(2,1)}) %reduce-scatter.8.cloned.1.call-update) | async-done | bytes 131088 | tf_op jit(solution)/shard_map/reduce_scatter | solution.py:112
  (11 shorter events, 0.1 us)
Async XLA Ops:
  7.2 3.4 copy-start
  7.2 59.6 %all-gather.6.cloned.1.call-start = ((), (), s32[]{:S(2)}) async-start(), calls=%async_computation.6 | async-start | bytes 2228224 | tf_op jit(solution)/shard_map/all_gather | solution.py:90
  7.9 115.6 %all-gather.4.cloned.1.call-start = ((), (), s32[]{:S(2)}) async-start(), calls=%async_computation.3 | async-start | bytes 2228224 | tf_op jit(solution)/shard_map/all_gather | solution.py:89
  10.5 5.7 %copy-start.5 = (bf16[1,128,1024]{2,1,0:T(8,128)(2,1)S(1)}, bf16[1,128,1024]{2,1,0:T(8,128)(2,1)}, u32[]{:S(2)}) copy-start(bf16[1,128,1024]{2,1,0:T(8,128)(2,1)} %param.8) | copy-start | bytes 786436
  10.5 5.9 %copy-start.7 = (s32[1,2048]{1,0:T(1,128)S(1)}, s32[1,2048]{1,0:T(1,128)}, u32[]{:S(2)}) copy-start(s32[1,2048]{1,0:T(1,128)} %param.13) | copy-start | bytes 24580
  10.5 204.4 %reduce-scatter.6.cloned.1.call-start = ((), (), s32[]{:S(2)}) async-start(), calls=%async_computation.4 | async-start | bytes 4456448 | tf_op jit(solution)/shard_map/reduce_scatter | solution.py:33
  16.2 107.4 %copy-start.6 = (f32[128]{0:T(128)S(1)}, f32[128]{0:T(128)}, u32[]{:S(2)}) copy-start(f32[128]{0:T(128)} %param.11) | copy-start | bytes 1540
  16.2 296.5 %reduce-scatter.10.cloned.1.call-start = ((), (), s32[]{:S(2)}) async-start(), calls=%async_computation.7 | async-start | bytes 2228224
  126.8 3.2 copy-start.1
  216.0 6.4 %copy-start.2 = (f32[4,2048,128,2]{2,1,3,0:T(8,128)S(1)}, f32[4,2048,128,2]{2,1,3,0:T(8,128)}, u32[]{:S(2)}) copy-start(f32[4,2048,128,2]{2,1,3,0:T(8,128)} %copy-done.1) | copy-start | bytes 25165828
  216.0 7.1 %copy-start.4 = (bf16[1,2048,512]{1,2,0:T(8,128)(2,1)S(1)}, bf16[1,2048,512]{1,2,0:T(8,128)(2,1)}, u32[]{:S(2)}) copy-start(bf16[1,2048,512]{1,2,0:T(8,128)(2,1)} %copy.64) | copy-start | bytes 6291460
  216.0 7.1 %copy-start.8 = (f32[4,2,128]{2,1,0:T(2,128)S(1)}, f32[4,2,128]{2,1,0:T(2,128)}, u32[]{:S(2)}) copy-start(f32[4,2,128]{2,1,0:T(2,128)} %log_add_fusion) | copy-start | bytes 12292
  221.9 4.5 %copy-start.11 = (bf16[128,4,2,128]{0,3,2,1:T(8,128)(2,1)}, bf16[128,4,2,128]{0,3,2,1:T(8,128)(2,1)S(1)}, u32[]{:S(2)}) copy-start(bf16[128,4,2,128]{0,3,2,1:T(8,128)(2,1)S(1)} %get-tuple-element.30) | copy-start | bytes 786436
  226.4 2.0 copy-start.3
  228.4 7.0 %copy-start.9 = (f32[4,2,128]{2,1,0:T(2,128)S(1)}, f32[4,2,128]{2,1,0:T(2,128)}, u32[]{:S(2)}) copy-start(f32[4,2,128]{2,1,0:T(2,128)} %log_add_fusion) | copy-start | bytes 12292
  235.1 160.6 %reduce-scatter.8.cloned.1.call-start = ((), (), s32[]{:S(2)}) async-start(), calls=%async_computation.5 | async-start | bytes 2228224 | tf_op jit(solution)/shard_map/reduce_scatter | solution.py:112
  242.1 71.6 %copy-start.10 = (f32[128]{0:T(128)S(1)}, f32[128]{0:T(128)}, u32[]{:S(2)}) copy-start(f32[128]{0:T(128)} %param.12) | copy-start | bytes 1540
Sparse Core Ops, SparseCore 0:
  10.7 56.0 all-gather.5
  69.9 53.5 all-gather.3
  127.9 86.9 reduce-scatter.5
  235.3 77.3 reduce-scatter.9
  317.9 77.8 reduce-scatter.7
where the time goes:
time: 403 us; the launch traced here: 402 us
  waiting for transfers between devices  252 us (63%)
  blocking collectives  75.7 us (19%)
  matrix products  31.3 us (8%)
  local copies, waits for them, and re-layouts  23.8 us (6%)
  between operations  14 us (3%)
  other arithmetic  4.68 us (1%)
    reduce_scatter x1, waiting for transfers between devices, on_device(): lax.psum_scatter(lax.dot_general(teacher_slab, mapping, (((0,), (0,)), ((...  82.6 us
    psum x1, blocking collectives, on_device(): q_total, k_total = lax.psum((q_part, k_part), ('dp', 'seq'))  75.7 us
    unnamed x6, waiting for transfers between devices  62.4 us
    all_gather x1, waiting for transfers between devices, on_device(): key_block = lax.all_gather(k_hat, 'seq', axis=0, tiled=True)  52.8 us
    all_gather x1, waiting for transfers between devices, on_device(): value_block = lax.all_gather(value_rows, 'seq', axis=0, tiled=True)  50 us
    unnamed x29, local copies, waits for them, and re-layouts  14 us
  transfers between devices with their start and end apart: 5, of which 5 were waited for; matrix products, arithmetic and copies ran while one was open for 9% of the time, Pallas kernels for 0%

commit v1 on v0

v1 whole, which is shorter than its diff:
```python
import functools
import math

import jax
import jax.numpy as jnp
from jax import lax
from jax.experimental import pallas as pl
from jax.experimental.pallas import tpu as pltpu
from jax.sharding import PartitionSpec as P


EPS = 1e-06
NEG = -1e30
HEAD = 128
BLK = 128
NX = 4
F32 = jnp.float32
BF16 = jnp.bfloat16
NT = (((1,), (1,)), ((), ()))
VMEM_LIMIT = 48 * 1024 * 1024


def index_of(x, y, c):
    return (x % 4) * 4 + (y % 2) * 2 + (c % 2)


def shift(value, dx, dy, dc):
    pairs = []
    for x in range(4):
        for y in range(2):
            for c in range(2):
                pairs.append((index_of(x, y, c), index_of(x + dx, y + dy, c + dc)))
    return lax.ppermute(value, "seq", pairs)


def flip(value, dp_bits, seq_bits):
    size = 256
    pairs = [(i, ((i // 16) ^ dp_bits) * 16 + ((i % 16) ^ seq_bits)) for i in range(size)]
    return lax.ppermute(value, ("dp", "seq"), pairs)


def sum_over_four(value, first, second):
    both = (first[0] ^ second[0], first[1] ^ second[1])
    a, b, c = (flip(value, *bits) for bits in (first, second, both))
    return (value + a) + (b + c)


def call(kernel, outs, coords, *args, scratch=(), specs=None, out_specs=None, grid=None, flops=0, moved=0):
    whole = pl.BlockSpec(memory_space=pltpu.VMEM)
    in_specs = specs if specs is not None else [whole] * len(args)
    out_specs = out_specs if out_specs is not None else [whole] * len(outs)
    return pl.pallas_call(
        kernel,
        out_shape=outs,
        grid_spec=pltpu.PrefetchScalarGridSpec(
            num_scalar_prefetch=1,
            grid=grid if grid is not None else (1,),
            in_specs=in_specs,
            out_specs=out_specs,
            scratch_shapes=list(scratch),
        ),
        compiler_params=pltpu.CompilerParams(vmem_limit_bytes=VMEM_LIMIT),
        cost_estimate=pl.CostEstimate(flops=flops, bytes_accessed=moved, transcendentals=0),
    )(coords, *args)


def sds(shape, dtype=BF16):
    return jax.ShapeDtypeStruct(shape, dtype)


def pack_kernel(at, q_ref, k_ref, v_ref, *outs):
    x = at[0]
    for dx in range(NX):
        to = (x + dx) % NX
        outs[dx][:, 0:256] = q_ref[:, pl.ds(pl.multiple_of(to * 256, 256), 256)]
        outs[dx][:, 256:384] = k_ref[:, pl.ds(pl.multiple_of(to * 128, 128), 128)]
        outs[dx][:, 384:512] = v_ref[:, pl.ds(pl.multiple_of(to * 128, 128), 128)]


def copy_kernel(at, a_ref, b_ref, out_ref):
    out_ref[:, 0:128] = a_ref[...]
    out_ref[:, 128:256] = b_ref[...]


def goal_kernel(is_first, at, map_a, map_b, own_0, own_1, other, *refs):
    outs, turned = refs[:-1], refs[-1]
    x = at[0]
    step = pl.program_id(0)

    @pl.when(step == 0)
    def _():
        for dx in range(NX):
            cols = pl.ds(pl.multiple_of(((x + dx) % NX) * 256, 256), 256)
            turned[dx, :, 0:448] = map_a[:, cols].T
            turned[dx, :, 512:960] = map_b[:, cols].T

    own = jnp.concatenate([own_0[...], own_1[...]], axis=1)
    for dx in range(NX):
        part = jnp.dot(turned[dx, :, 0:448], own, preferred_element_type=F32)
        part += jnp.dot(turned[dx, :, 512:960], other[...], preferred_element_type=F32)
        part = part.astype(BF16)
        if is_first:
            outs[dx][0] = part
        else:
            outs[0][0, dx] = part


def unit_rows(rows):
    scale = lax.rsqrt(jnp.mean(rows * rows, axis=-1, keepdims=True) + EPS)
    return rows * scale, scale


def forward_kernel(
    at, kv_0, kv_y, kv_c, kv_yc, q_0, q_1, q_2, q_3, spans, q_gain, k_gain,
    k_hat, k_turned, v_all, k_unit, q_hat, outputs, log_total, s_ref, v_turned,
):
    x, y, c = at[0], at[1], at[2]
    for part, dy, dc in ((kv_0, 0, 0), (kv_y, 1, 0), (kv_c, 0, 1), (kv_yc, 1, 1)):
        for dx in range(NX):
            block = ((x + NX - dx) % NX) * 4 + ((y + dy) % 2) * 2 + (c + dc) % 2
            rows = pl.ds(pl.multiple_of(block * BLK, BLK), BLK)
            unit, _ = unit_rows(part[dx, :, 0:128].astype(F32))
            hat = (unit * k_gain[...]).astype(BF16)
            k_unit[rows, :] = unit
            k_hat[rows, :] = hat
            k_turned[:, rows] = hat.T
            value = part[dx, :, 128:256]
            v_all[rows, :] = value
            v_turned[:, rows] = value.T
    for dx, part in enumerate((q_0, q_1, q_2, q_3)):
        i = (x + NX - dx) % NX
        for g in range(2):
            unit, _ = unit_rows(part[:, g * 128 : (g + 1) * 128].astype(F32))
            q_hat[i, g * 128 : (g + 1) * 128, :] = (unit * q_gain[...]).astype(BF16)
    factor = HEAD ** (-0.5)
    for i in range(NX):
        start = spans[i : i + 1, :]
        place = spans[4 + i : 5 + i, :]
        top = jnp.full((1, 256), NEG, F32)
        for j in range(2 * (i + 1)):
            rows = slice(256 * j, 256 * (j + 1))
            s = lax.dot_general(k_hat[rows, :], q_hat[i], NT, preferred_element_type=F32) * factor
            at_key = lax.broadcasted_iota(jnp.int32, (256, 256), 0) + 256 * j
            allowed = at_key >= start
            if j >= 2 * i:
                allowed = allowed & (at_key <= place)
            s = jnp.where(allowed, s, NEG)
            s_ref[rows, :] = s
            top = jnp.maximum(top, jnp.max(s, axis=0, keepdims=True))
        total = jnp.zeros((1, 256), F32)
        for j in range(2 * (i + 1)):
            rows = slice(256 * j, 256 * (j + 1))
            total += jnp.sum(jnp.exp(s_ref[rows, :] - top), axis=0, keepdims=True)
        log_row = top + jnp.log(total)
        log_total[i : i + 1, :] = log_row
        result = jnp.zeros((128, 256), F32)
        for j in range(2 * (i + 1)):
            rows = slice(256 * j, 256 * (j + 1))
            probs_low = jnp.exp(s_ref[rows, :] - log_row).astype(BF16)
            result += jnp.dot(v_turned[:, rows], probs_low, preferred_element_type=F32)
        outputs[i] = result


def backward_kernel(
    at, k_hat, k_turned, v_all, k_unit, q_hat, outputs, log_total, goal_a, goal_b,
    q_0, q_1, q_2, q_3, spans, q_gain, dq_0, dq_1, dq_2, dq_3, send_c, keep_c, gains,
    d_key, d_value, q_rows, dq_rows,
):
    x, y, c = at[0], at[1], at[2]
    factor = HEAD ** (-0.5)
    for dx, part in enumerate((q_0, q_1, q_2, q_3)):
        i = (x + NX - dx) % NX
        for g in range(2):
            q_rows[i, g * 128 : (g + 1) * 128, :] = part[:, g * 128 : (g + 1) * 128]
    q_part = jnp.zeros((1, 128), F32)
    for i in reversed(range(NX)):
        start = spans[i : i + 1, :]
        place = spans[4 + i : 5 + i, :]
        log_row = log_total[i : i + 1, :]
        goal = goal_a if i < 2 else goal_b
        lanes = slice(128 * (i % 2), 128 * (i % 2) + 128)
        goal = jnp.concatenate([goal[0:128, lanes], goal[128:256, lanes]], axis=1)
        out = outputs[i]
        d_out = (out - goal).astype(BF16)
        delta = jnp.sum(d_out.astype(F32) * out, axis=0, keepdims=True)
        d_out_rows = d_out.T
        query = q_hat[i]
        d_query = jnp.zeros((128, 256), F32)
        for j in range(2 * (i + 1)):
            rows = slice(256 * j, 256 * (j + 1))
            s = lax.dot_general(k_hat[rows, :], query, NT, preferred_element_type=F32) * factor
            at_key = lax.broadcasted_iota(jnp.int32, (256, 256), 0) + 256 * j
            allowed = at_key >= start
            if j >= 2 * i:
                allowed = allowed & (at_key <= place)
            probs = jnp.exp(jnp.where(allowed, s, NEG) - log_row)
            d_probs = jnp.dot(v_all[rows, :], d_out, preferred_element_type=F32)
            d_scores = (factor * probs * (d_probs - delta)).astype(BF16)
            new_value = jnp.dot(probs.astype(BF16), d_out_rows, preferred_element_type=F32)
            new_key = jnp.dot(d_scores, query, preferred_element_type=F32)
            if i == NX - 1:
                d_value[rows, :] = new_value
                d_key[rows, :] = new_key
            else:
                d_value[rows, :] += new_value
                d_key[rows, :] += new_key
            d_query += jnp.dot(k_turned[:, rows], d_scores, preferred_element_type=F32)
        unit, scale = unit_rows(q_rows[i].astype(F32))
        grad = d_query.T
        q_part += jnp.sum(grad * unit, axis=0, keepdims=True)
        grad_unit = grad * q_gain[...]
        dq = scale * (grad_unit - unit * jnp.mean(grad_unit * unit, axis=-1, keepdims=True))
        dq = dq.astype(BF16)
        dq_rows[i, :, 0:128] = dq[0:128]
        dq_rows[i, :, 128:256] = dq[128:256]
    for dx, out in enumerate((dq_0, dq_1, dq_2, dq_3)):
        out[...] = dq_rows[(x + dx) % NX]
    k_part = jnp.zeros((1, 128), F32)
    for j in range(8):
        rows = slice(256 * j, 256 * (j + 1))
        k_part += jnp.sum(d_key[rows, :] * k_unit[rows, :], axis=0, keepdims=True)
    gains[...] = jnp.concatenate([q_part, k_part, jnp.zeros((6, 128), F32)], axis=0)
    for out, dc in ((keep_c, 0), (send_c, 1)):
        for dy in range(2):
            for i in range(NX):
                block = i * 4 + ((y + dy) % 2) * 2 + (c + dc) % 2
                rows = pl.ds(pl.multiple_of(block * BLK, BLK), BLK)
                out[dy, i, :, 0:128] = d_key[rows, :].astype(BF16)
                out[dy, i, :, 128:256] = d_value[rows, :].astype(BF16)


def key_kernel(at, mine, from_y, kv_0, k_gain, out_0, out_1, out_2, out_3):
    x = at[0]
    for dx, out in enumerate((out_0, out_1, out_2, out_3)):
        i = (x + dx) % NX
        total = mine[i] + from_y[i].astype(F32)
        raw = kv_0[(NX - dx) % NX, :, 0:128].astype(F32)
        unit, scale = unit_rows(raw)
        grad_unit = total[:, 0:128] * k_gain[...]
        dk = scale * (grad_unit - unit * jnp.mean(grad_unit * unit, axis=-1, keepdims=True))
        out[:, 0:128] = dk.astype(BF16)
        out[:, 128:256] = total[:, 128:256].astype(BF16)


def unpack_kernel(at, q_0, q_1, q_2, q_3, kv_0, kv_1, kv_2, kv_3, dq, dk, dv):
    x = at[0]
    for dx, (q, kv) in enumerate(((q_0, kv_0), (q_1, kv_1), (q_2, kv_2), (q_3, kv_3))):
        j = (x + NX - dx) % NX
        dq[:, pl.ds(pl.multiple_of(j * 256, 256), 256)] = q[...]
        dk[:, pl.ds(pl.multiple_of(j * 128, 128), 128)] = kv[:, 0:128]
        dv[:, pl.ds(pl.multiple_of(j * 128, 128), 128)] = kv[:, 128:256]


def on_device(q_in, k_in, v_in, q_gain, k_gain, seg_ids, teacher, mapping):
    place = lax.axis_index("seq")
    x, y, c = place // 4, (place // 2) % 2, place % 2
    at = jnp.stack([x, y, c]).astype(jnp.int32)
    q_gain_row, k_gain_row = q_gain.reshape(1, HEAD), k_gain.reshape(1, HEAD)
    teacher_slab = teacher[0]
    whole = pl.BlockSpec(memory_space=pltpu.VMEM)

    half = [
        pl.BlockSpec(
            (448, 128),
            functools.partial(
                lambda i2, s, at: (0, 4 * (2 * (s // 2) + i2) + 2 * ((at[1] + s) % 2) + 1 - at[2]), i2
            ),
        )
        for i2 in range(2)
    ]
    teacher_out = call(
        copy_kernel, sds((448, 1024)), at, teacher_slab, teacher_slab,
        specs=half, out_specs=pl.BlockSpec((448, 256), lambda s, at: (0, s)), grid=(4,),
        moved=2 * 448 * 1024 * 2,
    )
    packed = call(
        pack_kernel, [sds((BLK, 512))] * NX, at, q_in[0], k_in[0], v_in[0], moved=2 * BLK * 2048 * 2
    )
    mapping_other = shift(mapping, 0, 0, 1)
    teacher_other = shift(teacher_out, 0, 0, 1)
    pieces = [packed[0]] + [shift(packed[dx], dx, 0, 0) for dx in (1, 3, 2)]
    pieces = [pieces[0], pieces[1], pieces[3], pieces[2]]

    def goal_parts(first):
        base = 0 if first else 2
        own = [
            pl.BlockSpec(
                (448, 128),
                functools.partial(
                    lambda i2, s, at: (0, 4 * (base + i2) + 2 * ((at[1] + s) % 2) + at[2]), i2
                ),
            )
            for i2 in range(2)
        ]
        specs = [whole, whole, *own, pl.BlockSpec((448, 256), lambda s, at: (0, base + s))]
        if first:
            outs = [sds((2, 256, 256))] * NX
            out_specs = [pl.BlockSpec((1, 256, 256), lambda s, at: (s, 0, 0))] * NX
        else:
            outs = [sds((2, NX, 256, 256))]
            out_specs = [pl.BlockSpec((1, NX, 256, 256), lambda s, at: (s, 0, 0, 0))]
        return call(
            functools.partial(goal_kernel, first), outs, at,
            mapping, mapping_other, teacher_slab, teacher_slab, teacher_other,
            specs=specs, out_specs=out_specs, grid=(2,), scratch=[pltpu.VMEM((NX, 256, 1024), BF16)],
            flops=2 * 896 * 1024 * 512, moved=4 * 448 * 1024 * 2,
        )

    parts_a = goal_parts(True)
    (parts_b,) = goal_parts(False)

    kv_0 = jnp.stack([piece[:, 256:512] for piece in pieces])
    kv_y = shift(kv_0, 0, 1, 0)
    kv_c = shift(kv_0, 0, 0, 1)
    kv_yc = shift(kv_y, 0, 0, 1)

    from_x = [shift(parts_a[dx], dx, 0, 0) for dx in (1, 3, 2)]
    sum_a = sum((part.astype(F32) for part in from_x), parts_a[0].astype(F32))
    b_y = shift(parts_b[1], 0, 1, 0)
    sum_b = parts_b[0].astype(F32) + b_y.astype(F32)
    a_y = shift(sum_a[1].astype(BF16), 0, 1, 0)
    b_x = [shift(sum_b[dx].astype(BF16), dx, 0, 0) for dx in (1, 3, 2)]
    goal_a = sum_a[0] + a_y.astype(F32)
    goal_b = sum((part.astype(F32) for part in b_x), sum_b[0])

    segs = seg_ids[0]
    own_segs = lax.dynamic_index_in_dim(segs.reshape(4, 4, BLK), place % 4, 1, keepdims=False)
    starts = sum(
        jnp.where(own_segs >= d, jnp.sum((segs == d - 1).astype(jnp.int32)), 0) for d in range(1, 4)
    )
    places = (
        512 * jnp.arange(4, dtype=jnp.int32)[:, None]
        + BLK * (place % 4)
        + jnp.arange(BLK, dtype=jnp.int32)[None, :]
    )
    spans = jnp.concatenate([starts, places], axis=0).astype(jnp.int32)
    spans = jnp.concatenate([spans, spans], axis=1)

    q_specs = [pl.BlockSpec((BLK, 256), lambda s, at: (0, 0))] * NX
    fwd = call(
        forward_kernel,
        [
            sds((2048, HEAD)), sds((HEAD, 2048)), sds((2048, HEAD)), sds((2048, HEAD), F32),
            sds((NX, 256, HEAD)), sds((NX, HEAD, 256), F32), sds((8, 256), F32),
        ],
        at, kv_0, kv_y, kv_c, kv_yc, *pieces, spans, q_gain_row, k_gain_row,
        specs=[whole] * 4 + q_specs + [whole] * 3,
        scratch=[pltpu.VMEM((2048, 256), F32), pltpu.VMEM((HEAD, 2048), BF16)],
        flops=700_000_000, moved=4_000_000,
    )
    k_hat, k_turned, v_all, k_unit, q_hat, outputs, log_total = fwd
    bwd = call(
        backward_kernel,
        [sds((BLK, 256))] * NX + [sds((2, NX, BLK, 256))] * 2 + [sds((8, HEAD), F32)],
        at, k_hat, k_turned, v_all, k_unit, q_hat, outputs, log_total, goal_a, goal_b,
        *pieces, spans, q_gain_row,
        specs=[whole] * 9 + q_specs + [whole] * 2,
        scratch=[
            pltpu.VMEM((2048, HEAD), F32), pltpu.VMEM((2048, HEAD), F32),
            pltpu.VMEM((NX, 256, HEAD), BF16), pltpu.VMEM((NX, BLK, 256), BF16),
        ],
        flops=1_700_000_000, moved=5_000_000,
    )
    dq_parts, send_c, keep_c, gains = bwd[:4], bwd[4], bwd[5], bwd[6]

    from_c = shift(send_c, 0, 0, 1)
    sum_c = keep_c.astype(F32) + from_c.astype(F32)
    from_y = shift(sum_c[1].astype(BF16), 0, 1, 0)
    dq_got = [dq_parts[0]] + [shift(dq_parts[dx], dx, 0, 0) for dx in (1, 2, 3)]

    total = sum_over_four(gains, (1, 0), (2, 0))
    total = sum_over_four(total, (4, 0), (0, 1))
    total = sum_over_four(total, (8, 0), (0, 2))
    total = sum_over_four(total, (0, 4), (0, 8))

    dkv = call(
        key_kernel, [sds((BLK, 256))] * NX, at, sum_c[0], from_y, kv_0, k_gain_row, moved=2_000_000
    )
    dkv_got = [dkv[0]] + [shift(dkv[dx], dx, 0, 0) for dx in (1, 2, 3)]
    dq, dk, dv = call(
        unpack_kernel, [sds((BLK, 1024)), sds((BLK, 512)), sds((BLK, 512))], at, *dq_got, *dkv_got,
        moved=2 * BLK * 2048 * 2,
    )
    q_gain_grad = total[0] * (1.0 / math.sqrt(262144))
    key_gain_gradient = total[1] * (1.0 / math.sqrt(131072))
    return dq[None], dk[None], dv[None], q_gain_grad, key_gain_gradient


def solution(mesh):
    return jax.shard_map(
        on_device,
        mesh=mesh,
        in_specs=(
            P("dp", "seq", None),
            P("dp", "seq", None),
            P("dp", "seq", None),
            P(),
            P(),
            P("dp", None),
            P("dp", "seq", None),
            P("seq", None),
        ),
        out_specs=(P("dp", "seq", None), P("dp", "seq", None), P("dp", "seq", None), P(), P()),
        check_vma=False,
    )
```

time: 403 us -> 128 us (0.32)
  waiting for transfers between devices: 252 us -> 33.7 us
  blocking collectives: 75.7 us -> 0 us
  starting transfers between devices: 0.38 us -> 58.6 us
  matrix products: 31.3 us -> 0 us
  Pallas kernels: 0 us -> 24.6 us
  local copies, waits for them, and re-layouts: 23.8 us -> 5.08 us
  between operations: 14 us -> 0.93 us
    all_gather x2 -> x0, waiting for transfers between devices: 103 us -> none  [the longest x1 52.8 us: on_device(): key_block = lax.all_gather(k_hat, 'seq', axis=0, tiled=True)]
    reduce_scatter x2 -> x0, waiting for transfers between devices: 87.3 us -> none  [the longest x1 82.6 us: on_device(): lax.psum_scatter(lax.dot_general(teacher_slab, mapping, (((0,), (0,)), ((...]
    psum x1 -> x0, blocking collectives: 75.7 us -> none  [on_device(): q_total, k_total = lax.psum((q_part, k_part), ('dp', 'seq'))]
    unnamed x6 -> x0, waiting for transfers between devices: 62.4 us -> none
    ppermute x0 -> x36, starting transfers between devices: none -> 58.6 us  [the longest x24 38.8 us: shift(): return lax.ppermute(value, 'seq', pairs)]
    ppermute x0 -> x36, waiting for transfers between devices: none -> 33.7 us  [the longest x24 23.1 us: shift(): return lax.ppermute(value, 'seq', pairs)]
    dot_general x7 -> x0, matrix products: 31.3 us -> none  [the longest x1 6.72 us: on_device(): jnp.einsum('jgts,tjgd->sjd', probs_low, d_out, preferred_element_type=jnp...]
    pallas_call x0 -> x8, Pallas kernels: none -> 24.6 us  [call(): pl.pallas_call(kernel, out_shape=outs, grid_spec=pltpu.PrefetchScalarGrid...]
  transfers between devices with their start and end apart: 5 -> 36, of which waited for: 5 -> 15; matrix products, arithmetic and copies ran while one was open for 9% -> 4% of each run, Pallas kernels for 0% -> 13%
where the time goes in v1:
time: 128 us
  starting transfers between devices  58.6 us (46%)
  waiting for transfers between devices  33.7 us (26%)
  Pallas kernels  24.6 us (19%)
  local copies, waits for them, and re-layouts  5.08 us (4%)
  other arithmetic  4.67 us (4%)
    ppermute x24, starting transfers between devices, shift(): return lax.ppermute(value, 'seq', pairs)  38.8 us
    pallas_call x8, Pallas kernels, call(): pl.pallas_call(kernel, out_shape=outs, grid_spec=pltpu.PrefetchScalarGrid...  24.6 us
    ppermute x24, waiting for transfers between devices, shift(): return lax.ppermute(value, 'seq', pairs)  23.1 us
    ppermute x12, starting transfers between devices, flip(): return lax.ppermute(value, ('dp', 'seq'), pairs)  19.8 us
    ppermute x12, waiting for transfers between devices, flip(): return lax.ppermute(value, ('dp', 'seq'), pairs)  10.5 us
    unnamed x18, local copies, waits for them, and re-layouts  4.28 us
  transfers between devices with their start and end apart: 36, of which 15 were waited for; matrix products, arithmetic and copies ran while one was open for 4% of the time, Pallas kernels for 13%

profile of v1, /device:TPU:32, one launch (start us, length us, event | category | flops | bytes accessed | tf_op | source)
XLA Modules:
  0.0 127.5 jit_solution(13696336098791134848)
XLA Ops:
  0.8 0.9 copy-done.3
  1.7 0.9 copy-done.4
  2.6 0.9 copy-done.5
  3.5 1.3 %shard_map.119 = (bf16[128,512]{1,0:T(8,128)(2,1)S(1)}, bf16[128,512]{1,0:T(8,128)(2,1)}, bf16[128,512]{1,0:T(8,128)(2,1)S(1)}, bf16[128,512]{1,0:T(8,128)(2,1)S(1)}) custom-call(s32[3]{0:T(128)S(1)} %pad_add_fusion.at, bf16[128,1024]{1,0:T(8,128)(2,1)S(1)} %bitcast.67, bf16[128,512]{1,0:T(8,128)(2,1)S(1)} %bitcast.68, bf16[128,512]{1,0:T(8,128)(2,1)S(1)} %bitcast.69), custom_call_target="tpu_custom_call" | custom-call | bytes 1048576 | tf_op jit(solution)/shard_map/pallas_call | solution.py:52
  4.8 1.5 %collective-permute-start = (bf16[128,512]{1,0:T(8,128)(2,1)}, bf16[128,512]{1,0:T(8,128)(2,1)S(1)}, u32[]{:S(2)}, u32[]{:S(2)}) collective-permute-start(bf16[128,512]{1,0:T(8,128)(2,1)} %get-tuple-element.35), channel_id=1, source_target_pairs={{0,4},{1,5},{2,6},{3,7},{4,8},{5,9},{6,10},{7,11},{8,12},{9,13},{1... | collective-permute-start | bytes 393224 | tf_op jit(solution)/shard_map/ppermute | solution.py:33
  6.3 2.7 %collective-permute-start.1 = (bf16[128,512]{1,0:T(8,128)(2,1)S(1)}, bf16[128,512]{1,0:T(8,128)(2,1)S(1)}, u32[]{:S(2)}, u32[]{:S(2)}) collective-permute-start(bf16[128,512]{1,0:T(8,128)(2,1)S(1)} %get-tuple-element.36), channel_id=1, source_target_pairs={{0,8},{1,9},{2,10},{3,11},{4,12},{5,13},{6,14},{7,15},{8,0},{9,1},... | collective-permute-start | bytes 393224 | tf_op jit(solution)/shard_map/ppermute | solution.py:33
  9.0 1.4 %collective-permute-start.2 = (bf16[128,512]{1,0:T(8,128)(2,1)S(1)}, bf16[128,512]{1,0:T(8,128)(2,1)S(1)}, u32[]{:S(2)}, u32[]{:S(2)}) collective-permute-start(bf16[128,512]{1,0:T(8,128)(2,1)S(1)} %get-tuple-element.37), channel_id=1, source_target_pairs={{0,12},{1,13},{2,14},{3,15},{4,0},{5,1},{6,2},{7,3},{8,4},{9,5},{1... | collective-permute-start | bytes 393224 | tf_op jit(solution)/shard_map/ppermute | solution.py:33
  10.4 1.5 %copy-done = bf16[1,448,2048]{2,1,0:T(8,128)(2,1)S(1)} copy-done((bf16[1,448,2048]{2,1,0:T(8,128)(2,1)S(1)}, bf16[1,448,2048]{2,1,0:T(8,128)(2,1)}, u32[]{:S(2)}) %copy-start) | copy-done | bytes 1835032
  12.0 2.5 %shard_map.121 = bf16[448,1024]{1,0:T(8,128)(2,1)} custom-call(s32[3]{0:T(128)S(1)} %pad_add_fusion.at, bf16[448,2048]{1,0:T(8,128)(2,1)S(1)} %bitcast.61, bf16[448,2048]{1,0:T(8,128)(2,1)S(1)} %bitcast.62), custom_call_target="tpu_custom_call" | custom-call | bytes 1835008 | tf_op jit(solution)/shard_map/pallas_call | solution.py:52
  14.4 0.5 collective-permute-start.6
  15.0 0.7 fusion.6
  15.6 0.6 slice_bitcast_fusion.11
  16.3 1.9 %add_bitcast_fusion = s32[4,128]{1,0:T(4,128)S(1)} fusion(s32[4,1,128]{2,0,1:T(4,128)S(1)} %bitcast.75, s32[]{:T(128)} %get-tuple-element.64, s32[]{:T(128)} %get-tuple-element.65, s32[]{:T(128)} %get-tuple-element.63), kind=kLoop, calls=%fused_computation.36 | loop fusion | flops 4096 | bytes 4108 | tf_op jit(solution)/shard_map/add | solution.py:328
  18.3 0.9 pad_maximum_fusion.kv_0
  19.2 3.3 %collective-permute-start.3 = (bf16[4,128,256]{2,1,0:T(8,128)(2,1)S(1)}, bf16[4,128,256]{2,1,0:T(8,128)(2,1)S(1)}, u32[]{:S(2)}, u32[]{:S(2)}) collective-permute-start(bf16[4,128,256]{2,1,0:T(8,128)(2,1)S(1)} %pad_maximum_fusion.kv_0), channel_id=1, source_target_pairs={{0,2},{1,3},{2,0},{3,1},{4,6},{5,7},{6,4},{7,5},{8,10},{9,11},{10,... | collective-permute-start | bytes 786440 | tf_op jit(solution)/shard_map/ppermute | solution.py:33
  22.6 6.4 %collective-permute-done.3.kv_y = bf16[4,128,256]{2,1,0:T(8,128)(2,1)S(1)} collective-permute-done((bf16[4,128,256]{2,1,0:T(8,128)(2,1)S(1)}, bf16[4,128,256]{2,1,0:T(8,128)(2,1)S(1)}, u32[]{:S(2)}, u32[]{:S(2)}) %collective-permute-start.3) | collective-permute-done | bytes 262176 | tf_op jit(solution)/shard_map/ppermute | solution.py:33
  29.0 4.1 %shard_map.122 = (bf16[2,256,256]{2,1,0:T(8,128)(2,1)S(1)}, bf16[2,256,256]{2,1,0:T(8,128)(2,1)S(1)}, bf16[2,256,256]{2,1,0:T(8,128)(2,1)S(1)}, bf16[2,256,256]{2,1,0:T(8,128)(2,1)S(1)}) custom-call(s32[3]{0:T(128)S(1)} %pad_add_fusion.at, bf16[448,1024]{1,0:T(8,128)(2,1)S(1)} %copy-done.2, bf16[448,1024]{1,0:T(8,128)(2,1)} %collective-permute-done.6.map_b, ...), custom_call_target="tpu_custom_call" | custom-call | flops 939524096 | bytes 3670016 | tf_op jit(solution)/shard_map/pallas_call | solution.py:52
  33.1 0.7 collective-permute-start.8
  33.8 2.6 %collective-permute-start.9 = (bf16[2,256,256]{2,1,0:T(8,128)(2,1)S(1)}, bf16[2,256,256]{2,1,0:T(8,128)(2,1)S(1)}, u32[]{:S(2)}, u32[]{:S(2)}) collective-permute-start(bf16[2,256,256]{2,1,0:T(8,128)(2,1)S(1)} %get-tuple-element.47), channel_id=1, source_target_pairs={{0,12},{1,13},{2,14},{3,15},{4,0},{5,1},{6,2},{7,3},{8,4},{9,5},{1... | collective-permute-start | bytes 786440 | tf_op jit(solution)/shard_map/ppermute | solution.py:33
  36.5 4.1 %shard_map.123 = bf16[2,4,256,256]{3,2,1,0:T(8,128)(2,1)S(1)} custom-call(s32[3]{0:T(128)S(1)} %pad_add_fusion.at, bf16[448,1024]{1,0:T(8,128)(2,1)S(1)} %copy-done.2, bf16[448,1024]{1,0:T(8,128)(2,1)} %collective-permute-done.6.map_b, bf16[448,2048]{1,0:T(8,128)(2,1)S(1)} %bitcast.65, bf16[448,2048]{1,0:T(8,128)(2,1)S(1)} %bitcast.66, ...), custom_call_target="tpu_custom_call" | custom-call | flops 939524096 | bytes 3670016 | tf_op jit(solution)/shard_map/pallas_call | solution.py:52
  40.6 3.5 %collective-permute-start.12 = (bf16[4,256,256]{2,1,0:T(8,128)(2,1)S(1)}, bf16[4,256,256]{2,1,0:T(8,128)(2,1)S(1)}, u32[]{:S(2)}, u32[]{:S(2)}) collective-permute-start(bf16[4,256,256]{2,1,0:T(8,128)(2,1)S(1)} %slice_bitcast_fusion.1), channel_id=1, source_target_pairs={{0,2},{1,3},{2,0},{3,1},{4,6},{5,7},{6,4},{7,5},{8,10},{9,11},{10,... | collective-permute-start | bytes 1572872 | tf_op jit(solution)/shard_map/ppermute | solution.py:33
  44.1 4.6 %shard_map.120 = (bf16[2048,128]{1,0:T(8,128)(2,1)S(1)}, bf16[128,2048]{1,0:T(8,128)(2,1)S(1)}, bf16[2048,128]{1,0:T(8,128)(2,1)S(1)}, f32[2048,128]{1,0:T(8,128...) custom-call(s32[3]{0:T(128)S(1)} %pad_add_fusion.at, ...), custom_call_target="tpu_custom_call" | custom-call | flops 700000000 | bytes 4000000 | tf_op jit(solution)/shard_map/pallas_call | solution.py:52
  48.8 0.1 convert_add_fusion.2
  48.9 3.3 %collective-permute-start.11 = (bf16[256,256]{1,0:T(8,128)(2,1)S(1)}, bf16[256,256]{1,0:T(8,128)(2,1)S(1)}, u32[]{:S(2)}, u32[]{:S(2)}) collective-permute-start(bf16[256,256]{1,0:T(8,128)(2,1)S(1)} %fusion.5), channel_id=1, source_target_pairs={{0,2},{1,3},{2,0},{3,1},{4,6},{5,7},{6,4},{7,5},{8,10},{9,11},{10,... | collective-permute-start | bytes 393224 | tf_op jit(solution)/shard_map/ppermute | solution.py:33
  52.2 5.0 %collective-permute-done.12 = bf16[4,256,256]{2,1,0:T(8,128)(2,1)S(1)} collective-permute-done((bf16[4,256,256]{2,1,0:T(8,128)(2,1)S(1)}, bf16[4,256,256]{2,1,0:T(8,128)(2,1)S(1)}, u32[]{:S(2)}, u32[]{:S(2)}) %collective-permute-start.12) | collective-permute-done | bytes 524320 | tf_op jit(solution)/shard_map/ppermute | solution.py:33
  57.2 0.1 fusion.9
  57.4 0.9 collective-permute-start.13
  58.3 2.8 %collective-permute-start.15 = (bf16[256,256]{1,0:T(8,128)(2,1)S(1)}, bf16[256,256]{1,0:T(8,128)(2,1)S(1)}, u32[]{:S(2)}, u32[]{:S(2)}) collective-permute-start(bf16[256,256]{1,0:T(8,128)(2,1)S(1)} %get-tuple-element.69), channel_id=1, source_target_pairs={{0,8},{1,9},{2,10},{3,11},{4,12},{5,13},{6,14},{7,15},{8,0},{9,1},... | collective-permute-start | bytes 393224 | tf_op jit(solution)/shard_map/ppermute | solution.py:33
  61.1 2.5 %collective-permute-start.14 = (bf16[256,256]{1,0:T(8,128)(2,1)S(1)}, bf16[256,256]{1,0:T(8,128)(2,1)S(1)}, u32[]{:S(2)}, u32[]{:S(2)}) collective-permute-start(bf16[256,256]{1,0:T(8,128)(2,1)S(1)} %get-tuple-element.70), channel_id=1, source_target_pairs={{0,12},{1,13},{2,14},{3,15},{4,0},{5,1},{6,2},{7,3},{8,4},{9,5},{1... | collective-permute-start | bytes 393224 | tf_op jit(solution)/shard_map/ppermute | solution.py:33
  63.7 1.7 %collective-permute-done.15 = bf16[256,256]{1,0:T(8,128)(2,1)S(1)} collective-permute-done((bf16[256,256]{1,0:T(8,128)(2,1)S(1)}, bf16[256,256]{1,0:T(8,128)(2,1)S(1)}, u32[]{:S(2)}, u32[]{:S(2)}) %collective-permute-start.15) | collective-permute-done | bytes 131104 | tf_op jit(solution)/shard_map/ppermute | solution.py:33
  65.4 0.8 collective-permute-done.14
  66.2 5.9 %shard_map.124 = (bf16[128,256]{1,0:T(8,128)(2,1)S(1)}, bf16[128,256]{1,0:T(8,128)(2,1)S(1)}, bf16[128,256]{1,0:T(8,128)(2,1)S(1)}, bf16[128,256]{1,0:T(8,128)(2...) custom-call(s32[3]{0:T(128)S(1)} %pad_add_fusion.at, ...), custom_call_target="tpu_custom_call" | custom-call | flops 1700000000 | bytes 5000000 | tf_op jit(solution)/shard_map/pallas_call | solution.py:52
  72.1 2.2 %collective-permute-start.26 = (f32[8,128]{1,0:T(8,128)S(1)}, f32[8,128]{1,0:T(8,128)S(1)}, u32[]{:S(2)}, u32[]{:S(2)}) collective-permute-start(f32[8,128]{1,0:T(8,128)S(1)} %get-tuple-element.62), channel_id=1, source_target_pairs={{0,48},{1,49},{2,50},{3,51},{4,52},{5,53},{6,54},{7,55},{8,56},{9,... | collective-permute-start | bytes 12296 | tf_op jit(solution)/shard_map/ppermute | solution.py:39
  74.4 1.5 %collective-permute-start.25 = (f32[8,128]{1,0:T(8,128)S(1)}, f32[8,128]{1,0:T(8,128)S(1)}, u32[]{:S(2)}, u32[]{:S(2)}) collective-permute-start(f32[8,128]{1,0:T(8,128)S(1)} %get-tuple-element.62), channel_id=1, source_target_pairs={{0,32},{1,33},{2,34},{3,35},{4,36},{5,37},{6,38},{7,39},{8,40},{9,... | collective-permute-start | bytes 12296 | tf_op jit(solution)/shard_map/ppermute | solution.py:39
  75.8 1.4 %collective-permute-start.24 = (f32[8,128]{1,0:T(8,128)S(1)}, f32[8,128]{1,0:T(8,128)S(1)}, u32[]{:S(2)}, u32[]{:S(2)}) collective-permute-start(f32[8,128]{1,0:T(8,128)S(1)} %get-tuple-element.62), channel_id=1, source_target_pairs={{0,16},{1,17},{2,18},{3,19},{4,20},{5,21},{6,22},{7,23},{8,24},{9,... | collective-permute-start | bytes 12296 | tf_op jit(solution)/shard_map/ppermute | solution.py:39
  77.2 1.7 %collective-permute-done.25 = f32[8,128]{1,0:T(8,128)S(1)} collective-permute-done((f32[8,128]{1,0:T(8,128)S(1)}, f32[8,128]{1,0:T(8,128)S(1)}, u32[]{:S(2)}, u32[]{:S(2)}) %collective-permute-start.25) | collective-permute-done | bytes 4128 | tf_op jit(solution)/shard_map/ppermute | solution.py:39
  78.9 0.6 collective-permute-done.24
  79.4 3.0 %collective-permute-start.29 = (f32[8,128]{1,0:T(8,128)S(1)}, f32[8,128]{1,0:T(8,128)S(1)}, u32[]{:S(2)}, u32[]{:S(2)}) collective-permute-start(f32[8,128]{1,0:T(8,128)S(1)} %add_add_fusion.4), channel_id=1, source_target_pairs={{0,65},{1,64},{2,67},{3,66},{4,69},{5,68},{6,71},{7,70},{8,73},{9,... | collective-permute-start | bytes 12296 | tf_op jit(solution)/shard_map/ppermute | solution.py:39
  82.5 3.4 %collective-permute-start.28 = (f32[8,128]{1,0:T(8,128)S(1)}, f32[8,128]{1,0:T(8,128)S(1)}, u32[]{:S(2)}, u32[]{:S(2)}) collective-permute-start(f32[8,128]{1,0:T(8,128)S(1)} %add_add_fusion.4), channel_id=1, source_target_pairs={{0,1},{1,0},{2,3},{3,2},{4,5},{5,4},{6,7},{7,6},{8,9},{9,8},{10,11... | collective-permute-start | bytes 12296 | tf_op jit(solution)/shard_map/ppermute | solution.py:39
  85.9 0.5 collective-permute-done.29
  86.4 0.3 collective-permute-done.28
  86.7 6.7 %collective-permute-done.27 = f32[8,128]{1,0:T(8,128)S(1)} collective-permute-done((f32[8,128]{1,0:T(8,128)S(1)}, f32[8,128]{1,0:T(8,128)S(1)}, u32[]{:S(2)}, u32[]{:S(2)}) %collective-permute-start.27) | collective-permute-done | bytes 4128 | tf_op jit(solution)/shard_map/ppermute | solution.py:39
  93.4 3.0 %collective-permute-start.32 = (f32[8,128]{1,0:T(8,128)S(1)}, f32[8,128]{1,0:T(8,128)S(1)}, u32[]{:S(2)}, u32[]{:S(2)}) collective-permute-start(f32[8,128]{1,0:T(8,128)S(1)} %add_add_fusion.3), channel_id=1, source_target_pairs={{0,130},{1,131},{2,128},{3,129},{4,134},{5,135},{6,132},{7,133},{8... | collective-permute-start | bytes 12296 | tf_op jit(solution)/shard_map/ppermute | solution.py:39
  96.4 0.6 collective-permute-start.31
  97.0 0.4 collective-permute-start.30
  97.5 1.8 %collective-permute-start.16 = (bf16[128,256]{1,0:T(8,128)(2,1)S(1)}, bf16[128,256]{1,0:T(8,128)(2,1)S(1)}, u32[]{:S(2)}, u32[]{:S(2)}) collective-permute-start(bf16[128,256]{1,0:T(8,128)(2,1)S(1)} %get-tuple-element.50), channel_id=1, source_target_pairs={{0,4},{1,5},{2,6},{3,7},{4,8},{5,9},{6,10},{7,11},{8,12},{9,13},{1... | collective-permute-start | bytes 196616 | tf_op jit(solution)/shard_map/ppermute | solution.py:33
  99.2 3.4 %collective-permute-start.17 = (bf16[128,256]{1,0:T(8,128)(2,1)S(1)}, bf16[128,256]{1,0:T(8,128)(2,1)S(1)}, u32[]{:S(2)}, u32[]{:S(2)}) collective-permute-start(bf16[128,256]{1,0:T(8,128)(2,1)S(1)} %get-tuple-element.51), channel_id=1, source_target_pairs={{0,8},{1,9},{2,10},{3,11},{4,12},{5,13},{6,14},{7,15},{8,0},{9,1},... | collective-permute-start | bytes 196616 | tf_op jit(solution)/shard_map/ppermute | solution.py:33
  102.6 2.7 %collective-permute-start.35 = (f32[8,128]{1,0:T(8,128)S(1)}, f32[8,128]{1,0:T(8,128)S(1)}, u32[]{:S(2)}, u32[]{:S(2)}) collective-permute-start(f32[8,128]{1,0:T(8,128)S(1)} %add_add_fusion.2), channel_id=1, source_target_pairs={{0,12},{1,13},{2,14},{3,15},{4,8},{5,9},{6,10},{7,11},{8,4},{9,5},... | collective-permute-start | bytes 12296 | tf_op jit(solution)/shard_map/ppermute | solution.py:39
  105.2 0.1 collective-permute-start.34
  105.4 1.4 %collective-permute-start.33 = (f32[8,128]{1,0:T(8,128)S(1)}, f32[8,128]{1,0:T(8,128)S(1)}, u32[]{:S(2)}, u32[]{:S(2)}) collective-permute-start(f32[8,128]{1,0:T(8,128)S(1)} %add_add_fusion.2), channel_id=1, source_target_pairs={{0,4},{1,5},{2,6},{3,7},{4,0},{5,1},{6,2},{7,3},{8,12},{9,13},{10,... | collective-permute-start | bytes 12296 | tf_op jit(solution)/shard_map/ppermute | solution.py:39
  106.8 0.1 convert_add_fusion.1
  106.9 0.6 collective-permute-done.35
  107.5 2.6 %collective-permute-start.18 = (bf16[128,256]{1,0:T(8,128)(2,1)S(1)}, bf16[128,256]{1,0:T(8,128)(2,1)S(1)}, u32[]{:S(2)}, u32[]{:S(2)}) collective-permute-start(bf16[128,256]{1,0:T(8,128)(2,1)S(1)} %get-tuple-element.52), channel_id=1, source_target_pairs={{0,12},{1,13},{2,14},{3,15},{4,0},{5,1},{6,2},{7,3},{8,4},{9,5},{1... | collective-permute-start | bytes 196616 | tf_op jit(solution)/shard_map/ppermute | solution.py:33
  110.1 0.3 collective-permute-done.34
  110.4 1.9 %collective-permute-start.20 = (bf16[4,128,256]{2,1,0:T(8,128)(2,1)S(1)}, bf16[4,128,256]{2,1,0:T(8,128)(2,1)S(1)}, u32[]{:S(2)}, u32[]{:S(2)}) collective-permute-start(bf16[4,128,256]{2,1,0:T(8,128)(2,1)S(1)} %fusion), channel_id=1, source_target_pairs={{0,2},{1,3},{2,0},{3,1},{4,6},{5,7},{6,4},{7,5},{8,10},{9,11},{10,... | collective-permute-start | bytes 786440 | tf_op jit(solution)/shard_map/ppermute | solution.py:33
  112.3 5.9 %collective-permute-done.20.from_y = bf16[4,128,256]{2,1,0:T(8,128)(2,1)S(1)} collective-permute-done((bf16[4,128,256]{2,1,0:T(8,128)(2,1)S(1)}, bf16[4,128,256]{2,1,0:T(8,128)(2,1)S(1)}, u32[]{:S(2)}, u32[]{:S(2)}) %collective-permute-start.20) | collective-permute-done | bytes 262176 | tf_op jit(solution)/shard_map/ppermute | solution.py:33
  118.2 0.8 shard_map.125
  119.0 0.1 collective-permute-start.21
  119.1 2.1 %collective-permute-start.22 = (bf16[128,256]{1,0:T(8,128)(2,1)S(1)}, bf16[128,256]{1,0:T(8,128)(2,1)S(1)}, u32[]{:S(2)}, u32[]{:S(2)}) collective-permute-start(bf16[128,256]{1,0:T(8,128)(2,1)S(1)} %get-tuple-element.57), channel_id=1, source_target_pairs={{0,8},{1,9},{2,10},{3,11},{4,12},{5,13},{6,14},{7,15},{8,0},{9,1},... | collective-permute-start | bytes 196616 | tf_op jit(solution)/shard_map/ppermute | solution.py:33
  121.2 1.1 collective-permute-start.23
  122.3 0.5 multiply_bitcast_fusion
  122.9 2.4 %collective-permute-done.21.kv_1 = bf16[128,256]{1,0:T(8,128)(2,1)S(1)} collective-permute-done((bf16[128,256]{1,0:T(8,128)(2,1)S(1)}, bf16[128,256]{1,0:T(8,128)(2,1)S(1)}, u32[]{:S(2)}, u32[]{:S(2)}) %collective-permute-start.21) | collective-permute-done | bytes 65568 | tf_op jit(solution)/shard_map/ppermute | solution.py:33
  125.3 0.9 collective-permute-done.23.kv_3
  126.1 1.4 %shard_map.126 = (bf16[128,1024]{1,0:T(8,128)(2,1)}, bf16[128,512]{1,0:T(8,128)(2,1)}, bf16[128,512]{1,0:T(8,128)(2,1)}) custom-call(s32[3]{0:T(128)S(1)} %pad_add_fusion.at, bf16[128,256]{1,0:T(8,128)(2,1)S(1)} %get-tuple-element.49.q_0, bf16[128,256]{1,0:T(8,128)(2,1)S(1)} %collective-permute-done.16.q_1, ...), custom_call_target="tpu_custom_call" | custom-call | bytes 1048576 | tf_op jit(solution)/shard_map/pallas_call | solution.py:52
  (61 shorter events, 0.7 us)
Async XLA Ops:
  0.7 1.0 copy-start.3
  1.7 0.9 copy-start.4
  2.6 0.9 copy-start.5
  4.8 13.5 %collective-permute-start = (bf16[128,512]{1,0:T(8,128)(2,1)}, bf16[128,512]{1,0:T(8,128)(2,1)S(1)}, u32[]{:S(2)}, u32[]{:S(2)}) collective-permute-start(bf16[128,512]{1,0:T(8,128)(2,1)} %get-tuple-element.35), channel_id=1, source_target_pairs={{0,4},{1,5},{2,6},{3,7},{4,8},{5,9},{6,10},{7,11},{8,12},{9,13},{1... | collective-permute-start | bytes 393224 | tf_op jit(solution)/shard_map/ppermute | solution.py:33
  6.3 12.0 %collective-permute-start.1 = (bf16[128,512]{1,0:T(8,128)(2,1)S(1)}, bf16[128,512]{1,0:T(8,128)(2,1)S(1)}, u32[]{:S(2)}, u32[]{:S(2)}) collective-permute-start(bf16[128,512]{1,0:T(8,128)(2,1)S(1)} %get-tuple-element.36), channel_id=1, source_target_pairs={{0,8},{1,9},{2,10},{3,11},{4,12},{5,13},{6,14},{7,15},{8,0},{9,1},... | collective-permute-start | bytes 393224 | tf_op jit(solution)/shard_map/ppermute | solution.py:33
  9.0 9.3 %collective-permute-start.2 = (bf16[128,512]{1,0:T(8,128)(2,1)S(1)}, bf16[128,512]{1,0:T(8,128)(2,1)S(1)}, u32[]{:S(2)}, u32[]{:S(2)}) collective-permute-start(bf16[128,512]{1,0:T(8,128)(2,1)S(1)} %get-tuple-element.37), channel_id=1, source_target_pairs={{0,12},{1,13},{2,14},{3,15},{4,0},{5,1},{6,2},{7,3},{8,4},{9,5},{1... | collective-permute-start | bytes 393224 | tf_op jit(solution)/shard_map/ppermute | solution.py:33
  10.4 1.5 %copy-start = (bf16[1,448,2048]{2,1,0:T(8,128)(2,1)S(1)}, bf16[1,448,2048]{2,1,0:T(8,128)(2,1)}, u32[]{:S(2)}) copy-start(bf16[1,448,2048]{2,1,0:T(8,128)(2,1)} %param.14) | copy-start | bytes 5505028
  11.9 2.5 %copy-start.2 = (bf16[448,1024]{1,0:T(8,128)(2,1)S(1)}, bf16[448,1024]{1,0:T(8,128)(2,1)}, u32[]{:S(2)}) copy-start(bf16[448,1024]{1,0:T(8,128)(2,1)} %map_a.3) | copy-start | bytes 2752516
  11.9 3.0 %copy-start.8 = (s32[1,2048]{1,0:T(1,128)S(1)}, s32[1,2048]{1,0:T(1,128)}, u32[]{:S(2)}) copy-start(s32[1,2048]{1,0:T(1,128)} %param.13) | copy-start | bytes 24580
  11.9 17.1 %copy-start.1 = (bf16[1,448,2048]{2,1,0:T(8,128)(2,1)S(1)}, bf16[1,448,2048]{2,1,0:T(8,128)(2,1)}, u32[]{:S(2)}) copy-start(bf16[1,448,2048]{2,1,0:T(8,128)(2,1)} %param.14) | copy-start | bytes 5505028
  14.4 14.6 %collective-permute-start.7 = (bf16[448,1024]{1,0:T(8,128)(2,1)}, bf16[448,1024]{1,0:T(8,128)(2,1)}, u32[]{:S(2)}, u32[]{:S(2)}) collective-permute-start(bf16[448,1024]{1,0:T(8,128)(2,1)} %shard_map.121), channel_id=1, source_target_pairs={{0,1},{1,0},{2,3},{3,2},{4,5},{5,4},{6,7},{7,6},{8,9},{9,8},{10,11... | collective-permute-start | bytes 2752520 | tf_op jit(solution)/shard_map/ppermute | solution.py:33
  14.4 14.6 %collective-permute-start.6 = (bf16[448,1024]{1,0:T(8,128)(2,1)S(1)}, bf16[448,1024]{1,0:T(8,128)(2,1)}, u32[]{:S(2)}, u32[]{:S(2)}) collective-permute-start(bf16[448,1024]{1,0:T(8,128)(2,1)S(1)} %copy-done.2), channel_id=1, source_target_pairs={{0,1},{1,0},{2,3},{3,2},{4,5},{5,4},{6,7},{7,6},{8,9},{9,8},{10,11... | collective-permute-start | bytes 2752520 | tf_op jit(solution)/shard_map/ppermute | solution.py:33
  19.2 9.8 %collective-permute-start.3 = (bf16[4,128,256]{2,1,0:T(8,128)(2,1)S(1)}, bf16[4,128,256]{2,1,0:T(8,128)(2,1)S(1)}, u32[]{:S(2)}, u32[]{:S(2)}) collective-permute-start(bf16[4,128,256]{2,1,0:T(8,128)(2,1)S(1)} %pad_maximum_fusion.kv_0), channel_id=1, source_target_pairs={{0,2},{1,3},{2,0},{3,1},{4,6},{5,7},{6,4},{7,5},{8,10},{9,11},{10,... | collective-permute-start | bytes 786440 | tf_op jit(solution)/shard_map/ppermute | solution.py:33
  22.6 18.0 %collective-permute-start.4 = (bf16[4,128,256]{2,1,0:T(8,128)(2,1)S(1)}, bf16[4,128,256]{2,1,0:T(8,128)(2,1)S(1)}, u32[]{:S(2)}, u32[]{:S(2)}) collective-permute-start(bf16[4,128,256]{2,1,0:T(8,128)(2,1)S(1)} %pad_maximum_fusion.kv_0), channel_id=1, source_target_pairs={{0,1},{1,0},{2,3},{3,2},{4,5},{5,4},{6,7},{7,6},{8,9},{9,8},{10,11... | collective-permute-start | bytes 786440 | tf_op jit(solution)/shard_map/ppermute | solution.py:33
  29.0 15.1 %collective-permute-start.5 = (bf16[4,128,256]{2,1,0:T(8,128)(2,1)S(1)}, bf16[4,128,256]{2,1,0:T(8,128)(2,1)S(1)}, u32[]{:S(2)}, u32[]{:S(2)}) collective-permute-start(bf16[4,128,256]{2,1,0:T(8,128)(2,1)S(1)} %collective-permute-done.3.kv_y), channel_id=1, source_target_pairs={{0,1},{1,0},{2,3},{3,2},{4,5},{5,4},{6,7},{7,6},{8,9},{9,8},{10,11... | collective-permute-start | bytes 786440 | tf_op jit(solution)/shard_map/ppermute | solution.py:33
  33.1 15.6 %collective-permute-start.8 = (bf16[2,256,256]{2,1,0:T(8,128)(2,1)S(1)}, bf16[2,256,256]{2,1,0:T(8,128)(2,1)S(1)}, u32[]{:S(2)}, u32[]{:S(2)}) collective-permute-start(bf16[2,256,256]{2,1,0:T(8,128)(2,1)S(1)} %get-tuple-element.46), channel_id=1, source_target_pairs={{0,4},{1,5},{2,6},{3,7},{4,8},{5,9},{6,10},{7,11},{8,12},{9,13},{1... | collective-permute-start | bytes 786440 | tf_op jit(solution)/shard_map/ppermute | solution.py:33
  33.8 14.9 %collective-permute-start.9 = (bf16[2,256,256]{2,1,0:T(8,128)(2,1)S(1)}, bf16[2,256,256]{2,1,0:T(8,128)(2,1)S(1)}, u32[]{:S(2)}, u32[]{:S(2)}) collective-permute-start(bf16[2,256,256]{2,1,0:T(8,128)(2,1)S(1)} %get-tuple-element.47), channel_id=1, source_target_pairs={{0,12},{1,13},{2,14},{3,15},{4,0},{5,1},{6,2},{7,3},{8,4},{9,5},{1... | collective-permute-start | bytes 786440 | tf_op jit(solution)/shard_map/ppermute | solution.py:33
  36.4 7.6 %copy-start.6 = (f32[128]{0:T(128)S(1)}, f32[128]{0:T(128)}, u32[]{:S(2)}) copy-start(f32[128]{0:T(128)} %param.12) | copy-start | bytes 1540
  36.4 7.6 %copy-start.7 = (f32[128]{0:T(128)S(1)}, f32[128]{0:T(128)}, u32[]{:S(2)}) copy-start(f32[128]{0:T(128)} %param.11) | copy-start | bytes 1540
  36.5 12.3 %collective-permute-start.10 = (bf16[2,256,256]{2,1,0:T(8,128)(2,1)S(1)}, bf16[2,256,256]{2,1,0:T(8,128)(2,1)S(1)}, u32[]{:S(2)}, u32[]{:S(2)}) collective-permute-start(bf16[2,256,256]{2,1,0:T(8,128)(2,1)S(1)} %get-tuple-element.48), channel_id=1, source_target_pairs={{0,8},{1,9},{2,10},{3,11},{4,12},{5,13},{6,14},{7,15},{8,0},{9,1},... | collective-permute-start | bytes 786440 | tf_op jit(solution)/shard_map/ppermute | solution.py:33
  40.6 16.6 %collective-permute-start.12 = (bf16[4,256,256]{2,1,0:T(8,128)(2,1)S(1)}, bf16[4,256,256]{2,1,0:T(8,128)(2,1)S(1)}, u32[]{:S(2)}, u32[]{:S(2)}) collective-permute-start(bf16[4,256,256]{2,1,0:T(8,128)(2,1)S(1)} %slice_bitcast_fusion.1), channel_id=1, source_target_pairs={{0,2},{1,3},{2,0},{3,1},{4,6},{5,7},{6,4},{7,5},{8,10},{9,11},{10,... | collective-permute-start | bytes 1572872 | tf_op jit(solution)/shard_map/ppermute | solution.py:33
  48.9 14.7 %collective-permute-start.11 = (bf16[256,256]{1,0:T(8,128)(2,1)S(1)}, bf16[256,256]{1,0:T(8,128)(2,1)S(1)}, u32[]{:S(2)}, u32[]{:S(2)}) collective-permute-start(bf16[256,256]{1,0:T(8,128)(2,1)S(1)} %fusion.5), channel_id=1, source_target_pairs={{0,2},{1,3},{2,0},{3,1},{4,6},{5,7},{6,4},{7,5},{8,10},{9,11},{10,... | collective-permute-start | bytes 393224 | tf_op jit(solution)/shard_map/ppermute | solution.py:33
  57.4 6.3 %collective-permute-start.13 = (bf16[256,256]{1,0:T(8,128)(2,1)S(1)}, bf16[256,256]{1,0:T(8,128)(2,1)S(1)}, u32[]{:S(2)}, u32[]{:S(2)}) collective-permute-start(bf16[256,256]{1,0:T(8,128)(2,1)S(1)} %get-tuple-element.68), channel_id=1, source_target_pairs={{0,4},{1,5},{2,6},{3,7},{4,8},{5,9},{6,10},{7,11},{8,12},{9,13},{1... | collective-permute-start | bytes 393224 | tf_op jit(solution)/shard_map/ppermute | solution.py:33
  58.3 7.1 %collective-permute-start.15 = (bf16[256,256]{1,0:T(8,128)(2,1)S(1)}, bf16[256,256]{1,0:T(8,128)(2,1)S(1)}, u32[]{:S(2)}, u32[]{:S(2)}) collective-permute-start(bf16[256,256]{1,0:T(8,128)(2,1)S(1)} %get-tuple-element.69), channel_id=1, source_target_pairs={{0,8},{1,9},{2,10},{3,11},{4,12},{5,13},{6,14},{7,15},{8,0},{9,1},... | collective-permute-start | bytes 393224 | tf_op jit(solution)/shard_map/ppermute | solution.py:33
  61.1 5.1 %collective-permute-start.14 = (bf16[256,256]{1,0:T(8,128)(2,1)S(1)}, bf16[256,256]{1,0:T(8,128)(2,1)S(1)}, u32[]{:S(2)}, u32[]{:S(2)}) collective-permute-start(bf16[256,256]{1,0:T(8,128)(2,1)S(1)} %get-tuple-element.70), channel_id=1, source_target_pairs={{0,12},{1,13},{2,14},{3,15},{4,0},{5,1},{6,2},{7,3},{8,4},{9,5},{1... | collective-permute-start | bytes 393224 | tf_op jit(solution)/shard_map/ppermute | solution.py:33
  72.1 5.1 %collective-permute-start.26 = (f32[8,128]{1,0:T(8,128)S(1)}, f32[8,128]{1,0:T(8,128)S(1)}, u32[]{:S(2)}, u32[]{:S(2)}) collective-permute-start(f32[8,128]{1,0:T(8,128)S(1)} %get-tuple-element.62), channel_id=1, source_target_pairs={{0,48},{1,49},{2,50},{3,51},{4,52},{5,53},{6,54},{7,55},{8,56},{9,... | collective-permute-start | bytes 12296 | tf_op jit(solution)/shard_map/ppermute | solution.py:39
  74.4 4.5 %collective-permute-start.25 = (f32[8,128]{1,0:T(8,128)S(1)}, f32[8,128]{1,0:T(8,128)S(1)}, u32[]{:S(2)}, u32[]{:S(2)}) collective-permute-start(f32[8,128]{1,0:T(8,128)S(1)} %get-tuple-element.62), channel_id=1, source_target_pairs={{0,32},{1,33},{2,34},{3,35},{4,36},{5,37},{6,38},{7,39},{8,40},{9,... | collective-permute-start | bytes 12296 | tf_op jit(solution)/shard_map/ppermute | solution.py:39
  75.8 3.6 %collective-permute-start.24 = (f32[8,128]{1,0:T(8,128)S(1)}, f32[8,128]{1,0:T(8,128)S(1)}, u32[]{:S(2)}, u32[]{:S(2)}) collective-permute-start(f32[8,128]{1,0:T(8,128)S(1)} %get-tuple-element.62), channel_id=1, source_target_pairs={{0,16},{1,17},{2,18},{3,19},{4,20},{5,21},{6,22},{7,23},{8,24},{9,... | collective-permute-start | bytes 12296 | tf_op jit(solution)/shard_map/ppermute | solution.py:39
  77.2 28.2 %collective-permute-start.19 = (bf16[2,4,128,256]{3,2,1,0:T(8,128)(2,1)S(1)}, bf16[2,4,128,256]{3,2,1,0:T(8,128)(2,1)S(1)}, u32[]{:S(2)}, u32[]{:S(2)}) collective-permute-start(bf16[2,4,128,256]{3,2,1,0:T(8,128)(2,1)S(1)} %get-tuple-element.54), channel_id=1, source_target_pairs={{0,1},{1,0},{2,3},{3,2},{4,5},{5,4},{6,7},{7,6},{8,9},{9,8},{10,11... | collective-permute-start | bytes 1572872 | tf_op jit(solution)/shard_map/ppermute | solution.py:33
  79.4 6.9 %collective-permute-start.29 = (f32[8,128]{1,0:T(8,128)S(1)}, f32[8,128]{1,0:T(8,128)S(1)}, u32[]{:S(2)}, u32[]{:S(2)}) collective-permute-start(f32[8,128]{1,0:T(8,128)S(1)} %add_add_fusion.4), channel_id=1, source_target_pairs={{0,65},{1,64},{2,67},{3,66},{4,69},{5,68},{6,71},{7,70},{8,73},{9,... | collective-permute-start | bytes 12296 | tf_op jit(solution)/shard_map/ppermute | solution.py:39
  82.5 4.2 %collective-permute-start.28 = (f32[8,128]{1,0:T(8,128)S(1)}, f32[8,128]{1,0:T(8,128)S(1)}, u32[]{:S(2)}, u32[]{:S(2)}) collective-permute-start(f32[8,128]{1,0:T(8,128)S(1)} %add_add_fusion.4), channel_id=1, source_target_pairs={{0,1},{1,0},{2,3},{3,2},{4,5},{5,4},{6,7},{7,6},{8,9},{9,8},{10,11... | collective-permute-start | bytes 12296 | tf_op jit(solution)/shard_map/ppermute | solution.py:39
  85.8 7.5 %collective-permute-start.27 = (f32[8,128]{1,0:T(8,128)S(1)}, f32[8,128]{1,0:T(8,128)S(1)}, u32[]{:S(2)}, u32[]{:S(2)}) collective-permute-start(f32[8,128]{1,0:T(8,128)S(1)} %add_add_fusion.4), channel_id=1, source_target_pairs={{0,64},{1,65},{2,66},{3,67},{4,68},{5,69},{6,70},{7,71},{8,72},{9,... | collective-permute-start | bytes 12296 | tf_op jit(solution)/shard_map/ppermute | solution.py:39
  93.4 5.9 %collective-permute-start.32 = (f32[8,128]{1,0:T(8,128)S(1)}, f32[8,128]{1,0:T(8,128)S(1)}, u32[]{:S(2)}, u32[]{:S(2)}) collective-permute-start(f32[8,128]{1,0:T(8,128)S(1)} %add_add_fusion.3), channel_id=1, source_target_pairs={{0,130},{1,131},{2,128},{3,129},{4,134},{5,135},{6,132},{7,133},{8... | collective-permute-start | bytes 12296 | tf_op jit(solution)/shard_map/ppermute | solution.py:39
  96.4 6.2 %collective-permute-start.31 = (f32[8,128]{1,0:T(8,128)S(1)}, f32[8,128]{1,0:T(8,128)S(1)}, u32[]{:S(2)}, u32[]{:S(2)}) collective-permute-start(f32[8,128]{1,0:T(8,128)S(1)} %add_add_fusion.3), channel_id=1, source_target_pairs={{0,2},{1,3},{2,0},{3,1},{4,6},{5,7},{6,4},{7,5},{8,10},{9,11},{10,... | collective-permute-start | bytes 12296 | tf_op jit(solution)/shard_map/ppermute | solution.py:39
  97.0 5.6 %collective-permute-start.30 = (f32[8,128]{1,0:T(8,128)S(1)}, f32[8,128]{1,0:T(8,128)S(1)}, u32[]{:S(2)}, u32[]{:S(2)}) collective-permute-start(f32[8,128]{1,0:T(8,128)S(1)} %add_add_fusion.3), channel_id=1, source_target_pairs={{0,128},{1,129},{2,130},{3,131},{4,132},{5,133},{6,134},{7,135},{8... | collective-permute-start | bytes 12296 | tf_op jit(solution)/shard_map/ppermute | solution.py:39
  97.5 23.8 %collective-permute-start.16 = (bf16[128,256]{1,0:T(8,128)(2,1)S(1)}, bf16[128,256]{1,0:T(8,128)(2,1)S(1)}, u32[]{:S(2)}, u32[]{:S(2)}) collective-permute-start(bf16[128,256]{1,0:T(8,128)(2,1)S(1)} %get-tuple-element.50), channel_id=1, source_target_pairs={{0,4},{1,5},{2,6},{3,7},{4,8},{5,9},{6,10},{7,11},{8,12},{9,13},{1... | collective-permute-start | bytes 196616 | tf_op jit(solution)/shard_map/ppermute | solution.py:33
  99.2 23.6 %collective-permute-start.17 = (bf16[128,256]{1,0:T(8,128)(2,1)S(1)}, bf16[128,256]{1,0:T(8,128)(2,1)S(1)}, u32[]{:S(2)}, u32[]{:S(2)}) collective-permute-start(bf16[128,256]{1,0:T(8,128)(2,1)S(1)} %get-tuple-element.51), channel_id=1, source_target_pairs={{0,8},{1,9},{2,10},{3,11},{4,12},{5,13},{6,14},{7,15},{8,0},{9,1},... | collective-permute-start | bytes 196616 | tf_op jit(solution)/shard_map/ppermute | solution.py:33
  102.6 4.9 %collective-permute-start.35 = (f32[8,128]{1,0:T(8,128)S(1)}, f32[8,128]{1,0:T(8,128)S(1)}, u32[]{:S(2)}, u32[]{:S(2)}) collective-permute-start(f32[8,128]{1,0:T(8,128)S(1)} %add_add_fusion.2), channel_id=1, source_target_pairs={{0,12},{1,13},{2,14},{3,15},{4,8},{5,9},{6,10},{7,11},{8,4},{9,5},... | collective-permute-start | bytes 12296 | tf_op jit(solution)/shard_map/ppermute | solution.py:39
  105.2 5.1 %collective-permute-start.34 = (f32[8,128]{1,0:T(8,128)S(1)}, f32[8,128]{1,0:T(8,128)S(1)}, u32[]{:S(2)}, u32[]{:S(2)}) collective-permute-start(f32[8,128]{1,0:T(8,128)S(1)} %add_add_fusion.2), channel_id=1, source_target_pairs={{0,8},{1,9},{2,10},{3,11},{4,12},{5,13},{6,14},{7,15},{8,0},{9,1},... | collective-permute-start | bytes 12296 | tf_op jit(solution)/shard_map/ppermute | solution.py:39
  105.4 6.9 %collective-permute-start.33 = (f32[8,128]{1,0:T(8,128)S(1)}, f32[8,128]{1,0:T(8,128)S(1)}, u32[]{:S(2)}, u32[]{:S(2)}) collective-permute-start(f32[8,128]{1,0:T(8,128)S(1)} %add_add_fusion.2), channel_id=1, source_target_pairs={{0,4},{1,5},{2,6},{3,7},{4,0},{5,1},{6,2},{7,3},{8,12},{9,13},{10,... | collective-permute-start | bytes 12296 | tf_op jit(solution)/shard_map/ppermute | solution.py:39
  107.5 15.4 %collective-permute-start.18 = (bf16[128,256]{1,0:T(8,128)(2,1)S(1)}, bf16[128,256]{1,0:T(8,128)(2,1)S(1)}, u32[]{:S(2)}, u32[]{:S(2)}) collective-permute-start(bf16[128,256]{1,0:T(8,128)(2,1)S(1)} %get-tuple-element.52), channel_id=1, source_target_pairs={{0,12},{1,13},{2,14},{3,15},{4,0},{5,1},{6,2},{7,3},{8,4},{9,5},{1... | collective-permute-start | bytes 196616 | tf_op jit(solution)/shard_map/ppermute | solution.py:33
  110.4 7.9 %collective-permute-start.20 = (bf16[4,128,256]{2,1,0:T(8,128)(2,1)S(1)}, bf16[4,128,256]{2,1,0:T(8,128)(2,1)S(1)}, u32[]{:S(2)}, u32[]{:S(2)}) collective-permute-start(bf16[4,128,256]{2,1,0:T(8,128)(2,1)S(1)} %fusion), channel_id=1, source_target_pairs={{0,2},{1,3},{2,0},{3,1},{4,6},{5,7},{6,4},{7,5},{8,10},{9,11},{10,... | collective-permute-start | bytes 786440 | tf_op jit(solution)/shard_map/ppermute | solution.py:33
  119.0 6.3 %collective-permute-start.21 = (bf16[128,256]{1,0:T(8,128)(2,1)S(1)}, bf16[128,256]{1,0:T(8,128)(2,1)S(1)}, u32[]{:S(2)}, u32[]{:S(2)}) collective-permute-start(bf16[128,256]{1,0:T(8,128)(2,1)S(1)} %get-tuple-element.56), channel_id=1, source_target_pairs={{0,4},{1,5},{2,6},{3,7},{4,8},{5,9},{6,10},{7,11},{8,12},{9,13},{1... | collective-permute-start | bytes 196616 | tf_op jit(solution)/shard_map/ppermute | solution.py:33
  119.1 6.2 %collective-permute-start.22 = (bf16[128,256]{1,0:T(8,128)(2,1)S(1)}, bf16[128,256]{1,0:T(8,128)(2,1)S(1)}, u32[]{:S(2)}, u32[]{:S(2)}) collective-permute-start(bf16[128,256]{1,0:T(8,128)(2,1)S(1)} %get-tuple-element.57), channel_id=1, source_target_pairs={{0,8},{1,9},{2,10},{3,11},{4,12},{5,13},{6,14},{7,15},{8,0},{9,1},... | collective-permute-start | bytes 196616 | tf_op jit(solution)/shard_map/ppermute | solution.py:33
  121.2 4.9 %collective-permute-start.23 = (bf16[128,256]{1,0:T(8,128)(2,1)S(1)}, bf16[128,256]{1,0:T(8,128)(2,1)S(1)}, u32[]{:S(2)}, u32[]{:S(2)}) collective-permute-start(bf16[128,256]{1,0:T(8,128)(2,1)S(1)} %get-tuple-element.58), channel_id=1, source_target_pairs={{0,12},{1,13},{2,14},{3,15},{4,0},{5,1},{6,2},{7,3},{8,4},{9,5},{1... | collective-permute-start | bytes 196616 | tf_op jit(solution)/shard_map/ppermute | solution.py:33

commit v2 on v1

v2 whole, which is shorter than its diff:
```python
import functools
import math

import jax
import jax.numpy as jnp
from jax import lax
from jax.experimental import pallas as pl
from jax.experimental.pallas import tpu as pltpu
from jax.sharding import PartitionSpec as P


EPS = 1e-06
NEG = -1e30
HEAD = 128
ROWS_A = 160
ROWS_B = 256 - ROWS_A
BLK = 128
NX = 4
F32 = jnp.float32
BF16 = jnp.bfloat16
NT = (((1,), (1,)), ((), ()))
VMEM_LIMIT = 48 * 1024 * 1024
VMEM_MOST = 63 * 1024 * 1024


def index_of(x, y, c):
    return (x % 4) * 4 + (y % 2) * 2 + (c % 2)


def shift(value, dx, dy, dc):
    pairs = []
    for x in range(4):
        for y in range(2):
            for c in range(2):
                pairs.append((index_of(x, y, c), index_of(x + dx, y + dy, c + dc)))
    return lax.ppermute(value, "seq", pairs)


def flip(value, dp_bits, seq_bits):
    size = 256
    pairs = [(i, ((i // 16) ^ dp_bits) * 16 + ((i % 16) ^ seq_bits)) for i in range(size)]
    return lax.ppermute(value, ("dp", "seq"), pairs)


def sum_over_four(value, first, second):
    both = (first[0] ^ second[0], first[1] ^ second[1])
    a, b, c = (flip(value, *bits) for bits in (first, second, both))
    return (value + a) + (b + c)


def along_z(value, step):
    pairs = [((i // 8) * 8 + (i + step) % 8, i) for i in range(16)]
    return lax.ppermute(value, "dp", pairs)


def call(kernel, outs, *args, scratch=(), after=(), hbm_in=False, hbm_out=False, limit=VMEM_LIMIT, flops=1):
    vmem, hbm = pl.BlockSpec(memory_space=pltpu.VMEM), pl.BlockSpec(memory_space=pltpu.HBM)
    used = len(args)

    def body(*refs):
        place = lax.axis_index("seq")
        at = (place // 4, (place // 2) % 2, place % 2, lax.axis_index("dp") % 8)
        kernel(at, *refs[:used], *refs[used + len(after) :])

    return pl.pallas_call(
        body,
        out_shape=outs,
        in_specs=[hbm if hbm_in else vmem] * used + [pl.BlockSpec(memory_space=pl.ANY)] * len(after),
        out_specs=[hbm if hbm_out else vmem] * len(outs),
        scratch_shapes=list(scratch),
        compiler_params=pltpu.CompilerParams(vmem_limit_bytes=limit),
        cost_estimate=pl.CostEstimate(flops=flops, bytes_accessed=1, transcendentals=0),
    )(*args, *after)


def sds(shape, dtype=BF16):
    return jax.ShapeDtypeStruct(shape, dtype)


def goal_kernel(
    at, mapping, teacher, q_ref, k_ref, v_ref, a_other, b_other, a_own, b_own, out_0, out_1, out_2, out_3,
    turned, held_map, held, a_held, b_held, packed, sems, out_sems, pack_sems,
):
    x, y, c = at[0], at[1], at[2]
    copies = [pltpu.make_async_copy(mapping, held_map, sems.at[4])]
    for n in range(4):
        lanes = slice(512 * n, 512 * (n + 1))
        copies.append(pltpu.make_async_copy(teacher.at[:, lanes], held.at[:, lanes], sems.at[n]))
    for copy in copies:
        copy.start()
    outs = (out_0, out_1, out_2, out_3)
    pieces = []
    for dx in range(NX):
        to = (x + dx) % NX
        wide = pl.ds(pl.multiple_of(to * 256, 256), 256)
        narrow = pl.ds(pl.multiple_of(to * 128, 128), 128)
        for n, (ref, cols, lanes) in enumerate(
            ((q_ref, wide, slice(0, 256)), (k_ref, narrow, slice(256, 384)), (v_ref, narrow, slice(384, 512)))
        ):
            piece = pltpu.make_async_copy(ref.at[:, cols], packed.at[dx, :, lanes], pack_sems.at[3 * dx + n])
            piece.start()
            pieces.append(piece)
    copies[0].wait()
    for n in range(NX):
        turned[256 * n : 256 * (n + 1), :] = held_map[:, 256 * n : 256 * (n + 1)].T
    for copy in copies[1:] + pieces:
        copy.wait()
    stores = []
    for dx in range(NX):
        copy = pltpu.make_async_copy(packed.at[dx], outs[dx], pack_sems.at[12 + dx])
        copy.start()
        stores.append(copy)
    for core, a_out, b_out in ((1, a_other, b_other), (0, a_own, b_own)):
        for dy in range(2):
            blocks = [4 * i + 2 * ((y + dy) % 2) + (c + core) % 2 for i in range(4)]
            columns = [held[:, pl.ds(pl.multiple_of(block * BLK, BLK), BLK)] for block in blocks]
            columns = jnp.concatenate(columns, axis=1)
            for dx in range(NX):
                rows = pl.ds(pl.multiple_of(((x + dx) % NX) * 256, 256), 256)
                part = jnp.dot(turned[rows, :], columns, preferred_element_type=F32).astype(BF16)
                a_held[core, dx, dy] = part[:ROWS_A]
                b_held[core, dy, dx] = part[ROWS_A:]
            for n, (held_ref, out) in enumerate(
                ((a_held.at[core, :, dy], a_out.at[:, dy]), (b_held.at[core, dy], b_out.at[dy]))
            ):
                copy = pltpu.make_async_copy(held_ref, out, out_sems.at[4 * core + 2 * dy + n])
                copy.start()
                stores.append(copy)
    for copy in stores:
        copy.wait()


def kv_kernel(at, p_0, p_1, p_2, p_3, out):
    for dx, part in enumerate((p_0, p_1, p_2, p_3)):
        out[dx] = part[:, 256:512]


def pair_kernel(at, own, other, out):
    out[0] = own[...]
    out[1] = other[...]


def unit_rows(rows):
    scale = lax.rsqrt(jnp.mean(rows * rows, axis=-1, keepdims=True) + EPS)
    return rows * scale, scale


def forward_kernel(
    at, kv_both, kv_swapped, q_0, q_1, q_2, q_3, segs, q_gain, k_gain,
    k_hat, k_turned, v_all, k_unit, q_hat, outputs, log_total, spans, s_ref, v_turned,
):
    x, y, c = at[0], at[1], at[2]
    before = []
    for d in range(3):
        hits = jnp.sum((segs[...] == d).astype(F32), axis=1, keepdims=True)
        before.append(jnp.sum(hits, axis=0, keepdims=True).astype(jnp.int32))
    lane = lax.broadcasted_iota(jnp.int32, (1, BLK), 1)
    for i in range(NX):
        block = 4 * i + 2 * y + c
        own = segs[pl.ds(block, 1), :]
        first = sum(jnp.where(own > d, before[d], 0) for d in range(3))
        spans[i : i + 1, :] = jnp.concatenate([first, first], axis=1)
        here = block * BLK + lane
        spans[4 + i : 5 + i, :] = jnp.concatenate([here, here], axis=1)
    for part, dy, dc in ((kv_both, 0, 0), (kv_both, 1, 0), (kv_swapped, 0, 1), (kv_swapped, 1, 1)):
        for dx in range(NX):
            block = ((x + NX - dx) % NX) * 4 + ((y + dy) % 2) * 2 + (c + dc) % 2
            rows = pl.ds(pl.multiple_of(block * BLK, BLK), BLK)
            unit, _ = unit_rows(part[dy, dx, :, 0:128].astype(F32))
            hat = (unit * k_gain[...]).astype(BF16)
            k_unit[rows, :] = unit
            k_hat[rows, :] = hat
            k_turned[:, rows] = hat.T
            value = part[dy, dx, :, 128:256]
            v_all[rows, :] = value
            v_turned[:, rows] = value.T
    for dx, part in enumerate((q_0, q_1, q_2, q_3)):
        i = (x + NX - dx) % NX
        for g in range(2):
            unit, _ = unit_rows(part[:, g * 128 : (g + 1) * 128].astype(F32))
            q_hat[i, g * 128 : (g + 1) * 128, :] = (unit * q_gain[...]).astype(BF16)
    factor = HEAD ** (-0.5)
    for i in range(NX):
        start = spans[i : i + 1, :]
        place = spans[4 + i : 5 + i, :]
        top = jnp.full((1, 256), NEG, F32)
        for j in range(2 * (i + 1)):
            rows = slice(256 * j, 256 * (j + 1))
            s = lax.dot_general(k_hat[rows, :], q_hat[i], NT, preferred_element_type=F32) * factor
            at_key = lax.broadcasted_iota(jnp.int32, (256, 256), 0) + 256 * j
            allowed = at_key >= start
            if j >= 2 * i:
                allowed = allowed & (at_key <= place)
            s = jnp.where(allowed, s, NEG)
            s_ref[rows, :] = s
            top = jnp.maximum(top, jnp.max(s, axis=0, keepdims=True))
        total = jnp.zeros((1, 256), F32)
        for j in range(2 * (i + 1)):
            rows = slice(256 * j, 256 * (j + 1))
            total += jnp.sum(jnp.exp(s_ref[rows, :] - top), axis=0, keepdims=True)
        log_row = top + jnp.log(total)
        log_total[i : i + 1, :] = log_row
        result = jnp.zeros((128, 256), F32)
        for j in range(2 * (i + 1)):
            rows = slice(256 * j, 256 * (j + 1))
            probs_low = jnp.exp(s_ref[rows, :] - log_row).astype(BF16)
            result += jnp.dot(v_turned[:, rows], probs_low, preferred_element_type=F32)
        outputs[i] = result


def backward_kernel(
    at, k_hat, k_turned, v_all, k_unit, q_hat, outputs, log_total, goal_a, goal_b,
    q_0, q_1, q_2, q_3, spans, q_gain, dq_0, dq_1, dq_2, dq_3, send_c, keep_c, gains,
    d_key, d_value, q_rows, dq_rows,
):
    x, y, c = at[0], at[1], at[2]
    factor = HEAD ** (-0.5)
    for dx, part in enumerate((q_0, q_1, q_2, q_3)):
        i = (x + NX - dx) % NX
        for g in range(2):
            q_rows[i, g * 128 : (g + 1) * 128, :] = part[:, g * 128 : (g + 1) * 128]
    q_part = jnp.zeros((1, 128), F32)
    for i in reversed(range(NX)):
        start = spans[i : i + 1, :]
        place = spans[4 + i : 5 + i, :]
        log_row = log_total[i : i + 1, :]
        lanes = slice(128 * i, 128 * (i + 1))
        goal = jnp.concatenate([goal_a[:, lanes], goal_b[:, lanes]], axis=0)
        goal = jnp.concatenate([goal[0:128], goal[128:256]], axis=1)
        out = outputs[i]
        d_out = (out - goal).astype(BF16)
        delta = jnp.sum(d_out.astype(F32) * out, axis=0, keepdims=True)
        d_out_rows = d_out.T
        query = q_hat[i]
        d_query = jnp.zeros((128, 256), F32)
        for j in range(2 * (i + 1)):
            rows = slice(256 * j, 256 * (j + 1))
            s = lax.dot_general(k_hat[rows, :], query, NT, preferred_element_type=F32) * factor
            at_key = lax.broadcasted_iota(jnp.int32, (256, 256), 0) + 256 * j
            allowed = at_key >= start
            if j >= 2 * i:
                allowed = allowed & (at_key <= place)
            probs = jnp.exp(jnp.where(allowed, s, NEG) - log_row)
            d_probs = jnp.dot(v_all[rows, :], d_out, preferred_element_type=F32)
            d_scores = (factor * probs * (d_probs - delta)).astype(BF16)
            new_value = jnp.dot(probs.astype(BF16), d_out_rows, preferred_element_type=F32)
            new_key = jnp.dot(d_scores, query, preferred_element_type=F32)
            if i == NX - 1:
                d_value[rows, :] = new_value
                d_key[rows, :] = new_key
            else:
                d_value[rows, :] += new_value
                d_key[rows, :] += new_key
            d_query += jnp.dot(k_turned[:, rows], d_scores, preferred_element_type=F32)
        unit, scale = unit_rows(q_rows[i].astype(F32))
        grad = d_query.T
        q_part += jnp.sum(grad * unit, axis=0, keepdims=True)
        grad_unit = grad * q_gain[...]
        dq = scale * (grad_unit - unit * jnp.mean(grad_unit * unit, axis=-1, keepdims=True))
        dq = dq.astype(BF16)
        dq_rows[i, :, 0:128] = dq[0:128]
        dq_rows[i, :, 128:256] = dq[128:256]
    for dx, out in enumerate((dq_0, dq_1, dq_2, dq_3)):
        out[...] = dq_rows[(x + dx) % NX]
    k_part = jnp.zeros((1, 128), F32)
    for j in range(8):
        rows = slice(256 * j, 256 * (j + 1))
        k_part += jnp.sum(d_key[rows, :] * k_unit[rows, :], axis=0, keepdims=True)
    gains[...] = jnp.concatenate([q_part, k_part, jnp.zeros((6, 128), F32)], axis=0)
    for out, dc in ((keep_c, 0), (send_c, 1)):
        for dy in range(2):
            for i in range(NX):
                block = i * 4 + ((y + dy) % 2) * 2 + (c + dc) % 2
                rows = pl.ds(pl.multiple_of(block * BLK, BLK), BLK)
                out[dy, i, :, 0:128] = d_key[rows, :].astype(BF16)
                out[dy, i, :, 128:256] = d_value[rows, :].astype(BF16)


def key_kernel(at, mine, from_y, kv_0, k_gain, gains, dq_0, dq_1, dq_2, dq_3, out_0, out_1, out_2, out_3):
    x = at[0]
    for dx, (dq, out) in enumerate(((dq_0, out_0), (dq_1, out_1), (dq_2, out_2), (dq_3, out_3))):
        i = (x + dx) % NX
        total = mine[i] + from_y[i].astype(F32)
        raw = kv_0[(NX - dx) % NX, :, 0:128].astype(F32)
        unit, scale = unit_rows(raw)
        grad_unit = total[:, 0:128] * k_gain[...]
        dk = scale * (grad_unit - unit * jnp.mean(grad_unit * unit, axis=-1, keepdims=True))
        out[0:BLK, 0:256] = dq[...]
        out[0:BLK, 256:384] = dk.astype(BF16)
        out[0:BLK, 384:512] = total[:, 128:256].astype(BF16)
        rest = jnp.concatenate([gains[...], jnp.zeros((8, HEAD), F32)], axis=0)
        for term in range(3):
            high = rest.astype(BF16)
            out[BLK:, 128 * term : 128 * (term + 1)] = high
            rest = rest - high.astype(F32)
        out[BLK:, 384:512] = jnp.zeros((16, HEAD), BF16)


def add_kernel(at, a, b, out):
    out[...] = a[...] + b[...]


def gains_kernel(at, p_0, p_1, p_2, p_3, out, held):
    x = at[0]
    for dx, part in enumerate((p_0, p_1, p_2, p_3)):
        terms = [part[BLK:, 128 * t : 128 * (t + 1)].astype(F32) for t in range(3)]
        held[(x + NX - dx) % NX] = (terms[0] + terms[1]) + terms[2]
    total = (held[0] + held[1]) + (held[2] + held[3])
    out[...] = total[0:8]


def total_kernel(at, mine, above, below, q_out, k_out, held):
    z = at[3]
    for part, step in ((mine, 0), (above, 3), (below, 5)):
        for row, more in ((0, 0), (2, 1), (4, 7)):
            held[(z + step + more) % 8] = part[row : row + 2, :]
    total = ((held[0] + held[1]) + (held[2] + held[3])) + ((held[4] + held[5]) + (held[6] + held[7]))
    q_out[...] = total[0:1] * (1.0 / math.sqrt(262144))
    k_out[...] = total[1:2] * (1.0 / math.sqrt(131072))


def unpack_kernel(at, p_0, p_1, p_2, p_3, dq, dk, dv):
    x = at[0]
    for dx, part in enumerate((p_0, p_1, p_2, p_3)):
        j = (x + NX - dx) % NX
        dq[:, pl.ds(pl.multiple_of(j * 256, 256), 256)] = part[0:BLK, 0:256]
        dk[:, pl.ds(pl.multiple_of(j * 128, 128), 128)] = part[0:BLK, 256:384]
        dv[:, pl.ds(pl.multiple_of(j * 128, 128), 128)] = part[0:BLK, 384:512]


def on_device(q_in, k_in, v_in, q_gain, k_gain, seg_ids, teacher, mapping):
    q_gain_row, k_gain_row = q_gain.reshape(1, HEAD), k_gain.reshape(1, HEAD)
    teacher_slab = teacher[0]

    a_shape, b_shape = sds((NX, 2, ROWS_A, 512)), sds((2, NX, ROWS_B, 512))
    a_other, b_other, a_own, b_own, *packed = call(
        goal_kernel, [a_shape, b_shape, a_shape, b_shape] + [sds((BLK, 512))] * NX,
        mapping, teacher_slab, q_in[0], k_in[0], v_in[0],
        hbm_in=True, hbm_out=True, limit=VMEM_MOST, flops=6_000_000_000,
        scratch=[
            pltpu.VMEM((1024, 448), BF16), pltpu.VMEM((448, 1024), BF16), pltpu.VMEM((448, 2048), BF16),
            pltpu.VMEM((2, NX, 2, ROWS_A, 512), BF16), pltpu.VMEM((2, 2, NX, ROWS_B, 512), BF16),
            pltpu.VMEM((NX, BLK, 512), BF16),
            pltpu.SemaphoreType.DMA((5,)), pltpu.SemaphoreType.DMA((8,)), pltpu.SemaphoreType.DMA((16,)),
        ],
    )
    pieces = [packed[0]] + [shift(packed[dx], dx, 0, 0) for dx in (1, 2, 3)]
    b_swapped = shift(b_other, 0, 0, 1)
    a_swapped = shift(a_other, 0, 0, 1)
    b_send = (b_own[1].astype(F32) + b_swapped[1].astype(F32)).astype(BF16)
    b_keep = b_own[0].astype(F32) + b_swapped[0].astype(F32)
    b_y = shift(b_send, 0, 1, 0)
    parts_a = [
        (a_own[dx].astype(F32) + a_swapped[dx].astype(F32)).astype(BF16) for dx in range(NX)
    ]
    from_x = [shift(parts_a[dx], dx, 0, 0) for dx in (1, 2, 3)]

    (kv_0,) = call(kv_kernel, [sds((NX, BLK, 256))], *pieces, after=[b_send])
    kv_y = shift(kv_0, 0, 1, 0)
    kv_y, from_x, b_y = lax.optimization_barrier((kv_y, from_x, b_y))
    (kv_both,) = call(pair_kernel, [sds((2, NX, BLK, 256))], kv_0, kv_y)
    kv_swapped = shift(kv_both, 0, 0, 1)

    fwd = call(
        forward_kernel,
        [
            sds((2048, HEAD)), sds((HEAD, 2048)), sds((2048, HEAD)), sds((2048, HEAD), F32),
            sds((NX, 256, HEAD)), sds((NX, HEAD, 256), F32), sds((8, 256), F32), sds((8, 256), jnp.int32),
        ],
        kv_both, kv_swapped, *pieces, seg_ids.reshape(16, BLK), q_gain_row, k_gain_row,
        scratch=[pltpu.VMEM((2048, 256), F32), pltpu.VMEM((HEAD, 2048), BF16)],
    )

    sum_a = sum((part.astype(F32) for part in from_x), parts_a[0].astype(F32))
    sum_b = b_keep + b_y.astype(F32)
    a_y = shift(sum_a[1].astype(BF16), 0, 1, 0)
    b_x = [shift(sum_b[dx].astype(BF16), dx, 0, 0) for dx in (1, 2, 3)]
    fwd, a_y, b_x = lax.optimization_barrier((fwd, a_y, b_x))
    goal_a = sum_a[0] + a_y.astype(F32)
    goal_b = sum((part.astype(F32) for part in b_x), sum_b[0])

    k_hat, k_turned, v_all, k_unit, q_hat, outputs, log_total, spans = fwd
    bwd = call(
        backward_kernel,
        [sds((BLK, 256))] * NX + [sds((2, NX, BLK, 256))] * 2 + [sds((8, HEAD), F32)],
        k_hat, k_turned, v_all, k_unit, q_hat, outputs, log_total, goal_a, goal_b,
        *pieces, spans, q_gain_row,
        scratch=[
            pltpu.VMEM((2048, HEAD), F32), pltpu.VMEM((2048, HEAD), F32),
            pltpu.VMEM((NX, 256, HEAD), BF16), pltpu.VMEM((NX, BLK, 256), BF16),
        ],
    )
    dq_parts, send_c, keep_c, gains = bwd[:4], bwd[4], bwd[5], bwd[6]
    sum_c = keep_c.astype(F32) + shift(send_c, 0, 0, 1).astype(F32)
    y_send, gains, gains_c = lax.optimization_barrier(
        (sum_c[1].astype(BF16), gains, shift(gains, 0, 0, 1))
    )
    from_y = shift(y_send, 0, 1, 0)
    (gains,) = call(add_kernel, [sds((8, HEAD), F32)], gains, gains_c, flops=20_000_000_000)
    gains = sum_over_four(gains, (0, 2), (8, 0))
    above, below = along_z(gains, 1), along_z(gains, -1)
    gains = jnp.concatenate([gains[0:2], above[0:2], below[0:2], gains[6:8]], axis=0)
    back = call(
        key_kernel, [sds((BLK + 16, 512))] * NX, sum_c[0], from_y, kv_0, k_gain_row, gains, *dq_parts,
    )
    got = [back[0]] + [shift(back[dx], dx, 0, 0) for dx in (1, 2, 3)]
    (total,) = call(
        gains_kernel, [sds((8, HEAD), F32)], *got,
        scratch=[pltpu.VMEM((NX, 16, HEAD), F32)],
    )
    q_gain_grad, key_gain_gradient = call(
        total_kernel, [sds((1, HEAD), F32)] * 2, total, along_z(total, 3), along_z(total, -3),
        scratch=[pltpu.VMEM((8, 2, HEAD), F32)],
    )
    dq, dk, dv = call(
        unpack_kernel, [sds((BLK, 1024)), sds((BLK, 512)), sds((BLK, 512))], *got,
    )
    return dq[None], dk[None], dv[None], q_gain_grad.reshape(HEAD), key_gain_gradient.reshape(HEAD)


def solution(mesh):
    return jax.shard_map(
        on_device,
        mesh=mesh,
        in_specs=(
            P("dp", "seq", None),
            P("dp", "seq", None),
            P("dp", "seq", None),
            P(),
            P(),
            P("dp", None),
            P("dp", "seq", None),
            P("seq", None),
        ),
        out_specs=(P("dp", "seq", None), P("dp", "seq", None), P("dp", "seq", None), P(), P()),
        check_vma=False,
    )
```

time: 128 us -> 93.1 us (0.73)
  starting transfers between devices: 58.6 us -> 34.9 us
  Pallas kernels: 24.6 us -> 16.9 us
  local copies, waits for them, and re-layouts: 5.08 us -> 0.14 us
  waiting for transfers between devices: 33.7 us -> 35.9 us
    ppermute x24 -> x21, starting transfers between devices: 38.8 us -> 22.1 us  [shift(): return lax.ppermute(value, 'seq', pairs)]
    ppermute x12 -> x3, starting transfers between devices: 19.8 us -> 4.79 us  [flip(): return lax.ppermute(value, ('dp', 'seq'), pairs)]
    ppermute x0 -> x4, waiting for transfers between devices: none -> 9.09 us  [along_z(): return lax.ppermute(value, 'dp', pairs)]
    ppermute x12 -> x3, waiting for transfers between devices: 10.5 us -> 1.45 us  [flip(): return lax.ppermute(value, ('dp', 'seq'), pairs)]
    ppermute x0 -> x4, starting transfers between devices: none -> 8.07 us  [along_z(): return lax.ppermute(value, 'dp', pairs)]
    pallas_call x8 -> x10, Pallas kernels: 24.6 us -> 16.9 us  [call(): pl.pallas_call(body, out_shape=outs, in_specs=[hbm if hbm_in else vmem] *...]
    unnamed x18 -> x10, local copies, waits for them, and re-layouts: 4.28 us -> 0.03 us
    convert_element_type x0 -> x2, other arithmetic: none -> 2.59 us  [the longest x1 1.49 us: on_device(): (a_own[dx].astype(F32) + a_swapped[dx].astype(F32)).astype(BF16)]
  transfers between devices with their start and end apart: 36 -> 28, of which waited for: 15 -> 14; matrix products, arithmetic and copies ran while one was open for 4% -> 3% of each run, Pallas kernels for 13% -> 5%
where the time goes in v2:
time: 93.1 us; the launch traced here: 92.9 us
  waiting for transfers between devices  35.9 us (39%)
  starting transfers between devices  34.9 us (37%)
  Pallas kernels  16.9 us (18%)
  other arithmetic  4.16 us (4%)
    ppermute x21, waiting for transfers between devices, shift(): return lax.ppermute(value, 'seq', pairs)  25.4 us
    ppermute x21, starting transfers between devices, shift(): return lax.ppermute(value, 'seq', pairs)  22.1 us
    pallas_call x10, Pallas kernels, call(): pl.pallas_call(body, out_shape=outs, in_specs=[hbm if hbm_in else vmem] *...  16.9 us
    ppermute x4, waiting for transfers between devices, along_z(): return lax.ppermute(value, 'dp', pairs)  9.09 us
    ppermute x4, starting transfers between devices, along_z(): return lax.ppermute(value, 'dp', pairs)  8.07 us
    ppermute x3, starting transfers between devices, flip(): return lax.ppermute(value, ('dp', 'seq'), pairs)  4.79 us
  transfers between devices with their start and end apart: 28, of which 14 were waited for; matrix products, arithmetic and copies ran while one was open for 3% of the time, Pallas kernels for 5%

profile of v2, /device:TPU:32, one launch (start us, length us, event | category | flops | bytes accessed | tf_op | source)
XLA Modules:
  0.0 92.9 jit_solution(9212799529369998877)
XLA Ops:
  0.6 5.7 %shard_map.119 = (bf16[4,2,160,512]{3,2,1,0:T(8,128)(2,1)}, bf16[2,4,96,512]{3,2,1,0:T(8,128)(2,1)}, bf16[4,2,160,512]{3,2,1,0:T(8,128)(2,1)}, bf16[2,4,96,512]{...) custom-call(bf16[448,1024]{1,0:T(8,128)(2,1)} %refs_0_.1, ...), custom_call_target="tpu_custom_call" | custom-call | flops 6000000000 | bytes 1 | tf_op jit(solution)/shard_map/pallas_call | solution.py:65
  6.4 0.1 collective-permute-start.5
  6.5 0.5 collective-permute-start.3
  7.0 1.5 %collective-permute-start = (bf16[128,512]{1,0:T(8,128)(2,1)}, bf16[128,512]{1,0:T(8,128)(2,1)S(1)}, u32[]{:S(2)}, u32[]{:S(2)}) collective-permute-start(bf16[128,512]{1,0:T(8,128)(2,1)} %get-tuple-element.58), channel_id=1, source_target_pairs={{0,4},{1,5},{2,6},{3,7},{4,8},{5,9},{6,10},{7,11},{8,12},{9,13},{1... | collective-permute-start | bytes 393224 | tf_op jit(solution)/shard_map/ppermute | solution.py:36
  8.4 2.7 %collective-permute-start.1 = (bf16[128,512]{1,0:T(8,128)(2,1)}, bf16[128,512]{1,0:T(8,128)(2,1)S(1)}, u32[]{:S(2)}, u32[]{:S(2)}) collective-permute-start(bf16[128,512]{1,0:T(8,128)(2,1)} %get-tuple-element.59), channel_id=1, source_target_pairs={{0,8},{1,9},{2,10},{3,11},{4,12},{5,13},{6,14},{7,15},{8,0},{9,1},... | collective-permute-start | bytes 393224 | tf_op jit(solution)/shard_map/ppermute | solution.py:36
  11.2 1.4 %collective-permute-start.2 = (bf16[128,512]{1,0:T(8,128)(2,1)}, bf16[128,512]{1,0:T(8,128)(2,1)S(1)}, u32[]{:S(2)}, u32[]{:S(2)}) collective-permute-start(bf16[128,512]{1,0:T(8,128)(2,1)} %get-tuple-element.60), channel_id=1, source_target_pairs={{0,12},{1,13},{2,14},{3,15},{4,0},{5,1},{6,2},{7,3},{8,4},{9,5},{1... | collective-permute-start | bytes 393224 | tf_op jit(solution)/shard_map/ppermute | solution.py:36
  12.6 0.0 collective-permute-done.3
  12.6 1.1 %fusion.2.refs_4_ = bf16[4,96,512]{2,1,0:T(8,128)(2,1)S(1)} fusion(bf16[2,4,96,512]{3,2,1,0:T(8,128)(2,1)S(1)} %collective-permute-done.3, bf16[2,4,96,512]{3,2,1,0:T(8,128)(2,1)} %get-tuple-element.61), kind=kLoop, calls=%fused_computation.12 | loop fusion | flops 786432 | bytes 1179648 | tf_op jit(solution)/shard_map/convert_element_type | solution.py:350
  13.7 3.3 %collective-permute-start.9 = (bf16[4,96,512]{2,1,0:T(8,128)(2,1)S(1)}, bf16[4,96,512]{2,1,0:T(8,128)(2,1)S(1)}, u32[]{:S(2)}, u32[]{:S(2)}) collective-permute-start(bf16[4,96,512]{2,1,0:T(8,128)(2,1)S(1)} %fusion.2.refs_4_), channel_id=1, source_target_pairs={{0,2},{1,3},{2,0},{3,1},{4,6},{5,7},{6,4},{7,5},{8,10},{9,11},{10,... | collective-permute-start | bytes 1179656 | tf_op jit(solution)/shard_map/ppermute | solution.py:36
  17.0 0.0 collective-permute-done.5
  17.0 1.5 %fusion.5 = (bf16[2,160,512]{2,1,0:T(8,128)(2,1)S(1)}, bf16[2,160,512]{2,1,0:T(8,128)(2,1)S(1)}, bf16[2,160,512]{2,1,0:T(8,128)(2,1)S(1)}) fusion(bf16[4,2,160,512]{3,2,1,0:T(8,128)(2,1)S(1)} %collective-permute-done.5, bf16[4,2,160,512]{3,2,1,0:T(8,128)(2,1)} %get-tuple-element.63), kind=kLoop, calls=%fused_computation.15 | loop fusion | flops 1966080 | bytes 2949120 | tf_op jit(solution)/shard_map/convert_element_type | solution.py:354
  18.5 1.0 %collective-permute-start.8 = (bf16[2,160,512]{2,1,0:T(8,128)(2,1)S(1)}, bf16[2,160,512]{2,1,0:T(8,128)(2,1)S(1)}, u32[]{:S(2)}, u32[]{:S(2)}) collective-permute-start(bf16[2,160,512]{2,1,0:T(8,128)(2,1)S(1)} %get-tuple-element.111), channel_id=1, source_target_pairs={{0,12},{1,13},{2,14},{3,15},{4,0},{5,1},{6,2},{7,3},{8,4},{9,5},{1... | collective-permute-start | bytes 983048 | tf_op jit(solution)/shard_map/ppermute | solution.py:36
  19.5 0.0 collective-permute-done.refs_1_.refs_3_.refs_10_
  19.5 1.7 %collective-permute-start.7 = (bf16[2,160,512]{2,1,0:T(8,128)(2,1)S(1)}, bf16[2,160,512]{2,1,0:T(8,128)(2,1)S(1)}, u32[]{:S(2)}, u32[]{:S(2)}) collective-permute-start(bf16[2,160,512]{2,1,0:T(8,128)(2,1)S(1)} %get-tuple-element.112), channel_id=1, source_target_pairs={{0,8},{1,9},{2,10},{3,11},{4,12},{5,13},{6,14},{7,15},{8,0},{9,1},... | collective-permute-start | bytes 983048 | tf_op jit(solution)/shard_map/ppermute | solution.py:36
  21.3 0.4 collective-permute-start.4
  21.7 9.5 %collective-permute-done.4.refs_1_ = bf16[4,128,256]{2,1,0:T(8,128)(2,1)S(1)} collective-permute-done((bf16[4,128,256]{2,1,0:T(8,128)(2,1)S(1)}, bf16[4,128,256]{2,1,0:T(8,128)(2,1)S(1)}, u32[]{:S(2)}, u32[]{:S(2)}) %collective-permute-start.4) | collective-permute-done | bytes 262176 | tf_op jit(solution)/shard_map/ppermute | solution.py:36
  31.2 0.0 collective-permute-done.9
  31.2 2.4 %collective-permute-done.8 = bf16[2,160,512]{2,1,0:T(8,128)(2,1)S(1)} collective-permute-done((bf16[2,160,512]{2,1,0:T(8,128)(2,1)S(1)}, bf16[2,160,512]{2,1,0:T(8,128)(2,1)S(1)}, u32[]{:S(2)}, u32[]{:S(2)}) %collective-permute-start.8) | collective-permute-done | bytes 327712 | tf_op jit(solution)/shard_map/ppermute | solution.py:36
  33.6 0.0 collective-permute-done.7
  33.6 3.7 %collective-permute-done.6 = bf16[2,160,512]{2,1,0:T(8,128)(2,1)S(1)} collective-permute-done((bf16[2,160,512]{2,1,0:T(8,128)(2,1)S(1)}, bf16[2,160,512]{2,1,0:T(8,128)(2,1)S(1)}, u32[]{:S(2)}, u32[]{:S(2)}) %collective-permute-start.6) | collective-permute-done | bytes 327712 | tf_op jit(solution)/shard_map/ppermute | solution.py:36
  37.3 1.2 %fusion.1 = f32[2,160,512]{2,1,0:T(8,128)S(1)} fusion(bf16[2,160,512]{2,1,0:T(8,128)(2,1)S(1)} %collective-permute-done.8, bf16[2,160,512]{2,1,0:T(8,128)(2,1)S(1)} %collective-permute-done.7, bf16[2,160,512]{2,1,0:T(8,128)(2,1)S(1)} %collective-permute-done.6, bf16[4,2,160,512]{3,2,1,0:T(8,128)(2,1)S(1)} %collective-permute-done.5, ...), kind=kLoop, calls=%fused_computation.5 | loop fusion | flops 1802240 | bytes 2293760 | tf_op jit(solution)/shard_map/add | solution.py:374
  38.5 0.4 collective-permute-start.11
  38.9 0.0 copy-start.1
  38.9 0.0 copy-start.2
  38.9 0.0 copy-start.3
  39.0 0.1 collective-permute-start.10
  39.1 0.2 fusion.13
  39.3 0.7 collective-permute-start.14
  40.0 0.8 collective-permute-start.13
  40.8 0.8 collective-permute-start.12
  41.6 4.1 %shard_map.122 = (bf16[2048,128]{1,0:T(8,128)(2,1)S(1)}, bf16[128,2048]{1,0:T(8,128)(2,1)S(1)}, bf16[2048,128]{1,0:T(8,128)(2,1)S(1)}, f32[2048,128]{1,0:T(8,128...) custom-call(bf16[2,4,128,256]{3,2,1,0:T(8,128)(2,1)S(1)} %shard_map., ...), custom_call_target="tpu_custom_call" | custom-call | flops 1 | bytes 1 | tf_op jit(solution)/shard_map/pallas_call | solution.py:65
  45.7 0.0 collective-permute-done.14
  45.7 1.0 %collective-permute-done.13 = bf16[96,512]{1,0:T(8,128)(2,1)S(1)} collective-permute-done((bf16[96,512]{1,0:T(8,128)(2,1)S(1)}, bf16[96,512]{1,0:T(8,128)(2,1)S(1)}, u32[]{:S(2)}, u32[]{:S(2)}) %collective-permute-start.13) | collective-permute-done | bytes 98336 | tf_op jit(solution)/shard_map/ppermute | solution.py:36
  46.7 1.7 %collective-permute-done.12 = bf16[96,512]{1,0:T(8,128)(2,1)S(1)} collective-permute-done((bf16[96,512]{1,0:T(8,128)(2,1)S(1)}, bf16[96,512]{1,0:T(8,128)(2,1)S(1)}, u32[]{:S(2)}, u32[]{:S(2)}) %collective-permute-start.12) | collective-permute-done | bytes 98336 | tf_op jit(solution)/shard_map/ppermute | solution.py:36
  48.6 5.4 %shard_map.123 = (bf16[128,256]{1,0:T(8,128)(2,1)S(1)}, bf16[128,256]{1,0:T(8,128)(2,1)S(1)}, bf16[128,256]{1,0:T(8,128)(2,1)S(1)}, bf16[128,256]{1,0:T(8,128)(2...) custom-call(bf16[2048,128]{1,0:T(8,128)(2,1)S(1)} %get-tuple-element.78.re, ...), custom_call_target="tpu_custom_call" | custom-call | flops 1 | bytes 1 | tf_op jit(solution)/shard_map/pallas_call | solution.py:65
  54.0 0.1 collective-permute-start.15
  54.1 0.5 collective-permute-start.16
  54.6 1.4 %collective-permute-done.15 = bf16[2,4,128,256]{3,2,1,0:T(8,128)(2,1)S(1)} collective-permute-done((bf16[2,4,128,256]{3,2,1,0:T(8,128)(2,1)S(1)}, bf16[2,4,128,256]{3,2,1,0:T(8,128)(2,1)S(1)}, u32[]{:S(2)}, u32[]{:S(2)}) %collective-permute-start.15) | collective-permute-done | bytes 524320 | tf_op jit(solution)/shard_map/ppermute | solution.py:36
  56.0 0.1 convert_add_fusion
  56.2 3.1 %collective-permute-start.20 = (f32[8,128]{1,0:T(8,128)S(1)}, f32[8,128]{1,0:T(8,128)S(1)}, u32[]{:S(2)}, u32[]{:S(2)}) collective-permute-start(f32[8,128]{1,0:T(8,128)S(1)} %shard_map.124), channel_id=1, source_target_pairs={{0,130},{1,131},{2,128},{3,129},{4,134},{5,135},{6,132},{7,133},{8... | collective-permute-start | bytes 12296 | tf_op jit(solution)/shard_map/ppermute | solution.py:42
  59.3 0.1 collective-permute-start.19
  59.4 1.5 %collective-permute-start.18 = (f32[8,128]{1,0:T(8,128)S(1)}, f32[8,128]{1,0:T(8,128)S(1)}, u32[]{:S(2)}, u32[]{:S(2)}) collective-permute-start(f32[8,128]{1,0:T(8,128)S(1)} %shard_map.124), channel_id=1, source_target_pairs={{0,2},{1,3},{2,0},{3,1},{4,6},{5,7},{6,4},{7,5},{8,10},{9,11},{10,... | collective-permute-start | bytes 12296 | tf_op jit(solution)/shard_map/ppermute | solution.py:42
  61.0 2.1 %collective-permute-start.17 = (bf16[4,128,256]{2,1,0:T(8,128)(2,1)S(1)}, bf16[4,128,256]{2,1,0:T(8,128)(2,1)S(1)}, u32[]{:S(2)}, u32[]{:S(2)}) collective-permute-start(bf16[4,128,256]{2,1,0:T(8,128)(2,1)S(1)} %fusion.8), channel_id=1, source_target_pairs={{0,2},{1,3},{2,0},{3,1},{4,6},{5,7},{6,4},{7,5},{8,10},{9,11},{10,... | collective-permute-start | bytes 786440 | tf_op jit(solution)/shard_map/ppermute | solution.py:36
  63.1 0.0 collective-permute-done.20
  63.1 0.0 collective-permute-done.19
  63.1 1.4 %collective-permute-done.18 = f32[8,128]{1,0:T(8,128)S(1)} collective-permute-done((f32[8,128]{1,0:T(8,128)S(1)}, f32[8,128]{1,0:T(8,128)S(1)}, u32[]{:S(2)}, u32[]{:S(2)}) %collective-permute-start.18) | collective-permute-done | bytes 4128 | tf_op jit(solution)/shard_map/ppermute | solution.py:42
  64.5 1.9 %collective-permute-start.22 = (f32[8,128]{1,0:T(8,128)S(1)}, f32[8,128]{1,0:T(8,128)S(1)}, u32[]{:S(2)}, u32[]{:S(2)}) collective-permute-start(f32[8,128]{1,0:T(8,128)S(1)} %add_add_fusion), channel_id=1, source_target_pairs={{112,0},{0,16},{16,32},{32,48},{48,64},{64,80},{80,96},{96,112},{2... | collective-permute-start | bytes 12296 | tf_op jit(solution)/shard_map/ppermute | solution.py:53
  66.4 0.1 collective-permute-start.21
  66.6 1.6 %collective-permute-done.22 = f32[8,128]{1,0:T(8,128)S(1)} collective-permute-done((f32[8,128]{1,0:T(8,128)S(1)}, f32[8,128]{1,0:T(8,128)S(1)}, u32[]{:S(2)}, u32[]{:S(2)}) %collective-permute-start.22) | collective-permute-done | bytes 4128 | tf_op jit(solution)/shard_map/ppermute | solution.py:53
  68.1 1.9 %collective-permute-done.21 = f32[8,128]{1,0:T(8,128)S(1)} collective-permute-done((f32[8,128]{1,0:T(8,128)S(1)}, f32[8,128]{1,0:T(8,128)S(1)}, u32[]{:S(2)}, u32[]{:S(2)}) %collective-permute-start.21) | collective-permute-done | bytes 4128 | tf_op jit(solution)/shard_map/ppermute | solution.py:53
  70.1 0.2 collective-permute-done.17.refs_1_
  70.2 0.2 shard_map.125
  70.5 0.1 collective-permute-start.23
  70.6 2.3 %collective-permute-start.24 = (bf16[144,512]{1,0:T(8,128)(2,1)S(1)}, bf16[144,512]{1,0:T(8,128)(2,1)S(1)}, u32[]{:S(2)}, u32[]{:S(2)}) collective-permute-start(bf16[144,512]{1,0:T(8,128)(2,1)S(1)} %get-tuple-element.102), channel_id=1, source_target_pairs={{0,8},{1,9},{2,10},{3,11},{4,12},{5,13},{6,14},{7,15},{8,0},{9,1},... | collective-permute-start | bytes 442376 | tf_op jit(solution)/shard_map/ppermute | solution.py:36
  72.9 1.5 %collective-permute-start.25 = (bf16[144,512]{1,0:T(8,128)(2,1)S(1)}, bf16[144,512]{1,0:T(8,128)(2,1)S(1)}, u32[]{:S(2)}, u32[]{:S(2)}) collective-permute-start(bf16[144,512]{1,0:T(8,128)(2,1)S(1)} %get-tuple-element.103), channel_id=1, source_target_pairs={{0,12},{1,13},{2,14},{3,15},{4,0},{5,1},{6,2},{7,3},{8,4},{9,5},{1... | collective-permute-start | bytes 442376 | tf_op jit(solution)/shard_map/ppermute | solution.py:36
  74.4 4.8 %collective-permute-done.23.refs_1_ = bf16[144,512]{1,0:T(8,128)(2,1)S(1)} collective-permute-done((bf16[144,512]{1,0:T(8,128)(2,1)S(1)}, bf16[144,512]{1,0:T(8,128)(2,1)S(1)}, u32[]{:S(2)}, u32[]{:S(2)}) %collective-permute-start.23) | collective-permute-done | bytes 147488 | tf_op jit(solution)/shard_map/ppermute | solution.py:36
  79.2 0.0 collective-permute-done.24.refs_2_
  79.2 0.6 collective-permute-done.25.refs_3_
  79.9 5.9 %collective-permute-start.27 = (f32[8,128]{1,0:T(8,128)S(1)}, f32[8,128]{1,0:T(8,128)S(1)}, u32[]{:S(2)}, u32[]{:S(2)}) collective-permute-start(f32[8,128]{1,0:T(8,128)S(1)} %shard_map.127.refs_0_), channel_id=1, source_target_pairs={{80,0},{96,16},{112,32},{0,48},{16,64},{32,80},{48,96},{64,112},{2... | collective-permute-start | bytes 12296 | tf_op jit(solution)/shard_map/ppermute | solution.py:53
  85.8 0.1 collective-permute-start.26
  85.9 0.9 shard_map.126
  86.8 0.6 collective-permute-done.27.refs_2_
  87.4 5.0 %collective-permute-done.26.refs_1_ = f32[8,128]{1,0:T(8,128)S(1)} collective-permute-done((f32[8,128]{1,0:T(8,128)S(1)}, f32[8,128]{1,0:T(8,128)S(1)}, u32[]{:S(2)}, u32[]{:S(2)}) %collective-permute-start.26) | collective-permute-done | bytes 4128 | tf_op jit(solution)/shard_map/ppermute | solution.py:53
  92.4 0.5 shard_map.128
  (28 shorter events, 0.3 us)
Async XLA Ops:
  6.4 10.6 %collective-permute-start.5 = (bf16[4,2,160,512]{3,2,1,0:T(8,128)(2,1)}, bf16[4,2,160,512]{3,2,1,0:T(8,128)(2,1)S(1)}, u32[]{:S(2)}, u32[]{:S(2)}) collective-permute-start(bf16[4,2,160,512]{3,2,1,0:T(8,128)(2,1)} %get-tuple-element.64), channel_id=1, source_target_pairs={{0,1},{1,0},{2,3},{3,2},{4,5},{5,4},{6,7},{7,6},{8,9},{9,8},{10,11... | collective-permute-start | bytes 3932168 | tf_op jit(solution)/shard_map/ppermute | solution.py:36
  6.5 6.2 %collective-permute-start.3 = (bf16[2,4,96,512]{3,2,1,0:T(8,128)(2,1)}, bf16[2,4,96,512]{3,2,1,0:T(8,128)(2,1)S(1)}, u32[]{:S(2)}, u32[]{:S(2)}) collective-permute-start(bf16[2,4,96,512]{3,2,1,0:T(8,128)(2,1)} %get-tuple-element.62), channel_id=1, source_target_pairs={{0,1},{1,0},{2,3},{3,2},{4,5},{5,4},{6,7},{7,6},{8,9},{9,8},{10,11... | collective-permute-start | bytes 2359304 | tf_op jit(solution)/shard_map/ppermute | solution.py:36
  7.0 12.6 %collective-permute-start = (bf16[128,512]{1,0:T(8,128)(2,1)}, bf16[128,512]{1,0:T(8,128)(2,1)S(1)}, u32[]{:S(2)}, u32[]{:S(2)}) collective-permute-start(bf16[128,512]{1,0:T(8,128)(2,1)} %get-tuple-element.58), channel_id=1, source_target_pairs={{0,4},{1,5},{2,6},{3,7},{4,8},{5,9},{6,10},{7,11},{8,12},{9,13},{1... | collective-permute-start | bytes 393224 | tf_op jit(solution)/shard_map/ppermute | solution.py:36
  8.4 12.8 %collective-permute-start.1 = (bf16[128,512]{1,0:T(8,128)(2,1)}, bf16[128,512]{1,0:T(8,128)(2,1)S(1)}, u32[]{:S(2)}, u32[]{:S(2)}) collective-permute-start(bf16[128,512]{1,0:T(8,128)(2,1)} %get-tuple-element.59), channel_id=1, source_target_pairs={{0,8},{1,9},{2,10},{3,11},{4,12},{5,13},{6,14},{7,15},{8,0},{9,1},... | collective-permute-start | bytes 393224 | tf_op jit(solution)/shard_map/ppermute | solution.py:36
  11.2 10.1 %collective-permute-start.2 = (bf16[128,512]{1,0:T(8,128)(2,1)}, bf16[128,512]{1,0:T(8,128)(2,1)S(1)}, u32[]{:S(2)}, u32[]{:S(2)}) collective-permute-start(bf16[128,512]{1,0:T(8,128)(2,1)} %get-tuple-element.60), channel_id=1, source_target_pairs={{0,12},{1,13},{2,14},{3,15},{4,0},{5,1},{6,2},{7,3},{8,4},{9,5},{1... | collective-permute-start | bytes 393224 | tf_op jit(solution)/shard_map/ppermute | solution.py:36
  13.7 17.5 %collective-permute-start.9 = (bf16[4,96,512]{2,1,0:T(8,128)(2,1)S(1)}, bf16[4,96,512]{2,1,0:T(8,128)(2,1)S(1)}, u32[]{:S(2)}, u32[]{:S(2)}) collective-permute-start(bf16[4,96,512]{2,1,0:T(8,128)(2,1)S(1)} %fusion.2.refs_4_), channel_id=1, source_target_pairs={{0,2},{1,3},{2,0},{3,1},{4,6},{5,7},{6,4},{7,5},{8,10},{9,11},{10,... | collective-permute-start | bytes 1179656 | tf_op jit(solution)/shard_map/ppermute | solution.py:36
  17.0 4.3 %copy-start = (bf16[128,512]{1,0:T(8,128)(2,1)S(1)}, bf16[128,512]{1,0:T(8,128)(2,1)}, u32[]{:S(2)}) copy-start(bf16[128,512]{1,0:T(8,128)(2,1)} %get-tuple-element.57.refs_0_.refs_2_.refs_9_) | copy-start | bytes 393220
  18.5 15.1 %collective-permute-start.8 = (bf16[2,160,512]{2,1,0:T(8,128)(2,1)S(1)}, bf16[2,160,512]{2,1,0:T(8,128)(2,1)S(1)}, u32[]{:S(2)}, u32[]{:S(2)}) collective-permute-start(bf16[2,160,512]{2,1,0:T(8,128)(2,1)S(1)} %get-tuple-element.111), channel_id=1, source_target_pairs={{0,12},{1,13},{2,14},{3,15},{4,0},{5,1},{6,2},{7,3},{8,4},{9,5},{1... | collective-permute-start | bytes 983048 | tf_op jit(solution)/shard_map/ppermute | solution.py:36
  19.5 14.0 %collective-permute-start.7 = (bf16[2,160,512]{2,1,0:T(8,128)(2,1)S(1)}, bf16[2,160,512]{2,1,0:T(8,128)(2,1)S(1)}, u32[]{:S(2)}, u32[]{:S(2)}) collective-permute-start(bf16[2,160,512]{2,1,0:T(8,128)(2,1)S(1)} %get-tuple-element.112), channel_id=1, source_target_pairs={{0,8},{1,9},{2,10},{3,11},{4,12},{5,13},{6,14},{7,15},{8,0},{9,1},... | collective-permute-start | bytes 983048 | tf_op jit(solution)/shard_map/ppermute | solution.py:36
  21.2 16.0 %collective-permute-start.6 = (bf16[2,160,512]{2,1,0:T(8,128)(2,1)S(1)}, bf16[2,160,512]{2,1,0:T(8,128)(2,1)S(1)}, u32[]{:S(2)}, u32[]{:S(2)}) collective-permute-start(bf16[2,160,512]{2,1,0:T(8,128)(2,1)S(1)} %get-tuple-element.113), channel_id=1, source_target_pairs={{0,4},{1,5},{2,6},{3,7},{4,8},{5,9},{6,10},{7,11},{8,12},{9,13},{1... | collective-permute-start | bytes 983048 | tf_op jit(solution)/shard_map/ppermute | solution.py:36
  21.3 17.8 %copy-start.4 = (bf16[2,4,96,512]{3,2,1,0:T(8,128)(2,1)S(1)}, bf16[2,4,96,512]{3,2,1,0:T(8,128)(2,1)}, u32[]{:S(2)}) copy-start(bf16[2,4,96,512]{3,2,1,0:T(8,128)(2,1)} %get-tuple-element.61) | copy-start | bytes 2359300
  21.3 9.9 %collective-permute-start.4 = (bf16[4,128,256]{2,1,0:T(8,128)(2,1)S(1)}, bf16[4,128,256]{2,1,0:T(8,128)(2,1)S(1)}, u32[]{:S(2)}, u32[]{:S(2)}) collective-permute-start(bf16[4,128,256]{2,1,0:T(8,128)(2,1)S(1)} %shard_map.120.refs_0_.refs_2_), channel_id=1, source_target_pairs={{0,2},{1,3},{2,0},{3,1},{4,6},{5,7},{6,4},{7,5},{8,10},{9,11},{10,... | collective-permute-start | bytes 786440 | tf_op jit(solution)/shard_map/ppermute | solution.py:36
  38.5 10.0 %collective-permute-start.11 = (bf16[160,512]{1,0:T(8,128)(2,1)S(1)}, bf16[160,512]{1,0:T(8,128)(2,1)S(1)}, u32[]{:S(2)}, u32[]{:S(2)}) collective-permute-start(bf16[160,512]{1,0:T(8,128)(2,1)S(1)} %fusion.12), channel_id=1, source_target_pairs={{0,2},{1,3},{2,0},{3,1},{4,6},{5,7},{6,4},{7,5},{8,10},{9,11},{10,... | collective-permute-start | bytes 491528 | tf_op jit(solution)/shard_map/ppermute | solution.py:36
  38.9 2.7 %copy-start.1 = (s32[1,2048]{1,0:T(1,128)S(1)}, s32[1,2048]{1,0:T(1,128)}, u32[]{:S(2)}) copy-start(s32[1,2048]{1,0:T(1,128)} %param.13) | copy-start | bytes 24580
  38.9 2.7 %copy-start.2 = (f32[128]{0:T(128)S(1)}, f32[128]{0:T(128)}, u32[]{:S(2)}) copy-start(f32[128]{0:T(128)} %param.11) | copy-start | bytes 1540
  38.9 2.7 %copy-start.3 = (f32[128]{0:T(128)S(1)}, f32[128]{0:T(128)}, u32[]{:S(2)}) copy-start(f32[128]{0:T(128)} %param.12) | copy-start | bytes 1540
  39.0 2.7 %collective-permute-start.10 = (bf16[2,4,128,256]{3,2,1,0:T(8,128)(2,1)S(1)}, bf16[2,4,128,256]{3,2,1,0:T(8,128)(2,1)S(1)}, u32[]{:S(2)}, u32[]{:S(2)}) collective-permute-start(bf16[2,4,128,256]{3,2,1,0:T(8,128)(2,1)S(1)} %shard_map.121.refs_0_), channel_id=1, source_target_pairs={{0,1},{1,0},{2,3},{3,2},{4,5},{5,4},{6,7},{7,6},{8,9},{9,8},{10,11... | collective-permute-start | bytes 1572872 | tf_op jit(solution)/shard_map/ppermute | solution.py:36
  39.3 6.4 %collective-permute-start.14 = (bf16[96,512]{1,0:T(8,128)(2,1)S(1)}, bf16[96,512]{1,0:T(8,128)(2,1)S(1)}, u32[]{:S(2)}, u32[]{:S(2)}) collective-permute-start(bf16[96,512]{1,0:T(8,128)(2,1)S(1)} %get-tuple-element.114), channel_id=1, source_target_pairs={{0,12},{1,13},{2,14},{3,15},{4,0},{5,1},{6,2},{7,3},{8,4},{9,5},{1... | collective-permute-start | bytes 294920 | tf_op jit(solution)/shard_map/ppermute | solution.py:36
  40.0 6.8 %collective-permute-start.13 = (bf16[96,512]{1,0:T(8,128)(2,1)S(1)}, bf16[96,512]{1,0:T(8,128)(2,1)S(1)}, u32[]{:S(2)}, u32[]{:S(2)}) collective-permute-start(bf16[96,512]{1,0:T(8,128)(2,1)S(1)} %get-tuple-element.115), channel_id=1, source_target_pairs={{0,8},{1,9},{2,10},{3,11},{4,12},{5,13},{6,14},{7,15},{8,0},{9,1},... | collective-permute-start | bytes 294920 | tf_op jit(solution)/shard_map/ppermute | solution.py:36
  40.8 7.7 %collective-permute-start.12 = (bf16[96,512]{1,0:T(8,128)(2,1)S(1)}, bf16[96,512]{1,0:T(8,128)(2,1)S(1)}, u32[]{:S(2)}, u32[]{:S(2)}) collective-permute-start(bf16[96,512]{1,0:T(8,128)(2,1)S(1)} %get-tuple-element.116), channel_id=1, source_target_pairs={{0,4},{1,5},{2,6},{3,7},{4,8},{5,9},{6,10},{7,11},{8,12},{9,13},{1... | collective-permute-start | bytes 294920 | tf_op jit(solution)/shard_map/ppermute | solution.py:36
  54.0 2.0 %collective-permute-start.15 = (bf16[2,4,128,256]{3,2,1,0:T(8,128)(2,1)S(1)}, bf16[2,4,128,256]{3,2,1,0:T(8,128)(2,1)S(1)}, u32[]{:S(2)}, u32[]{:S(2)}) collective-permute-start(bf16[2,4,128,256]{3,2,1,0:T(8,128)(2,1)S(1)} %get-tuple-element.91), channel_id=1, source_target_pairs={{0,1},{1,0},{2,3},{3,2},{4,5},{5,4},{6,7},{7,6},{8,9},{9,8},{10,11... | collective-permute-start | bytes 1572872 | tf_op jit(solution)/shard_map/ppermute | solution.py:36
  54.1 2.0 %collective-permute-start.16 = (f32[8,128]{1,0:T(8,128)S(1)}, f32[8,128]{1,0:T(8,128)S(1)}, u32[]{:S(2)}, u32[]{:S(2)}) collective-permute-start(f32[8,128]{1,0:T(8,128)S(1)} %get-tuple-element.94.refs_0_), channel_id=1, source_target_pairs={{0,1},{1,0},{2,3},{3,2},{4,5},{5,4},{6,7},{7,6},{8,9},{9,8},{10,11... | collective-permute-start | bytes 12296 | tf_op jit(solution)/shard_map/ppermute | solution.py:36
  56.2 6.9 %collective-permute-start.20 = (f32[8,128]{1,0:T(8,128)S(1)}, f32[8,128]{1,0:T(8,128)S(1)}, u32[]{:S(2)}, u32[]{:S(2)}) collective-permute-start(f32[8,128]{1,0:T(8,128)S(1)} %shard_map.124), channel_id=1, source_target_pairs={{0,130},{1,131},{2,128},{3,129},{4,134},{5,135},{6,132},{7,133},{8... | collective-permute-start | bytes 12296 | tf_op jit(solution)/shard_map/ppermute | solution.py:42
  59.3 3.8 %collective-permute-start.19 = (f32[8,128]{1,0:T(8,128)S(1)}, f32[8,128]{1,0:T(8,128)S(1)}, u32[]{:S(2)}, u32[]{:S(2)}) collective-permute-start(f32[8,128]{1,0:T(8,128)S(1)} %shard_map.124), channel_id=1, source_target_pairs={{0,128},{1,129},{2,130},{3,131},{4,132},{5,133},{6,134},{7,135},{8... | collective-permute-start | bytes 12296 | tf_op jit(solution)/shard_map/ppermute | solution.py:42
  59.4 5.1 %collective-permute-start.18 = (f32[8,128]{1,0:T(8,128)S(1)}, f32[8,128]{1,0:T(8,128)S(1)}, u32[]{:S(2)}, u32[]{:S(2)}) collective-permute-start(f32[8,128]{1,0:T(8,128)S(1)} %shard_map.124), channel_id=1, source_target_pairs={{0,2},{1,3},{2,0},{3,1},{4,6},{5,7},{6,4},{7,5},{8,10},{9,11},{10,... | collective-permute-start | bytes 12296 | tf_op jit(solution)/shard_map/ppermute | solution.py:42
  61.0 9.3 %collective-permute-start.17 = (bf16[4,128,256]{2,1,0:T(8,128)(2,1)S(1)}, bf16[4,128,256]{2,1,0:T(8,128)(2,1)S(1)}, u32[]{:S(2)}, u32[]{:S(2)}) collective-permute-start(bf16[4,128,256]{2,1,0:T(8,128)(2,1)S(1)} %fusion.8), channel_id=1, source_target_pairs={{0,2},{1,3},{2,0},{3,1},{4,6},{5,7},{6,4},{7,5},{8,10},{9,11},{10,... | collective-permute-start | bytes 786440 | tf_op jit(solution)/shard_map/ppermute | solution.py:36
  64.5 3.6 %collective-permute-start.22 = (f32[8,128]{1,0:T(8,128)S(1)}, f32[8,128]{1,0:T(8,128)S(1)}, u32[]{:S(2)}, u32[]{:S(2)}) collective-permute-start(f32[8,128]{1,0:T(8,128)S(1)} %add_add_fusion), channel_id=1, source_target_pairs={{112,0},{0,16},{16,32},{32,48},{48,64},{64,80},{80,96},{96,112},{2... | collective-permute-start | bytes 12296 | tf_op jit(solution)/shard_map/ppermute | solution.py:53
  66.4 3.6 %collective-permute-start.21 = (f32[8,128]{1,0:T(8,128)S(1)}, f32[8,128]{1,0:T(8,128)S(1)}, u32[]{:S(2)}, u32[]{:S(2)}) collective-permute-start(f32[8,128]{1,0:T(8,128)S(1)} %add_add_fusion), channel_id=1, source_target_pairs={{16,0},{32,16},{48,32},{64,48},{80,64},{96,80},{112,96},{0,112},{1... | collective-permute-start | bytes 12296 | tf_op jit(solution)/shard_map/ppermute | solution.py:53
  70.5 8.7 %collective-permute-start.23 = (bf16[144,512]{1,0:T(8,128)(2,1)S(1)}, bf16[144,512]{1,0:T(8,128)(2,1)S(1)}, u32[]{:S(2)}, u32[]{:S(2)}) collective-permute-start(bf16[144,512]{1,0:T(8,128)(2,1)S(1)} %get-tuple-element.101), channel_id=1, source_target_pairs={{0,4},{1,5},{2,6},{3,7},{4,8},{5,9},{6,10},{7,11},{8,12},{9,13},{1... | collective-permute-start | bytes 442376 | tf_op jit(solution)/shard_map/ppermute | solution.py:36
  70.6 8.6 %collective-permute-start.24 = (bf16[144,512]{1,0:T(8,128)(2,1)S(1)}, bf16[144,512]{1,0:T(8,128)(2,1)S(1)}, u32[]{:S(2)}, u32[]{:S(2)}) collective-permute-start(bf16[144,512]{1,0:T(8,128)(2,1)S(1)} %get-tuple-element.102), channel_id=1, source_target_pairs={{0,8},{1,9},{2,10},{3,11},{4,12},{5,13},{6,14},{7,15},{8,0},{9,1},... | collective-permute-start | bytes 442376 | tf_op jit(solution)/shard_map/ppermute | solution.py:36
  72.9 7.0 %collective-permute-start.25 = (bf16[144,512]{1,0:T(8,128)(2,1)S(1)}, bf16[144,512]{1,0:T(8,128)(2,1)S(1)}, u32[]{:S(2)}, u32[]{:S(2)}) collective-permute-start(bf16[144,512]{1,0:T(8,128)(2,1)S(1)} %get-tuple-element.103), channel_id=1, source_target_pairs={{0,12},{1,13},{2,14},{3,15},{4,0},{5,1},{6,2},{7,3},{8,4},{9,5},{1... | collective-permute-start | bytes 442376 | tf_op jit(solution)/shard_map/ppermute | solution.py:36
  79.9 7.5 %collective-permute-start.27 = (f32[8,128]{1,0:T(8,128)S(1)}, f32[8,128]{1,0:T(8,128)S(1)}, u32[]{:S(2)}, u32[]{:S(2)}) collective-permute-start(f32[8,128]{1,0:T(8,128)S(1)} %shard_map.127.refs_0_), channel_id=1, source_target_pairs={{80,0},{96,16},{112,32},{0,48},{16,64},{32,80},{48,96},{64,112},{2... | collective-permute-start | bytes 12296 | tf_op jit(solution)/shard_map/ppermute | solution.py:53
  85.8 6.6 %collective-permute-start.26 = (f32[8,128]{1,0:T(8,128)S(1)}, f32[8,128]{1,0:T(8,128)S(1)}, u32[]{:S(2)}, u32[]{:S(2)}) collective-permute-start(f32[8,128]{1,0:T(8,128)S(1)} %shard_map.127.refs_0_), channel_id=1, source_target_pairs={{48,0},{64,16},{80,32},{96,48},{112,64},{0,80},{16,96},{32,112},{1... | collective-permute-start | bytes 12296 | tf_op jit(solution)/shard_map/ppermute | solution.py:53

commit v3 on v2

--- a/solution.py
+++ b/solution.py
@@ -12,7 +12,7 @@
 EPS = 1e-06
 NEG = -1e30
 HEAD = 128
-ROWS_A = 160
+ROWS_A = 144
 ROWS_B = 256 - ROWS_A
 BLK = 128
 NX = 4
@@ -115,11 +115,11 @@
             blocks = [4 * i + 2 * ((y + dy) % 2) + (c + core) % 2 for i in range(4)]
             columns = [held[:, pl.ds(pl.multiple_of(block * BLK, BLK), BLK)] for block in blocks]
             columns = jnp.concatenate(columns, axis=1)
-            for dx in range(NX):
-                rows = pl.ds(pl.multiple_of(((x + dx) % NX) * 256, 256), 256)
-                part = jnp.dot(turned[rows, :], columns, preferred_element_type=F32).astype(BF16)
-                a_held[core, dx, dy] = part[:ROWS_A]
-                b_held[core, dy, dx] = part[ROWS_A:]
+            part = jnp.dot(turned[...], columns, preferred_element_type=F32).astype(BF16)
+            for j in range(NX):
+                dx = (j + NX - x) % NX
+                a_held[core, dx, dy] = part[256 * j : 256 * j + ROWS_A]
+                b_held[core, dy, dx] = part[256 * j + ROWS_A : 256 * (j + 1)]
             for n, (held_ref, out) in enumerate(
                 ((a_held.at[core, :, dy], a_out.at[:, dy]), (b_held.at[core, dy], b_out.at[dy]))
             ):
@@ -184,25 +184,25 @@
         start = spans[i : i + 1, :]
         place = spans[4 + i : 5 + i, :]
         top = jnp.full((1, 256), NEG, F32)
-        for j in range(2 * (i + 1)):
-            rows = slice(256 * j, 256 * (j + 1))
+        for j in range(i + 1):
+            rows = slice(512 * j, 512 * (j + 1))
             s = lax.dot_general(k_hat[rows, :], q_hat[i], NT, preferred_element_type=F32) * factor
-            at_key = lax.broadcasted_iota(jnp.int32, (256, 256), 0) + 256 * j
+            at_key = lax.broadcasted_iota(jnp.int32, (512, 256), 0) + 512 * j
             allowed = at_key >= start
-            if j >= 2 * i:
+            if j == i:
                 allowed = allowed & (at_key <= place)
             s = jnp.where(allowed, s, NEG)
             s_ref[rows, :] = s
             top = jnp.maximum(top, jnp.max(s, axis=0, keepdims=True))
         total = jnp.zeros((1, 256), F32)
-        for j in range(2 * (i + 1)):
-            rows = slice(256 * j, 256 * (j + 1))
+        for j in range(i + 1):
+            rows = slice(512 * j, 512 * (j + 1))
             total += jnp.sum(jnp.exp(s_ref[rows, :] - top), axis=0, keepdims=True)
         log_row = top + jnp.log(total)
         log_total[i : i + 1, :] = log_row
         result = jnp.zeros((128, 256), F32)
-        for j in range(2 * (i + 1)):
-            rows = slice(256 * j, 256 * (j + 1))
+        for j in range(i + 1):
+            rows = slice(512 * j, 512 * (j + 1))
             probs_low = jnp.exp(s_ref[rows, :] - log_row).astype(BF16)
             result += jnp.dot(v_turned[:, rows], probs_low, preferred_element_type=F32)
         outputs[i] = result
@@ -233,12 +233,12 @@
         d_out_rows = d_out.T
         query = q_hat[i]
         d_query = jnp.zeros((128, 256), F32)
-        for j in range(2 * (i + 1)):
-            rows = slice(256 * j, 256 * (j + 1))
+        for j in range(i + 1):
+            rows = slice(512 * j, 512 * (j + 1))
             s = lax.dot_general(k_hat[rows, :], query, NT, preferred_element_type=F32) * factor
-            at_key = lax.broadcasted_iota(jnp.int32, (256, 256), 0) + 256 * j
+            at_key = lax.broadcasted_iota(jnp.int32, (512, 256), 0) + 512 * j
             allowed = at_key >= start
-            if j >= 2 * i:
+            if j == i:
                 allowed = allowed & (at_key <= place)
             probs = jnp.exp(jnp.where(allowed, s, NEG) - log_row)
             d_probs = jnp.dot(v_all[rows, :], d_out, preferred_element_type=F32)

time: 93.1 us -> 90.8 us (0.975)
  other arithmetic: 4.16 us -> 2.01 us
  Pallas kernels: 16.9 us -> 15.6 us
    pallas_call x10, Pallas kernels: 16.9 us -> 15.6 us  [call(): pl.pallas_call(body, out_shape=outs, in_specs=[hbm if hbm_in else vmem] *...]
    convert_element_type x1, other arithmetic: 1.49 us -> 0.27 us  [on_device(): (a_own[dx].astype(F32) + a_swapped[dx].astype(F32)).astype(BF16)]
    add x1, other arithmetic: 1.17 us -> 0.18 us  [on_device(): sum_a = sum((part.astype(F32) for part in from_x), parts_a[0].astype(F32))]
  transfers between devices with their start and end apart: 28 -> 28, of which waited for: 14 -> 13; matrix products, arithmetic and copies ran while one was open for 3% -> 2% of each run, Pallas kernels for 5% -> 6%
where the time goes in v3:
time: 90.8 us; the launch traced here: 90.6 us
  waiting for transfers between devices  36.4 us (40%)
  starting transfers between devices  35.6 us (39%)
  Pallas kernels  15.6 us (17%)
  other arithmetic  2.01 us (2%)
  between operations  0.91 us (1%)
    ppermute x21, waiting for transfers between devices, shift(): return lax.ppermute(value, 'seq', pairs)  25.8 us
    ppermute x21, starting transfers between devices, shift(): return lax.ppermute(value, 'seq', pairs)  22.8 us
    pallas_call x10, Pallas kernels, call(): pl.pallas_call(body, out_shape=outs, in_specs=[hbm if hbm_in else vmem] *...  15.6 us
    ppermute x4, waiting for transfers between devices, along_z(): return lax.ppermute(value, 'dp', pairs)  9.13 us
    ppermute x4, starting transfers between devices, along_z(): return lax.ppermute(value, 'dp', pairs)  8 us
    ppermute x3, starting transfers between devices, flip(): return lax.ppermute(value, ('dp', 'seq'), pairs)  4.79 us
  transfers between devices with their start and end apart: 28, of which 13 were waited for; matrix products, arithmetic and copies ran while one was open for 2% of the time, Pallas kernels for 6%

profile of v3, /device:TPU:32, one launch (start us, length us, event | category | flops | bytes accessed | tf_op | source)
XLA Modules:
  0.0 90.6 jit_solution(15617313581313972750)
XLA Ops:
  0.6 5.6 %shard_map.119 = (bf16[4,2,144,512]{3,2,1,0:T(8,128)(2,1)}, bf16[2,4,112,512]{3,2,1,0:T(8,128)(2,1)}, bf16[4,2,144,512]{3,2,1,0:T(8,128)(2,1)}, bf16[2,4,112,512...) custom-call(bf16[448,1024]{1,0:T(8,128)(2,1)} %refs_0_.1, ...), custom_call_target="tpu_custom_call" | custom-call | flops 6000000000 | bytes 1 | tf_op jit(solution)/shard_map/pallas_call | solution.py:65
  6.2 0.1 collective-permute-start.5
  6.3 0.5 collective-permute-start.3
  6.8 1.5 %collective-permute-start = (bf16[128,512]{1,0:T(8,128)(2,1)}, bf16[128,512]{1,0:T(8,128)(2,1)S(1)}, u32[]{:S(2)}, u32[]{:S(2)}) collective-permute-start(bf16[128,512]{1,0:T(8,128)(2,1)} %get-tuple-element.58), channel_id=1, source_target_pairs={{0,4},{1,5},{2,6},{3,7},{4,8},{5,9},{6,10},{7,11},{8,12},{9,13},{1... | collective-permute-start | bytes 393224 | tf_op jit(solution)/shard_map/ppermute | solution.py:36
  8.3 2.7 %collective-permute-start.1 = (bf16[128,512]{1,0:T(8,128)(2,1)}, bf16[128,512]{1,0:T(8,128)(2,1)S(1)}, u32[]{:S(2)}, u32[]{:S(2)}) collective-permute-start(bf16[128,512]{1,0:T(8,128)(2,1)} %get-tuple-element.59), channel_id=1, source_target_pairs={{0,8},{1,9},{2,10},{3,11},{4,12},{5,13},{6,14},{7,15},{8,0},{9,1},... | collective-permute-start | bytes 393224 | tf_op jit(solution)/shard_map/ppermute | solution.py:36
  11.1 1.4 %collective-permute-start.2 = (bf16[128,512]{1,0:T(8,128)(2,1)}, bf16[128,512]{1,0:T(8,128)(2,1)S(1)}, u32[]{:S(2)}, u32[]{:S(2)}) collective-permute-start(bf16[128,512]{1,0:T(8,128)(2,1)} %get-tuple-element.60), channel_id=1, source_target_pairs={{0,12},{1,13},{2,14},{3,15},{4,0},{5,1},{6,2},{7,3},{8,4},{9,5},{1... | collective-permute-start | bytes 393224 | tf_op jit(solution)/shard_map/ppermute | solution.py:36
  12.5 0.0 collective-permute-done.3
  12.5 1.1 %fusion.2.refs_4_ = bf16[4,112,512]{2,1,0:T(8,128)(2,1)S(1)} fusion(bf16[2,4,112,512]{3,2,1,0:T(8,128)(2,1)S(1)} %collective-permute-done.3, bf16[2,4,112,512]{3,2,1,0:T(8,128)(2,1)} %get-tuple-element.61), kind=kLoop, calls=%fused_computation.12 | loop fusion | flops 917504 | bytes 1376256 | tf_op jit(solution)/shard_map/convert_element_type | solution.py:350
  13.6 3.3 %collective-permute-start.9 = (bf16[4,112,512]{2,1,0:T(8,128)(2,1)S(1)}, bf16[4,112,512]{2,1,0:T(8,128)(2,1)S(1)}, u32[]{:S(2)}, u32[]{:S(2)}) collective-permute-start(bf16[4,112,512]{2,1,0:T(8,128)(2,1)S(1)} %fusion.2.refs_4_), channel_id=1, source_target_pairs={{0,2},{1,3},{2,0},{3,1},{4,6},{5,7},{6,4},{7,5},{8,10},{9,11},{10,... | collective-permute-start | bytes 1376264 | tf_op jit(solution)/shard_map/ppermute | solution.py:36
  16.9 0.0 collective-permute-done.5
  16.9 0.3 fusion.5
  17.2 1.1 %collective-permute-start.8 = (bf16[2,144,512]{2,1,0:T(8,128)(2,1)S(1)}, bf16[2,144,512]{2,1,0:T(8,128)(2,1)S(1)}, u32[]{:S(2)}, u32[]{:S(2)}) collective-permute-start(bf16[2,144,512]{2,1,0:T(8,128)(2,1)S(1)} %get-tuple-element.111), channel_id=1, source_target_pairs={{0,12},{1,13},{2,14},{3,15},{4,0},{5,1},{6,2},{7,3},{8,4},{9,5},{1... | collective-permute-start | bytes 884744 | tf_op jit(solution)/shard_map/ppermute | solution.py:36
  18.3 0.0 collective-permute-done.refs_1_.refs_3_.refs_10_
  18.3 1.7 %collective-permute-start.7 = (bf16[2,144,512]{2,1,0:T(8,128)(2,1)S(1)}, bf16[2,144,512]{2,1,0:T(8,128)(2,1)S(1)}, u32[]{:S(2)}, u32[]{:S(2)}) collective-permute-start(bf16[2,144,512]{2,1,0:T(8,128)(2,1)S(1)} %get-tuple-element.112), channel_id=1, source_target_pairs={{0,8},{1,9},{2,10},{3,11},{4,12},{5,13},{6,14},{7,15},{8,0},{9,1},... | collective-permute-start | bytes 884744 | tf_op jit(solution)/shard_map/ppermute | solution.py:36
  20.0 0.0 collective-permute-done.1.refs_2_.refs_4_.refs_11_
  20.0 0.0 collective-permute-start.6
  20.0 0.0 collective-permute-done.2.refs_3_.refs_5_.refs_12_
  20.0 1.4 %collective-permute-start.4 = (bf16[4,128,256]{2,1,0:T(8,128)(2,1)S(1)}, bf16[4,128,256]{2,1,0:T(8,128)(2,1)S(1)}, u32[]{:S(2)}, u32[]{:S(2)}) collective-permute-start(bf16[4,128,256]{2,1,0:T(8,128)(2,1)S(1)} %shard_map.120.refs_0_.refs_2_), channel_id=1, source_target_pairs={{0,2},{1,3},{2,0},{3,1},{4,6},{5,7},{6,4},{7,5},{8,10},{9,11},{10,... | collective-permute-start | bytes 786440 | tf_op jit(solution)/shard_map/ppermute | solution.py:36
  21.4 11.2 %collective-permute-done.4.refs_1_ = bf16[4,128,256]{2,1,0:T(8,128)(2,1)S(1)} collective-permute-done((bf16[4,128,256]{2,1,0:T(8,128)(2,1)S(1)}, bf16[4,128,256]{2,1,0:T(8,128)(2,1)S(1)}, u32[]{:S(2)}, u32[]{:S(2)}) %collective-permute-start.4) | collective-permute-done | bytes 262176 | tf_op jit(solution)/shard_map/ppermute | solution.py:36
  32.5 0.0 collective-permute-done.9
  32.5 0.0 collective-permute-done.8
  32.5 0.0 collective-permute-done.7
  32.6 2.0 %collective-permute-done.6 = bf16[2,144,512]{2,1,0:T(8,128)(2,1)S(1)} collective-permute-done((bf16[2,144,512]{2,1,0:T(8,128)(2,1)S(1)}, bf16[2,144,512]{2,1,0:T(8,128)(2,1)S(1)}, u32[]{:S(2)}, u32[]{:S(2)}) %collective-permute-start.6) | collective-permute-done | bytes 294944 | tf_op jit(solution)/shard_map/ppermute | solution.py:36
  34.6 0.2 fusion.1
  34.8 1.2 %collective-permute-start.11 = (bf16[144,512]{1,0:T(8,128)(2,1)S(1)}, bf16[144,512]{1,0:T(8,128)(2,1)S(1)}, u32[]{:S(2)}, u32[]{:S(2)}) collective-permute-start(bf16[144,512]{1,0:T(8,128)(2,1)S(1)} %fusion.12), channel_id=1, source_target_pairs={{0,2},{1,3},{2,0},{3,1},{4,6},{5,7},{6,4},{7,5},{8,10},{9,11},{10,... | collective-permute-start | bytes 442376 | tf_op jit(solution)/shard_map/ppermute | solution.py:36
  36.1 0.0 copy-start.1
  36.1 0.0 copy-start.2
  36.1 0.0 copy-start.3
  36.1 0.1 collective-permute-start.10
  36.3 0.2 fusion.13
  36.5 1.9 %collective-permute-start.14 = (bf16[112,512]{1,0:T(8,128)(2,1)S(1)}, bf16[112,512]{1,0:T(8,128)(2,1)S(1)}, u32[]{:S(2)}, u32[]{:S(2)}) collective-permute-start(bf16[112,512]{1,0:T(8,128)(2,1)S(1)} %get-tuple-element.114), channel_id=1, source_target_pairs={{0,12},{1,13},{2,14},{3,15},{4,0},{5,1},{6,2},{7,3},{8,4},{9,5},{1... | collective-permute-start | bytes 344072 | tf_op jit(solution)/shard_map/ppermute | solution.py:36
  38.4 0.8 collective-permute-start.13
  39.3 0.8 collective-permute-start.12
  40.1 4.1 %shard_map.122 = (bf16[2048,128]{1,0:T(8,128)(2,1)S(1)}, bf16[128,2048]{1,0:T(8,128)(2,1)S(1)}, bf16[2048,128]{1,0:T(8,128)(2,1)S(1)}, f32[2048,128]{1,0:T(8,128...) custom-call(bf16[2,4,128,256]{3,2,1,0:T(8,128)(2,1)S(1)} %shard_map., ...), custom_call_target="tpu_custom_call" | custom-call | flops 1 | bytes 1 | tf_op jit(solution)/shard_map/pallas_call | solution.py:65
  44.2 1.7 %collective-permute-done.13 = bf16[112,512]{1,0:T(8,128)(2,1)S(1)} collective-permute-done((bf16[112,512]{1,0:T(8,128)(2,1)S(1)}, bf16[112,512]{1,0:T(8,128)(2,1)S(1)}, u32[]{:S(2)}, u32[]{:S(2)}) %collective-permute-start.13) | collective-permute-done | bytes 114720 | tf_op jit(solution)/shard_map/ppermute | solution.py:36
  45.9 1.7 %collective-permute-done.12 = bf16[112,512]{1,0:T(8,128)(2,1)S(1)} collective-permute-done((bf16[112,512]{1,0:T(8,128)(2,1)S(1)}, bf16[112,512]{1,0:T(8,128)(2,1)S(1)}, u32[]{:S(2)}, u32[]{:S(2)}) %collective-permute-start.12) | collective-permute-done | bytes 114720 | tf_op jit(solution)/shard_map/ppermute | solution.py:36
  47.7 0.1 fusion.11.refs_8_
  47.8 4.2 %shard_map.123 = (bf16[128,256]{1,0:T(8,128)(2,1)S(1)}, bf16[128,256]{1,0:T(8,128)(2,1)S(1)}, bf16[128,256]{1,0:T(8,128)(2,1)S(1)}, bf16[128,256]{1,0:T(8,128)(2...) custom-call(bf16[2048,128]{1,0:T(8,128)(2,1)S(1)} %get-tuple-element.78.re, ...), custom_call_target="tpu_custom_call" | custom-call | flops 1 | bytes 1 | tf_op jit(solution)/shard_map/pallas_call | solution.py:65
  51.9 0.1 collective-permute-start.15
  52.0 0.5 collective-permute-start.16
  52.5 1.4 %collective-permute-done.15 = bf16[2,4,128,256]{3,2,1,0:T(8,128)(2,1)S(1)} collective-permute-done((bf16[2,4,128,256]{3,2,1,0:T(8,128)(2,1)S(1)}, bf16[2,4,128,256]{3,2,1,0:T(8,128)(2,1)S(1)}, u32[]{:S(2)}, u32[]{:S(2)}) %collective-permute-start.15) | collective-permute-done | bytes 524320 | tf_op jit(solution)/shard_map/ppermute | solution.py:36
  53.9 0.1 convert_add_fusion
  54.1 1.1 %collective-permute-start.20 = (f32[8,128]{1,0:T(8,128)S(1)}, f32[8,128]{1,0:T(8,128)S(1)}, u32[]{:S(2)}, u32[]{:S(2)}) collective-permute-start(f32[8,128]{1,0:T(8,128)S(1)} %shard_map.124), channel_id=1, source_target_pairs={{0,130},{1,131},{2,128},{3,129},{4,134},{5,135},{6,132},{7,133},{8... | collective-permute-start | bytes 12296 | tf_op jit(solution)/shard_map/ppermute | solution.py:42
  55.2 0.0 collective-permute-start.19
  55.3 3.6 %collective-permute-start.18 = (f32[8,128]{1,0:T(8,128)S(1)}, f32[8,128]{1,0:T(8,128)S(1)}, u32[]{:S(2)}, u32[]{:S(2)}) collective-permute-start(f32[8,128]{1,0:T(8,128)S(1)} %shard_map.124), channel_id=1, source_target_pairs={{0,2},{1,3},{2,0},{3,1},{4,6},{5,7},{6,4},{7,5},{8,10},{9,11},{10,... | collective-permute-start | bytes 12296 | tf_op jit(solution)/shard_map/ppermute | solution.py:42
  58.9 0.1 collective-permute-start.17
  59.1 1.5 %collective-permute-done.18 = f32[8,128]{1,0:T(8,128)S(1)} collective-permute-done((f32[8,128]{1,0:T(8,128)S(1)}, f32[8,128]{1,0:T(8,128)S(1)}, u32[]{:S(2)}, u32[]{:S(2)}) %collective-permute-start.18) | collective-permute-done | bytes 4128 | tf_op jit(solution)/shard_map/ppermute | solution.py:42
  60.5 1.9 %collective-permute-start.22 = (f32[8,128]{1,0:T(8,128)S(1)}, f32[8,128]{1,0:T(8,128)S(1)}, u32[]{:S(2)}, u32[]{:S(2)}) collective-permute-start(f32[8,128]{1,0:T(8,128)S(1)} %add_add_fusion), channel_id=1, source_target_pairs={{112,0},{0,16},{16,32},{32,48},{48,64},{64,80},{80,96},{96,112},{2... | collective-permute-start | bytes 12296 | tf_op jit(solution)/shard_map/ppermute | solution.py:53
  62.4 0.1 collective-permute-start.21
  62.6 1.6 %collective-permute-done.22 = f32[8,128]{1,0:T(8,128)S(1)} collective-permute-done((f32[8,128]{1,0:T(8,128)S(1)}, f32[8,128]{1,0:T(8,128)S(1)}, u32[]{:S(2)}, u32[]{:S(2)}) %collective-permute-start.22) | collective-permute-done | bytes 4128 | tf_op jit(solution)/shard_map/ppermute | solution.py:53
  64.1 1.9 %collective-permute-done.21 = f32[8,128]{1,0:T(8,128)S(1)} collective-permute-done((f32[8,128]{1,0:T(8,128)S(1)}, f32[8,128]{1,0:T(8,128)S(1)}, u32[]{:S(2)}, u32[]{:S(2)}) %collective-permute-start.21) | collective-permute-done | bytes 4128 | tf_op jit(solution)/shard_map/ppermute | solution.py:53
  66.0 2.0 %collective-permute-done.17.refs_1_ = bf16[4,128,256]{2,1,0:T(8,128)(2,1)S(1)} collective-permute-done((bf16[4,128,256]{2,1,0:T(8,128)(2,1)S(1)}, bf16[4,128,256]{2,1,0:T(8,128)(2,1)S(1)}, u32[]{:S(2)}, u32[]{:S(2)}) %collective-permute-start.17) | collective-permute-done | bytes 262176 | tf_op jit(solution)/shard_map/ppermute | solution.py:36
  68.0 0.2 shard_map.125
  68.3 0.1 collective-permute-start.23
  68.4 2.0 %collective-permute-start.24 = (bf16[144,512]{1,0:T(8,128)(2,1)S(1)}, bf16[144,512]{1,0:T(8,128)(2,1)S(1)}, u32[]{:S(2)}, u32[]{:S(2)}) collective-permute-start(bf16[144,512]{1,0:T(8,128)(2,1)S(1)} %get-tuple-element.102), channel_id=1, source_target_pairs={{0,8},{1,9},{2,10},{3,11},{4,12},{5,13},{6,14},{7,15},{8,0},{9,1},... | collective-permute-start | bytes 442376 | tf_op jit(solution)/shard_map/ppermute | solution.py:36
  70.4 1.4 %collective-permute-start.25 = (bf16[144,512]{1,0:T(8,128)(2,1)S(1)}, bf16[144,512]{1,0:T(8,128)(2,1)S(1)}, u32[]{:S(2)}, u32[]{:S(2)}) collective-permute-start(bf16[144,512]{1,0:T(8,128)(2,1)S(1)} %get-tuple-element.103), channel_id=1, source_target_pairs={{0,12},{1,13},{2,14},{3,15},{4,0},{5,1},{6,2},{7,3},{8,4},{9,5},{1... | collective-permute-start | bytes 442376 | tf_op jit(solution)/shard_map/ppermute | solution.py:36
  71.8 5.0 %collective-permute-done.23.refs_1_ = bf16[144,512]{1,0:T(8,128)(2,1)S(1)} collective-permute-done((bf16[144,512]{1,0:T(8,128)(2,1)S(1)}, bf16[144,512]{1,0:T(8,128)(2,1)S(1)}, u32[]{:S(2)}, u32[]{:S(2)}) %collective-permute-start.23) | collective-permute-done | bytes 147488 | tf_op jit(solution)/shard_map/ppermute | solution.py:36
  76.9 0.7 collective-permute-done.25.refs_3_
  77.5 5.9 %collective-permute-start.27 = (f32[8,128]{1,0:T(8,128)S(1)}, f32[8,128]{1,0:T(8,128)S(1)}, u32[]{:S(2)}, u32[]{:S(2)}) collective-permute-start(f32[8,128]{1,0:T(8,128)S(1)} %shard_map.127.refs_0_), channel_id=1, source_target_pairs={{80,0},{96,16},{112,32},{0,48},{16,64},{32,80},{48,96},{64,112},{2... | collective-permute-start | bytes 12296 | tf_op jit(solution)/shard_map/ppermute | solution.py:53
  83.5 0.1 collective-permute-start.26
  83.5 0.9 shard_map.126
  84.4 0.6 collective-permute-done.27.refs_2_
  85.0 5.1 %collective-permute-done.26.refs_1_ = f32[8,128]{1,0:T(8,128)S(1)} collective-permute-done((f32[8,128]{1,0:T(8,128)S(1)}, f32[8,128]{1,0:T(8,128)S(1)}, u32[]{:S(2)}, u32[]{:S(2)}) %collective-permute-start.26) | collective-permute-done | bytes 4128 | tf_op jit(solution)/shard_map/ppermute | solution.py:53
  90.1 0.5 shard_map.128
  (30 shorter events, 0.3 us)
Async XLA Ops:
  6.2 10.7 %copy-start.4 = (bf16[4,2,144,512]{3,2,1,0:T(8,128)(2,1)S(1)}, bf16[4,2,144,512]{3,2,1,0:T(8,128)(2,1)}, u32[]{:S(2)}) copy-start(bf16[4,2,144,512]{3,2,1,0:T(8,128)(2,1)} %get-tuple-element.63) | copy-start | bytes 3538948
  6.2 10.7 %collective-permute-start.5 = (bf16[4,2,144,512]{3,2,1,0:T(8,128)(2,1)}, bf16[4,2,144,512]{3,2,1,0:T(8,128)(2,1)S(1)}, u32[]{:S(2)}, u32[]{:S(2)}) collective-permute-start(bf16[4,2,144,512]{3,2,1,0:T(8,128)(2,1)} %get-tuple-element.64), channel_id=1, source_target_pairs={{0,1},{1,0},{2,3},{3,2},{4,5},{5,4},{6,7},{7,6},{8,9},{9,8},{10,11... | collective-permute-start | bytes 3538952 | tf_op jit(solution)/shard_map/ppermute | solution.py:36
  6.3 6.2 %collective-permute-start.3 = (bf16[2,4,112,512]{3,2,1,0:T(8,128)(2,1)}, bf16[2,4,112,512]{3,2,1,0:T(8,128)(2,1)S(1)}, u32[]{:S(2)}, u32[]{:S(2)}) collective-permute-start(bf16[2,4,112,512]{3,2,1,0:T(8,128)(2,1)} %get-tuple-element.62), channel_id=1, source_target_pairs={{0,1},{1,0},{2,3},{3,2},{4,5},{5,4},{6,7},{7,6},{8,9},{9,8},{10,11... | collective-permute-start | bytes 2752520 | tf_op jit(solution)/shard_map/ppermute | solution.py:36
  6.8 11.4 %collective-permute-start = (bf16[128,512]{1,0:T(8,128)(2,1)}, bf16[128,512]{1,0:T(8,128)(2,1)S(1)}, u32[]{:S(2)}, u32[]{:S(2)}) collective-permute-start(bf16[128,512]{1,0:T(8,128)(2,1)} %get-tuple-element.58), channel_id=1, source_target_pairs={{0,4},{1,5},{2,6},{3,7},{4,8},{5,9},{6,10},{7,11},{8,12},{9,13},{1... | collective-permute-start | bytes 393224 | tf_op jit(solution)/shard_map/ppermute | solution.py:36
  8.3 11.6 %collective-permute-start.1 = (bf16[128,512]{1,0:T(8,128)(2,1)}, bf16[128,512]{1,0:T(8,128)(2,1)S(1)}, u32[]{:S(2)}, u32[]{:S(2)}) collective-permute-start(bf16[128,512]{1,0:T(8,128)(2,1)} %get-tuple-element.59), channel_id=1, source_target_pairs={{0,8},{1,9},{2,10},{3,11},{4,12},{5,13},{6,14},{7,15},{8,0},{9,1},... | collective-permute-start | bytes 393224 | tf_op jit(solution)/shard_map/ppermute | solution.py:36
  11.1 8.9 %collective-permute-start.2 = (bf16[128,512]{1,0:T(8,128)(2,1)}, bf16[128,512]{1,0:T(8,128)(2,1)S(1)}, u32[]{:S(2)}, u32[]{:S(2)}) collective-permute-start(bf16[128,512]{1,0:T(8,128)(2,1)} %get-tuple-element.60), channel_id=1, source_target_pairs={{0,12},{1,13},{2,14},{3,15},{4,0},{5,1},{6,2},{7,3},{8,4},{9,5},{1... | collective-permute-start | bytes 393224 | tf_op jit(solution)/shard_map/ppermute | solution.py:36
  13.6 18.9 %collective-permute-start.9 = (bf16[4,112,512]{2,1,0:T(8,128)(2,1)S(1)}, bf16[4,112,512]{2,1,0:T(8,128)(2,1)S(1)}, u32[]{:S(2)}, u32[]{:S(2)}) collective-permute-start(bf16[4,112,512]{2,1,0:T(8,128)(2,1)S(1)} %fusion.2.refs_4_), channel_id=1, source_target_pairs={{0,2},{1,3},{2,0},{3,1},{4,6},{5,7},{6,4},{7,5},{8,10},{9,11},{10,... | collective-permute-start | bytes 1376264 | tf_op jit(solution)/shard_map/ppermute | solution.py:36
  16.9 3.1 %copy-start = (bf16[128,512]{1,0:T(8,128)(2,1)S(1)}, bf16[128,512]{1,0:T(8,128)(2,1)}, u32[]{:S(2)}) copy-start(bf16[128,512]{1,0:T(8,128)(2,1)} %get-tuple-element.57.refs_0_.refs_2_.refs_9_) | copy-start | bytes 393220
  17.2 15.3 %collective-permute-start.8 = (bf16[2,144,512]{2,1,0:T(8,128)(2,1)S(1)}, bf16[2,144,512]{2,1,0:T(8,128)(2,1)S(1)}, u32[]{:S(2)}, u32[]{:S(2)}) collective-permute-start(bf16[2,144,512]{2,1,0:T(8,128)(2,1)S(1)} %get-tuple-element.111), channel_id=1, source_target_pairs={{0,12},{1,13},{2,14},{3,15},{4,0},{5,1},{6,2},{7,3},{8,4},{9,5},{1... | collective-permute-start | bytes 884744 | tf_op jit(solution)/shard_map/ppermute | solution.py:36
  18.3 14.3 %collective-permute-start.7 = (bf16[2,144,512]{2,1,0:T(8,128)(2,1)S(1)}, bf16[2,144,512]{2,1,0:T(8,128)(2,1)S(1)}, u32[]{:S(2)}, u32[]{:S(2)}) collective-permute-start(bf16[2,144,512]{2,1,0:T(8,128)(2,1)S(1)} %get-tuple-element.112), channel_id=1, source_target_pairs={{0,8},{1,9},{2,10},{3,11},{4,12},{5,13},{6,14},{7,15},{8,0},{9,1},... | collective-permute-start | bytes 884744 | tf_op jit(solution)/shard_map/ppermute | solution.py:36
  20.0 14.6 %collective-permute-start.6 = (bf16[2,144,512]{2,1,0:T(8,128)(2,1)S(1)}, bf16[2,144,512]{2,1,0:T(8,128)(2,1)S(1)}, u32[]{:S(2)}, u32[]{:S(2)}) collective-permute-start(bf16[2,144,512]{2,1,0:T(8,128)(2,1)S(1)} %get-tuple-element.113), channel_id=1, source_target_pairs={{0,4},{1,5},{2,6},{3,7},{4,8},{5,9},{6,10},{7,11},{8,12},{9,13},{1... | collective-permute-start | bytes 884744 | tf_op jit(solution)/shard_map/ppermute | solution.py:36
  20.0 12.5 %collective-permute-start.4 = (bf16[4,128,256]{2,1,0:T(8,128)(2,1)S(1)}, bf16[4,128,256]{2,1,0:T(8,128)(2,1)S(1)}, u32[]{:S(2)}, u32[]{:S(2)}) collective-permute-start(bf16[4,128,256]{2,1,0:T(8,128)(2,1)S(1)} %shard_map.120.refs_0_.refs_2_), channel_id=1, source_target_pairs={{0,2},{1,3},{2,0},{3,1},{4,6},{5,7},{6,4},{7,5},{8,10},{9,11},{10,... | collective-permute-start | bytes 786440 | tf_op jit(solution)/shard_map/ppermute | solution.py:36
  34.8 1.5 %copy-start.5 = (bf16[2,4,112,512]{3,2,1,0:T(8,128)(2,1)S(1)}, bf16[2,4,112,512]{3,2,1,0:T(8,128)(2,1)}, u32[]{:S(2)}) copy-start(bf16[2,4,112,512]{3,2,1,0:T(8,128)(2,1)} %get-tuple-element.61) | copy-start | bytes 2752516
  34.8 12.8 %collective-permute-start.11 = (bf16[144,512]{1,0:T(8,128)(2,1)S(1)}, bf16[144,512]{1,0:T(8,128)(2,1)S(1)}, u32[]{:S(2)}, u32[]{:S(2)}) collective-permute-start(bf16[144,512]{1,0:T(8,128)(2,1)S(1)} %fusion.12), channel_id=1, source_target_pairs={{0,2},{1,3},{2,0},{3,1},{4,6},{5,7},{6,4},{7,5},{8,10},{9,11},{10,... | collective-permute-start | bytes 442376 | tf_op jit(solution)/shard_map/ppermute | solution.py:36
  36.1 4.0 %copy-start.1 = (s32[1,2048]{1,0:T(1,128)S(1)}, s32[1,2048]{1,0:T(1,128)}, u32[]{:S(2)}) copy-start(s32[1,2048]{1,0:T(1,128)} %param.13) | copy-start | bytes 24580
  36.1 4.0 %copy-start.2 = (f32[128]{0:T(128)S(1)}, f32[128]{0:T(128)}, u32[]{:S(2)}) copy-start(f32[128]{0:T(128)} %param.11) | copy-start | bytes 1540
  36.1 4.0 %copy-start.3 = (f32[128]{0:T(128)S(1)}, f32[128]{0:T(128)}, u32[]{:S(2)}) copy-start(f32[128]{0:T(128)} %param.12) | copy-start | bytes 1540
  36.1 4.0 %collective-permute-start.10 = (bf16[2,4,128,256]{3,2,1,0:T(8,128)(2,1)S(1)}, bf16[2,4,128,256]{3,2,1,0:T(8,128)(2,1)S(1)}, u32[]{:S(2)}, u32[]{:S(2)}) collective-permute-start(bf16[2,4,128,256]{3,2,1,0:T(8,128)(2,1)S(1)} %shard_map.121.refs_0_), channel_id=1, source_target_pairs={{0,1},{1,0},{2,3},{3,2},{4,5},{5,4},{6,7},{7,6},{8,9},{9,8},{10,11... | collective-permute-start | bytes 1572872 | tf_op jit(solution)/shard_map/ppermute | solution.py:36
  36.5 7.7 %collective-permute-start.14 = (bf16[112,512]{1,0:T(8,128)(2,1)S(1)}, bf16[112,512]{1,0:T(8,128)(2,1)S(1)}, u32[]{:S(2)}, u32[]{:S(2)}) collective-permute-start(bf16[112,512]{1,0:T(8,128)(2,1)S(1)} %get-tuple-element.114), channel_id=1, source_target_pairs={{0,12},{1,13},{2,14},{3,15},{4,0},{5,1},{6,2},{7,3},{8,4},{9,5},{1... | collective-permute-start | bytes 344072 | tf_op jit(solution)/shard_map/ppermute | solution.py:36
  38.4 7.5 %collective-permute-start.13 = (bf16[112,512]{1,0:T(8,128)(2,1)S(1)}, bf16[112,512]{1,0:T(8,128)(2,1)S(1)}, u32[]{:S(2)}, u32[]{:S(2)}) collective-permute-start(bf16[112,512]{1,0:T(8,128)(2,1)S(1)} %get-tuple-element.115), channel_id=1, source_target_pairs={{0,8},{1,9},{2,10},{3,11},{4,12},{5,13},{6,14},{7,15},{8,0},{9,1},... | collective-permute-start | bytes 344072 | tf_op jit(solution)/shard_map/ppermute | solution.py:36
  39.3 8.4 %collective-permute-start.12 = (bf16[112,512]{1,0:T(8,128)(2,1)S(1)}, bf16[112,512]{1,0:T(8,128)(2,1)S(1)}, u32[]{:S(2)}, u32[]{:S(2)}) collective-permute-start(bf16[112,512]{1,0:T(8,128)(2,1)S(1)} %get-tuple-element.116), channel_id=1, source_target_pairs={{0,4},{1,5},{2,6},{3,7},{4,8},{5,9},{6,10},{7,11},{8,12},{9,13},{1... | collective-permute-start | bytes 344072 | tf_op jit(solution)/shard_map/ppermute | solution.py:36
  51.9 2.0 %collective-permute-start.15 = (bf16[2,4,128,256]{3,2,1,0:T(8,128)(2,1)S(1)}, bf16[2,4,128,256]{3,2,1,0:T(8,128)(2,1)S(1)}, u32[]{:S(2)}, u32[]{:S(2)}) collective-permute-start(bf16[2,4,128,256]{3,2,1,0:T(8,128)(2,1)S(1)} %get-tuple-element.91), channel_id=1, source_target_pairs={{0,1},{1,0},{2,3},{3,2},{4,5},{5,4},{6,7},{7,6},{8,9},{9,8},{10,11... | collective-permute-start | bytes 1572872 | tf_op jit(solution)/shard_map/ppermute | solution.py:36
  52.0 2.1 %collective-permute-start.16 = (f32[8,128]{1,0:T(8,128)S(1)}, f32[8,128]{1,0:T(8,128)S(1)}, u32[]{:S(2)}, u32[]{:S(2)}) collective-permute-start(f32[8,128]{1,0:T(8,128)S(1)} %get-tuple-element.94.refs_0_), channel_id=1, source_target_pairs={{0,1},{1,0},{2,3},{3,2},{4,5},{5,4},{6,7},{7,6},{8,9},{9,8},{10,11... | collective-permute-start | bytes 12296 | tf_op jit(solution)/shard_map/ppermute | solution.py:36
  54.1 4.9 %collective-permute-start.20 = (f32[8,128]{1,0:T(8,128)S(1)}, f32[8,128]{1,0:T(8,128)S(1)}, u32[]{:S(2)}, u32[]{:S(2)}) collective-permute-start(f32[8,128]{1,0:T(8,128)S(1)} %shard_map.124), channel_id=1, source_target_pairs={{0,130},{1,131},{2,128},{3,129},{4,134},{5,135},{6,132},{7,133},{8... | collective-permute-start | bytes 12296 | tf_op jit(solution)/shard_map/ppermute | solution.py:42
  55.2 3.8 %collective-permute-start.19 = (f32[8,128]{1,0:T(8,128)S(1)}, f32[8,128]{1,0:T(8,128)S(1)}, u32[]{:S(2)}, u32[]{:S(2)}) collective-permute-start(f32[8,128]{1,0:T(8,128)S(1)} %shard_map.124), channel_id=1, source_target_pairs={{0,128},{1,129},{2,130},{3,131},{4,132},{5,133},{6,134},{7,135},{8... | collective-permute-start | bytes 12296 | tf_op jit(solution)/shard_map/ppermute | solution.py:42
  55.3 5.3 %collective-permute-start.18 = (f32[8,128]{1,0:T(8,128)S(1)}, f32[8,128]{1,0:T(8,128)S(1)}, u32[]{:S(2)}, u32[]{:S(2)}) collective-permute-start(f32[8,128]{1,0:T(8,128)S(1)} %shard_map.124), channel_id=1, source_target_pairs={{0,2},{1,3},{2,0},{3,1},{4,6},{5,7},{6,4},{7,5},{8,10},{9,11},{10,... | collective-permute-start | bytes 12296 | tf_op jit(solution)/shard_map/ppermute | solution.py:42
  58.9 9.1 %collective-permute-start.17 = (bf16[4,128,256]{2,1,0:T(8,128)(2,1)S(1)}, bf16[4,128,256]{2,1,0:T(8,128)(2,1)S(1)}, u32[]{:S(2)}, u32[]{:S(2)}) collective-permute-start(bf16[4,128,256]{2,1,0:T(8,128)(2,1)S(1)} %fusion.8), channel_id=1, source_target_pairs={{0,2},{1,3},{2,0},{3,1},{4,6},{5,7},{6,4},{7,5},{8,10},{9,11},{10,... | collective-permute-start | bytes 786440 | tf_op jit(solution)/shard_map/ppermute | solution.py:36
  60.5 3.6 %collective-permute-start.22 = (f32[8,128]{1,0:T(8,128)S(1)}, f32[8,128]{1,0:T(8,128)S(1)}, u32[]{:S(2)}, u32[]{:S(2)}) collective-permute-start(f32[8,128]{1,0:T(8,128)S(1)} %add_add_fusion), channel_id=1, source_target_pairs={{112,0},{0,16},{16,32},{32,48},{48,64},{64,80},{80,96},{96,112},{2... | collective-permute-start | bytes 12296 | tf_op jit(solution)/shard_map/ppermute | solution.py:53
  62.4 3.6 %collective-permute-start.21 = (f32[8,128]{1,0:T(8,128)S(1)}, f32[8,128]{1,0:T(8,128)S(1)}, u32[]{:S(2)}, u32[]{:S(2)}) collective-permute-start(f32[8,128]{1,0:T(8,128)S(1)} %add_add_fusion), channel_id=1, source_target_pairs={{16,0},{32,16},{48,32},{64,48},{80,64},{96,80},{112,96},{0,112},{1... | collective-permute-start | bytes 12296 | tf_op jit(solution)/shard_map/ppermute | solution.py:53
  68.3 8.6 %collective-permute-start.23 = (bf16[144,512]{1,0:T(8,128)(2,1)S(1)}, bf16[144,512]{1,0:T(8,128)(2,1)S(1)}, u32[]{:S(2)}, u32[]{:S(2)}) collective-permute-start(bf16[144,512]{1,0:T(8,128)(2,1)S(1)} %get-tuple-element.101), channel_id=1, source_target_pairs={{0,4},{1,5},{2,6},{3,7},{4,8},{5,9},{6,10},{7,11},{8,12},{9,13},{1... | collective-permute-start | bytes 442376 | tf_op jit(solution)/shard_map/ppermute | solution.py:36
  68.4 8.5 %collective-permute-start.24 = (bf16[144,512]{1,0:T(8,128)(2,1)S(1)}, bf16[144,512]{1,0:T(8,128)(2,1)S(1)}, u32[]{:S(2)}, u32[]{:S(2)}) collective-permute-start(bf16[144,512]{1,0:T(8,128)(2,1)S(1)} %get-tuple-element.102), channel_id=1, source_target_pairs={{0,8},{1,9},{2,10},{3,11},{4,12},{5,13},{6,14},{7,15},{8,0},{9,1},... | collective-permute-start | bytes 442376 | tf_op jit(solution)/shard_map/ppermute | solution.py:36
  70.4 7.1 %collective-permute-start.25 = (bf16[144,512]{1,0:T(8,128)(2,1)S(1)}, bf16[144,512]{1,0:T(8,128)(2,1)S(1)}, u32[]{:S(2)}, u32[]{:S(2)}) collective-permute-start(bf16[144,512]{1,0:T(8,128)(2,1)S(1)} %get-tuple-element.103), channel_id=1, source_target_pairs={{0,12},{1,13},{2,14},{3,15},{4,0},{5,1},{6,2},{7,3},{8,4},{9,5},{1... | collective-permute-start | bytes 442376 | tf_op jit(solution)/shard_map/ppermute | solution.py:36
  77.5 7.5 %collective-permute-start.27 = (f32[8,128]{1,0:T(8,128)S(1)}, f32[8,128]{1,0:T(8,128)S(1)}, u32[]{:S(2)}, u32[]{:S(2)}) collective-permute-start(f32[8,128]{1,0:T(8,128)S(1)} %shard_map.127.refs_0_), channel_id=1, source_target_pairs={{80,0},{96,16},{112,32},{0,48},{16,64},{32,80},{48,96},{64,112},{2... | collective-permute-start | bytes 12296 | tf_op jit(solution)/shard_map/ppermute | solution.py:53
  83.5 6.6 %collective-permute-start.26 = (f32[8,128]{1,0:T(8,128)S(1)}, f32[8,128]{1,0:T(8,128)S(1)}, u32[]{:S(2)}, u32[]{:S(2)}) collective-permute-start(f32[8,128]{1,0:T(8,128)S(1)} %shard_map.127.refs_0_), channel_id=1, source_target_pairs={{48,0},{64,16},{80,32},{96,48},{112,64},{0,80},{16,96},{32,112},{1... | collective-permute-start | bytes 12296 | tf_op jit(solution)/shard_map/ppermute | solution.py:53

commit v4 on v3

--- a/solution.py
+++ b/solution.py
@@ -359,6 +359,7 @@
     kv_y = shift(kv_0, 0, 1, 0)
     kv_y, from_x, b_y = lax.optimization_barrier((kv_y, from_x, b_y))
     (kv_both,) = call(pair_kernel, [sds((2, NX, BLK, 256))], kv_0, kv_y)
+    kv_both, from_x = lax.optimization_barrier((kv_both, from_x))
     kv_swapped = shift(kv_both, 0, 0, 1)
 
     fwd = call(

time: 90.8 us -> 90.7 us (level)
  transfers between devices with their start and end apart: 28 -> 28, of which waited for: 13 -> 13; matrix products, arithmetic and copies ran while one was open for 2% -> 2% of each run, Pallas kernels for 6% -> 5%
where the time goes in v4:
time: 90.7 us; the launch traced here: 90.5 us
  waiting for transfers between devices  36.4 us (40%)
  starting transfers between devices  35.5 us (39%)
  Pallas kernels  15.6 us (17%)
  other arithmetic  2.01 us (2%)
    ppermute x21, waiting for transfers between devices, shift(): return lax.ppermute(value, 'seq', pairs)  25.8 us
    ppermute x21, starting transfers between devices, shift(): return lax.ppermute(value, 'seq', pairs)  22.7 us
    pallas_call x10, Pallas kernels, call(): pl.pallas_call(body, out_shape=outs, in_specs=[hbm if hbm_in else vmem] *...  15.6 us
    ppermute x4, waiting for transfers between devices, along_z(): return lax.ppermute(value, 'dp', pairs)  9.13 us
    ppermute x4, starting transfers between devices, along_z(): return lax.ppermute(value, 'dp', pairs)  8 us
    ppermute x3, starting transfers between devices, flip(): return lax.ppermute(value, ('dp', 'seq'), pairs)  4.79 us
  transfers between devices with their start and end apart: 28, of which 13 were waited for; matrix products, arithmetic and copies ran while one was open for 2% of the time, Pallas kernels for 5%

profile of v4, /device:TPU:32, one launch (start us, length us, event | category | flops | bytes accessed | tf_op | source)
XLA Modules:
  0.0 90.5 jit_solution(1014621839785367583)
XLA Ops:
  0.6 5.6 %shard_map.119 = (bf16[4,2,144,512]{3,2,1,0:T(8,128)(2,1)}, bf16[2,4,112,512]{3,2,1,0:T(8,128)(2,1)}, bf16[4,2,144,512]{3,2,1,0:T(8,128)(2,1)}, bf16[2,4,112,512...) custom-call(bf16[448,1024]{1,0:T(8,128)(2,1)} %refs_0_.1, ...), custom_call_target="tpu_custom_call" | custom-call | flops 6000000000 | bytes 1 | tf_op jit(solution)/shard_map/pallas_call | solution.py:65
  6.2 0.1 collective-permute-start.5
  6.3 0.5 collective-permute-start.3
  6.8 1.5 %collective-permute-start = (bf16[128,512]{1,0:T(8,128)(2,1)}, bf16[128,512]{1,0:T(8,128)(2,1)S(1)}, u32[]{:S(2)}, u32[]{:S(2)}) collective-permute-start(bf16[128,512]{1,0:T(8,128)(2,1)} %get-tuple-element.62), channel_id=1, source_target_pairs={{0,4},{1,5},{2,6},{3,7},{4,8},{5,9},{6,10},{7,11},{8,12},{9,13},{1... | collective-permute-start | bytes 393224 | tf_op jit(solution)/shard_map/ppermute | solution.py:36
  8.3 2.7 %collective-permute-start.1 = (bf16[128,512]{1,0:T(8,128)(2,1)}, bf16[128,512]{1,0:T(8,128)(2,1)S(1)}, u32[]{:S(2)}, u32[]{:S(2)}) collective-permute-start(bf16[128,512]{1,0:T(8,128)(2,1)} %get-tuple-element.63), channel_id=1, source_target_pairs={{0,8},{1,9},{2,10},{3,11},{4,12},{5,13},{6,14},{7,15},{8,0},{9,1},... | collective-permute-start | bytes 393224 | tf_op jit(solution)/shard_map/ppermute | solution.py:36
  11.1 1.4 %collective-permute-start.2 = (bf16[128,512]{1,0:T(8,128)(2,1)}, bf16[128,512]{1,0:T(8,128)(2,1)S(1)}, u32[]{:S(2)}, u32[]{:S(2)}) collective-permute-start(bf16[128,512]{1,0:T(8,128)(2,1)} %get-tuple-element.64), channel_id=1, source_target_pairs={{0,12},{1,13},{2,14},{3,15},{4,0},{5,1},{6,2},{7,3},{8,4},{9,5},{1... | collective-permute-start | bytes 393224 | tf_op jit(solution)/shard_map/ppermute | solution.py:36
  12.5 0.0 collective-permute-done.3
  12.5 1.1 %fusion.2.refs_4_ = bf16[4,112,512]{2,1,0:T(8,128)(2,1)S(1)} fusion(bf16[2,4,112,512]{3,2,1,0:T(8,128)(2,1)S(1)} %collective-permute-done.3, bf16[2,4,112,512]{3,2,1,0:T(8,128)(2,1)} %get-tuple-element.65), kind=kLoop, calls=%fused_computation.12 | loop fusion | flops 917504 | bytes 1376256 | tf_op jit(solution)/shard_map/convert_element_type | solution.py:350
  13.6 3.3 %collective-permute-start.9 = (bf16[4,112,512]{2,1,0:T(8,128)(2,1)S(1)}, bf16[4,112,512]{2,1,0:T(8,128)(2,1)S(1)}, u32[]{:S(2)}, u32[]{:S(2)}) collective-permute-start(bf16[4,112,512]{2,1,0:T(8,128)(2,1)S(1)} %fusion.2.refs_4_), channel_id=1, source_target_pairs={{0,2},{1,3},{2,0},{3,1},{4,6},{5,7},{6,4},{7,5},{8,10},{9,11},{10,... | collective-permute-start | bytes 1376264 | tf_op jit(solution)/shard_map/ppermute | solution.py:36
  16.9 0.0 collective-permute-done.5
  16.9 0.3 fusion.5
  17.2 1.1 %collective-permute-start.8 = (bf16[2,144,512]{2,1,0:T(8,128)(2,1)S(1)}, bf16[2,144,512]{2,1,0:T(8,128)(2,1)S(1)}, u32[]{:S(2)}, u32[]{:S(2)}) collective-permute-start(bf16[2,144,512]{2,1,0:T(8,128)(2,1)S(1)} %get-tuple-element.119), channel_id=1, source_target_pairs={{0,12},{1,13},{2,14},{3,15},{4,0},{5,1},{6,2},{7,3},{8,4},{9,5},{1... | collective-permute-start | bytes 884744 | tf_op jit(solution)/shard_map/ppermute | solution.py:36
  18.3 0.0 collective-permute-done.refs_1_.refs_3_.refs_10_
  18.3 1.7 %collective-permute-start.7 = (bf16[2,144,512]{2,1,0:T(8,128)(2,1)S(1)}, bf16[2,144,512]{2,1,0:T(8,128)(2,1)S(1)}, u32[]{:S(2)}, u32[]{:S(2)}) collective-permute-start(bf16[2,144,512]{2,1,0:T(8,128)(2,1)S(1)} %get-tuple-element.120), channel_id=1, source_target_pairs={{0,8},{1,9},{2,10},{3,11},{4,12},{5,13},{6,14},{7,15},{8,0},{9,1},... | collective-permute-start | bytes 884744 | tf_op jit(solution)/shard_map/ppermute | solution.py:36
  20.0 0.0 collective-permute-done.1.refs_2_.refs_4_.refs_11_
  20.0 0.0 collective-permute-start.6
  20.0 0.0 collective-permute-done.2.refs_3_.refs_5_.refs_12_
  20.0 1.4 %collective-permute-start.4 = (bf16[4,128,256]{2,1,0:T(8,128)(2,1)S(1)}, bf16[4,128,256]{2,1,0:T(8,128)(2,1)S(1)}, u32[]{:S(2)}, u32[]{:S(2)}) collective-permute-start(bf16[4,128,256]{2,1,0:T(8,128)(2,1)S(1)} %shard_map.120.refs_0_.refs_2_), channel_id=1, source_target_pairs={{0,2},{1,3},{2,0},{3,1},{4,6},{5,7},{6,4},{7,5},{8,10},{9,11},{10,... | collective-permute-start | bytes 786440 | tf_op jit(solution)/shard_map/ppermute | solution.py:36
  21.4 11.2 %collective-permute-done.4.refs_1_ = bf16[4,128,256]{2,1,0:T(8,128)(2,1)S(1)} collective-permute-done((bf16[4,128,256]{2,1,0:T(8,128)(2,1)S(1)}, bf16[4,128,256]{2,1,0:T(8,128)(2,1)S(1)}, u32[]{:S(2)}, u32[]{:S(2)}) %collective-permute-start.4) | collective-permute-done | bytes 262176 | tf_op jit(solution)/shard_map/ppermute | solution.py:36
  32.5 0.0 collective-permute-done.9
  32.5 0.0 collective-permute-done.8
  32.5 0.0 collective-permute-done.7
  32.6 2.0 %collective-permute-done.6 = bf16[2,144,512]{2,1,0:T(8,128)(2,1)S(1)} collective-permute-done((bf16[2,144,512]{2,1,0:T(8,128)(2,1)S(1)}, bf16[2,144,512]{2,1,0:T(8,128)(2,1)S(1)}, u32[]{:S(2)}, u32[]{:S(2)}) %collective-permute-start.6) | collective-permute-done | bytes 294944 | tf_op jit(solution)/shard_map/ppermute | solution.py:36
  34.6 0.2 fusion.1
  34.9 0.0 copy-start.1
  34.9 0.0 copy-start.2
  34.9 0.0 copy-start.3
  34.9 1.2 %collective-permute-start.11 = (bf16[144,512]{1,0:T(8,128)(2,1)S(1)}, bf16[144,512]{1,0:T(8,128)(2,1)S(1)}, u32[]{:S(2)}, u32[]{:S(2)}) collective-permute-start(bf16[144,512]{1,0:T(8,128)(2,1)S(1)} %fusion.12), channel_id=1, source_target_pairs={{0,2},{1,3},{2,0},{3,1},{4,6},{5,7},{6,4},{7,5},{8,10},{9,11},{10,... | collective-permute-start | bytes 442376 | tf_op jit(solution)/shard_map/ppermute | solution.py:36
  36.1 0.0 collective-permute-start.10
  36.2 0.2 fusion.13
  36.4 1.9 %collective-permute-start.14 = (bf16[112,512]{1,0:T(8,128)(2,1)S(1)}, bf16[112,512]{1,0:T(8,128)(2,1)S(1)}, u32[]{:S(2)}, u32[]{:S(2)}) collective-permute-start(bf16[112,512]{1,0:T(8,128)(2,1)S(1)} %get-tuple-element.122), channel_id=1, source_target_pairs={{0,12},{1,13},{2,14},{3,15},{4,0},{5,1},{6,2},{7,3},{8,4},{9,5},{1... | collective-permute-start | bytes 344072 | tf_op jit(solution)/shard_map/ppermute | solution.py:36
  38.3 0.8 collective-permute-start.13
  39.2 0.8 collective-permute-start.12
  40.0 4.1 %shard_map.122 = (bf16[2048,128]{1,0:T(8,128)(2,1)S(1)}, bf16[128,2048]{1,0:T(8,128)(2,1)S(1)}, bf16[2048,128]{1,0:T(8,128)(2,1)S(1)}, f32[2048,128]{1,0:T(8,128...) custom-call(bf16[2,4,128,256]{3,2,1,0:T(8,128)(2,1)S(1)} %shard_map., ...), custom_call_target="tpu_custom_call" | custom-call | flops 1 | bytes 1 | tf_op jit(solution)/shard_map/pallas_call | solution.py:65
  44.1 1.7 %collective-permute-done.13 = bf16[112,512]{1,0:T(8,128)(2,1)S(1)} collective-permute-done((bf16[112,512]{1,0:T(8,128)(2,1)S(1)}, bf16[112,512]{1,0:T(8,128)(2,1)S(1)}, u32[]{:S(2)}, u32[]{:S(2)}) %collective-permute-start.13) | collective-permute-done | bytes 114720 | tf_op jit(solution)/shard_map/ppermute | solution.py:36
  45.8 1.8 %collective-permute-done.12 = bf16[112,512]{1,0:T(8,128)(2,1)S(1)} collective-permute-done((bf16[112,512]{1,0:T(8,128)(2,1)S(1)}, bf16[112,512]{1,0:T(8,128)(2,1)S(1)}, u32[]{:S(2)}, u32[]{:S(2)}) %collective-permute-start.12) | collective-permute-done | bytes 114720 | tf_op jit(solution)/shard_map/ppermute | solution.py:36
  47.6 0.1 fusion.11.refs_8_
  47.7 4.2 %shard_map.123 = (bf16[128,256]{1,0:T(8,128)(2,1)S(1)}, bf16[128,256]{1,0:T(8,128)(2,1)S(1)}, bf16[128,256]{1,0:T(8,128)(2,1)S(1)}, bf16[128,256]{1,0:T(8,128)(2...) custom-call(bf16[2048,128]{1,0:T(8,128)(2,1)S(1)} %get-tuple-element.86.re, ...), custom_call_target="tpu_custom_call" | custom-call | flops 1 | bytes 1 | tf_op jit(solution)/shard_map/pallas_call | solution.py:65
  51.8 0.1 collective-permute-start.15
  51.9 0.5 collective-permute-start.16
  52.4 1.4 %collective-permute-done.15 = bf16[2,4,128,256]{3,2,1,0:T(8,128)(2,1)S(1)} collective-permute-done((bf16[2,4,128,256]{3,2,1,0:T(8,128)(2,1)S(1)}, bf16[2,4,128,256]{3,2,1,0:T(8,128)(2,1)S(1)}, u32[]{:S(2)}, u32[]{:S(2)}) %collective-permute-start.15) | collective-permute-done | bytes 524320 | tf_op jit(solution)/shard_map/ppermute | solution.py:36
  53.8 0.1 convert_add_fusion
  54.0 1.1 %collective-permute-start.20 = (f32[8,128]{1,0:T(8,128)S(1)}, f32[8,128]{1,0:T(8,128)S(1)}, u32[]{:S(2)}, u32[]{:S(2)}) collective-permute-start(f32[8,128]{1,0:T(8,128)S(1)} %shard_map.124), channel_id=1, source_target_pairs={{0,130},{1,131},{2,128},{3,129},{4,134},{5,135},{6,132},{7,133},{8... | collective-permute-start | bytes 12296 | tf_op jit(solution)/shard_map/ppermute | solution.py:42
  55.1 0.0 collective-permute-start.19
  55.2 3.6 %collective-permute-start.18 = (f32[8,128]{1,0:T(8,128)S(1)}, f32[8,128]{1,0:T(8,128)S(1)}, u32[]{:S(2)}, u32[]{:S(2)}) collective-permute-start(f32[8,128]{1,0:T(8,128)S(1)} %shard_map.124), channel_id=1, source_target_pairs={{0,2},{1,3},{2,0},{3,1},{4,6},{5,7},{6,4},{7,5},{8,10},{9,11},{10,... | collective-permute-start | bytes 12296 | tf_op jit(solution)/shard_map/ppermute | solution.py:42
  58.8 0.1 collective-permute-start.17
  59.0 1.5 %collective-permute-done.18 = f32[8,128]{1,0:T(8,128)S(1)} collective-permute-done((f32[8,128]{1,0:T(8,128)S(1)}, f32[8,128]{1,0:T(8,128)S(1)}, u32[]{:S(2)}, u32[]{:S(2)}) %collective-permute-start.18) | collective-permute-done | bytes 4128 | tf_op jit(solution)/shard_map/ppermute | solution.py:42
  60.4 1.9 %collective-permute-start.22 = (f32[8,128]{1,0:T(8,128)S(1)}, f32[8,128]{1,0:T(8,128)S(1)}, u32[]{:S(2)}, u32[]{:S(2)}) collective-permute-start(f32[8,128]{1,0:T(8,128)S(1)} %add_add_fusion), channel_id=1, source_target_pairs={{112,0},{0,16},{16,32},{32,48},{48,64},{64,80},{80,96},{96,112},{2... | collective-permute-start | bytes 12296 | tf_op jit(solution)/shard_map/ppermute | solution.py:53
  62.3 0.1 collective-permute-start.21
  62.5 1.6 %collective-permute-done.22 = f32[8,128]{1,0:T(8,128)S(1)} collective-permute-done((f32[8,128]{1,0:T(8,128)S(1)}, f32[8,128]{1,0:T(8,128)S(1)}, u32[]{:S(2)}, u32[]{:S(2)}) %collective-permute-start.22) | collective-permute-done | bytes 4128 | tf_op jit(solution)/shard_map/ppermute | solution.py:53
  64.0 1.9 %collective-permute-done.21 = f32[8,128]{1,0:T(8,128)S(1)} collective-permute-done((f32[8,128]{1,0:T(8,128)S(1)}, f32[8,128]{1,0:T(8,128)S(1)}, u32[]{:S(2)}, u32[]{:S(2)}) %collective-permute-start.21) | collective-permute-done | bytes 4128 | tf_op jit(solution)/shard_map/ppermute | solution.py:53
  65.9 2.0 %collective-permute-done.17.refs_1_ = bf16[4,128,256]{2,1,0:T(8,128)(2,1)S(1)} collective-permute-done((bf16[4,128,256]{2,1,0:T(8,128)(2,1)S(1)}, bf16[4,128,256]{2,1,0:T(8,128)(2,1)S(1)}, u32[]{:S(2)}, u32[]{:S(2)}) %collective-permute-start.17) | collective-permute-done | bytes 262176 | tf_op jit(solution)/shard_map/ppermute | solution.py:36
  67.9 0.2 shard_map.125
  68.2 0.1 collective-permute-start.23
  68.3 2.0 %collective-permute-start.24 = (bf16[144,512]{1,0:T(8,128)(2,1)S(1)}, bf16[144,512]{1,0:T(8,128)(2,1)S(1)}, u32[]{:S(2)}, u32[]{:S(2)}) collective-permute-start(bf16[144,512]{1,0:T(8,128)(2,1)S(1)} %get-tuple-element.110), channel_id=1, source_target_pairs={{0,8},{1,9},{2,10},{3,11},{4,12},{5,13},{6,14},{7,15},{8,0},{9,1},... | collective-permute-start | bytes 442376 | tf_op jit(solution)/shard_map/ppermute | solution.py:36
  70.3 1.4 %collective-permute-start.25 = (bf16[144,512]{1,0:T(8,128)(2,1)S(1)}, bf16[144,512]{1,0:T(8,128)(2,1)S(1)}, u32[]{:S(2)}, u32[]{:S(2)}) collective-permute-start(bf16[144,512]{1,0:T(8,128)(2,1)S(1)} %get-tuple-element.111), channel_id=1, source_target_pairs={{0,12},{1,13},{2,14},{3,15},{4,0},{5,1},{6,2},{7,3},{8,4},{9,5},{1... | collective-permute-start | bytes 442376 | tf_op jit(solution)/shard_map/ppermute | solution.py:36
  71.7 5.0 %collective-permute-done.23.refs_1_ = bf16[144,512]{1,0:T(8,128)(2,1)S(1)} collective-permute-done((bf16[144,512]{1,0:T(8,128)(2,1)S(1)}, bf16[144,512]{1,0:T(8,128)(2,1)S(1)}, u32[]{:S(2)}, u32[]{:S(2)}) %collective-permute-start.23) | collective-permute-done | bytes 147488 | tf_op jit(solution)/shard_map/ppermute | solution.py:36
  76.8 0.7 collective-permute-done.25.refs_3_
  77.5 5.9 %collective-permute-start.27 = (f32[8,128]{1,0:T(8,128)S(1)}, f32[8,128]{1,0:T(8,128)S(1)}, u32[]{:S(2)}, u32[]{:S(2)}) collective-permute-start(f32[8,128]{1,0:T(8,128)S(1)} %shard_map.127.refs_0_), channel_id=1, source_target_pairs={{80,0},{96,16},{112,32},{0,48},{16,64},{32,80},{48,96},{64,112},{2... | collective-permute-start | bytes 12296 | tf_op jit(solution)/shard_map/ppermute | solution.py:53
  83.4 0.1 collective-permute-start.26
  83.4 0.9 shard_map.126
  84.3 0.6 collective-permute-done.27.refs_2_
  84.9 5.1 %collective-permute-done.26.refs_1_ = f32[8,128]{1,0:T(8,128)S(1)} collective-permute-done((f32[8,128]{1,0:T(8,128)S(1)}, f32[8,128]{1,0:T(8,128)S(1)}, u32[]{:S(2)}, u32[]{:S(2)}) %collective-permute-start.26) | collective-permute-done | bytes 4128 | tf_op jit(solution)/shard_map/ppermute | solution.py:53
  90.0 0.5 shard_map.128
  (30 shorter events, 0.3 us)
Async XLA Ops:
  6.2 10.7 %copy-start.4 = (bf16[4,2,144,512]{3,2,1,0:T(8,128)(2,1)S(1)}, bf16[4,2,144,512]{3,2,1,0:T(8,128)(2,1)}, u32[]{:S(2)}) copy-start(bf16[4,2,144,512]{3,2,1,0:T(8,128)(2,1)} %get-tuple-element.67) | copy-start | bytes 3538948
  6.2 10.7 %collective-permute-start.5 = (bf16[4,2,144,512]{3,2,1,0:T(8,128)(2,1)}, bf16[4,2,144,512]{3,2,1,0:T(8,128)(2,1)S(1)}, u32[]{:S(2)}, u32[]{:S(2)}) collective-permute-start(bf16[4,2,144,512]{3,2,1,0:T(8,128)(2,1)} %get-tuple-element.68), channel_id=1, source_target_pairs={{0,1},{1,0},{2,3},{3,2},{4,5},{5,4},{6,7},{7,6},{8,9},{9,8},{10,11... | collective-permute-start | bytes 3538952 | tf_op jit(solution)/shard_map/ppermute | solution.py:36
  6.3 6.2 %collective-permute-start.3 = (bf16[2,4,112,512]{3,2,1,0:T(8,128)(2,1)}, bf16[2,4,112,512]{3,2,1,0:T(8,128)(2,1)S(1)}, u32[]{:S(2)}, u32[]{:S(2)}) collective-permute-start(bf16[2,4,112,512]{3,2,1,0:T(8,128)(2,1)} %get-tuple-element.66), channel_id=1, source_target_pairs={{0,1},{1,0},{2,3},{3,2},{4,5},{5,4},{6,7},{7,6},{8,9},{9,8},{10,11... | collective-permute-start | bytes 2752520 | tf_op jit(solution)/shard_map/ppermute | solution.py:36
  6.8 11.4 %collective-permute-start = (bf16[128,512]{1,0:T(8,128)(2,1)}, bf16[128,512]{1,0:T(8,128)(2,1)S(1)}, u32[]{:S(2)}, u32[]{:S(2)}) collective-permute-start(bf16[128,512]{1,0:T(8,128)(2,1)} %get-tuple-element.62), channel_id=1, source_target_pairs={{0,4},{1,5},{2,6},{3,7},{4,8},{5,9},{6,10},{7,11},{8,12},{9,13},{1... | collective-permute-start | bytes 393224 | tf_op jit(solution)/shard_map/ppermute | solution.py:36
  8.3 11.6 %collective-permute-start.1 = (bf16[128,512]{1,0:T(8,128)(2,1)}, bf16[128,512]{1,0:T(8,128)(2,1)S(1)}, u32[]{:S(2)}, u32[]{:S(2)}) collective-permute-start(bf16[128,512]{1,0:T(8,128)(2,1)} %get-tuple-element.63), channel_id=1, source_target_pairs={{0,8},{1,9},{2,10},{3,11},{4,12},{5,13},{6,14},{7,15},{8,0},{9,1},... | collective-permute-start | bytes 393224 | tf_op jit(solution)/shard_map/ppermute | solution.py:36
  11.1 8.9 %collective-permute-start.2 = (bf16[128,512]{1,0:T(8,128)(2,1)}, bf16[128,512]{1,0:T(8,128)(2,1)S(1)}, u32[]{:S(2)}, u32[]{:S(2)}) collective-permute-start(bf16[128,512]{1,0:T(8,128)(2,1)} %get-tuple-element.64), channel_id=1, source_target_pairs={{0,12},{1,13},{2,14},{3,15},{4,0},{5,1},{6,2},{7,3},{8,4},{9,5},{1... | collective-permute-start | bytes 393224 | tf_op jit(solution)/shard_map/ppermute | solution.py:36
  13.6 18.9 %collective-permute-start.9 = (bf16[4,112,512]{2,1,0:T(8,128)(2,1)S(1)}, bf16[4,112,512]{2,1,0:T(8,128)(2,1)S(1)}, u32[]{:S(2)}, u32[]{:S(2)}) collective-permute-start(bf16[4,112,512]{2,1,0:T(8,128)(2,1)S(1)} %fusion.2.refs_4_), channel_id=1, source_target_pairs={{0,2},{1,3},{2,0},{3,1},{4,6},{5,7},{6,4},{7,5},{8,10},{9,11},{10,... | collective-permute-start | bytes 1376264 | tf_op jit(solution)/shard_map/ppermute | solution.py:36
  16.9 3.1 %copy-start = (bf16[128,512]{1,0:T(8,128)(2,1)S(1)}, bf16[128,512]{1,0:T(8,128)(2,1)}, u32[]{:S(2)}) copy-start(bf16[128,512]{1,0:T(8,128)(2,1)} %get-tuple-element.61.refs_0_.refs_2_.refs_9_) | copy-start | bytes 393220
  17.2 15.3 %collective-permute-start.8 = (bf16[2,144,512]{2,1,0:T(8,128)(2,1)S(1)}, bf16[2,144,512]{2,1,0:T(8,128)(2,1)S(1)}, u32[]{:S(2)}, u32[]{:S(2)}) collective-permute-start(bf16[2,144,512]{2,1,0:T(8,128)(2,1)S(1)} %get-tuple-element.119), channel_id=1, source_target_pairs={{0,12},{1,13},{2,14},{3,15},{4,0},{5,1},{6,2},{7,3},{8,4},{9,5},{1... | collective-permute-start | bytes 884744 | tf_op jit(solution)/shard_map/ppermute | solution.py:36
  18.3 14.3 %collective-permute-start.7 = (bf16[2,144,512]{2,1,0:T(8,128)(2,1)S(1)}, bf16[2,144,512]{2,1,0:T(8,128)(2,1)S(1)}, u32[]{:S(2)}, u32[]{:S(2)}) collective-permute-start(bf16[2,144,512]{2,1,0:T(8,128)(2,1)S(1)} %get-tuple-element.120), channel_id=1, source_target_pairs={{0,8},{1,9},{2,10},{3,11},{4,12},{5,13},{6,14},{7,15},{8,0},{9,1},... | collective-permute-start | bytes 884744 | tf_op jit(solution)/shard_map/ppermute | solution.py:36
  20.0 14.6 %collective-permute-start.6 = (bf16[2,144,512]{2,1,0:T(8,128)(2,1)S(1)}, bf16[2,144,512]{2,1,0:T(8,128)(2,1)S(1)}, u32[]{:S(2)}, u32[]{:S(2)}) collective-permute-start(bf16[2,144,512]{2,1,0:T(8,128)(2,1)S(1)} %get-tuple-element.121), channel_id=1, source_target_pairs={{0,4},{1,5},{2,6},{3,7},{4,8},{5,9},{6,10},{7,11},{8,12},{9,13},{1... | collective-permute-start | bytes 884744 | tf_op jit(solution)/shard_map/ppermute | solution.py:36
  20.0 12.5 %collective-permute-start.4 = (bf16[4,128,256]{2,1,0:T(8,128)(2,1)S(1)}, bf16[4,128,256]{2,1,0:T(8,128)(2,1)S(1)}, u32[]{:S(2)}, u32[]{:S(2)}) collective-permute-start(bf16[4,128,256]{2,1,0:T(8,128)(2,1)S(1)} %shard_map.120.refs_0_.refs_2_), channel_id=1, source_target_pairs={{0,2},{1,3},{2,0},{3,1},{4,6},{5,7},{6,4},{7,5},{8,10},{9,11},{10,... | collective-permute-start | bytes 786440 | tf_op jit(solution)/shard_map/ppermute | solution.py:36
  34.6 1.5 %copy-start.5 = (bf16[2,4,112,512]{3,2,1,0:T(8,128)(2,1)S(1)}, bf16[2,4,112,512]{3,2,1,0:T(8,128)(2,1)}, u32[]{:S(2)}) copy-start(bf16[2,4,112,512]{3,2,1,0:T(8,128)(2,1)} %get-tuple-element.65) | copy-start | bytes 2752516
  34.9 5.1 %copy-start.1 = (s32[1,2048]{1,0:T(1,128)S(1)}, s32[1,2048]{1,0:T(1,128)}, u32[]{:S(2)}) copy-start(s32[1,2048]{1,0:T(1,128)} %param.13) | copy-start | bytes 24580
  34.9 5.1 %copy-start.2 = (f32[128]{0:T(128)S(1)}, f32[128]{0:T(128)}, u32[]{:S(2)}) copy-start(f32[128]{0:T(128)} %param.11) | copy-start | bytes 1540
  34.9 5.1 %copy-start.3 = (f32[128]{0:T(128)S(1)}, f32[128]{0:T(128)}, u32[]{:S(2)}) copy-start(f32[128]{0:T(128)} %param.12) | copy-start | bytes 1540
  34.9 12.7 %collective-permute-start.11 = (bf16[144,512]{1,0:T(8,128)(2,1)S(1)}, bf16[144,512]{1,0:T(8,128)(2,1)S(1)}, u32[]{:S(2)}, u32[]{:S(2)}) collective-permute-start(bf16[144,512]{1,0:T(8,128)(2,1)S(1)} %fusion.12), channel_id=1, source_target_pairs={{0,2},{1,3},{2,0},{3,1},{4,6},{5,7},{6,4},{7,5},{8,10},{9,11},{10,... | collective-permute-start | bytes 442376 | tf_op jit(solution)/shard_map/ppermute | solution.py:36
  36.1 3.8 %collective-permute-start.10 = (bf16[2,4,128,256]{3,2,1,0:T(8,128)(2,1)S(1)}, bf16[2,4,128,256]{3,2,1,0:T(8,128)(2,1)S(1)}, u32[]{:S(2)}, u32[]{:S(2)}) collective-permute-start(bf16[2,4,128,256]{3,2,1,0:T(8,128)(2,1)S(1)} %shard_map.121.refs_0_), channel_id=1, source_target_pairs={{0,1},{1,0},{2,3},{3,2},{4,5},{5,4},{6,7},{7,6},{8,9},{9,8},{10,11... | collective-permute-start | bytes 1572872 | tf_op jit(solution)/shard_map/ppermute | solution.py:36
  36.4 7.7 %collective-permute-start.14 = (bf16[112,512]{1,0:T(8,128)(2,1)S(1)}, bf16[112,512]{1,0:T(8,128)(2,1)S(1)}, u32[]{:S(2)}, u32[]{:S(2)}) collective-permute-start(bf16[112,512]{1,0:T(8,128)(2,1)S(1)} %get-tuple-element.122), channel_id=1, source_target_pairs={{0,12},{1,13},{2,14},{3,15},{4,0},{5,1},{6,2},{7,3},{8,4},{9,5},{1... | collective-permute-start | bytes 344072 | tf_op jit(solution)/shard_map/ppermute | solution.py:36
  38.3 7.5 %collective-permute-start.13 = (bf16[112,512]{1,0:T(8,128)(2,1)S(1)}, bf16[112,512]{1,0:T(8,128)(2,1)S(1)}, u32[]{:S(2)}, u32[]{:S(2)}) collective-permute-start(bf16[112,512]{1,0:T(8,128)(2,1)S(1)} %get-tuple-element.123), channel_id=1, source_target_pairs={{0,8},{1,9},{2,10},{3,11},{4,12},{5,13},{6,14},{7,15},{8,0},{9,1},... | collective-permute-start | bytes 344072 | tf_op jit(solution)/shard_map/ppermute | solution.py:36
  39.2 8.4 %collective-permute-start.12 = (bf16[112,512]{1,0:T(8,128)(2,1)S(1)}, bf16[112,512]{1,0:T(8,128)(2,1)S(1)}, u32[]{:S(2)}, u32[]{:S(2)}) collective-permute-start(bf16[112,512]{1,0:T(8,128)(2,1)S(1)} %get-tuple-element.124), channel_id=1, source_target_pairs={{0,4},{1,5},{2,6},{3,7},{4,8},{5,9},{6,10},{7,11},{8,12},{9,13},{1... | collective-permute-start | bytes 344072 | tf_op jit(solution)/shard_map/ppermute | solution.py:36
  51.8 2.0 %collective-permute-start.15 = (bf16[2,4,128,256]{3,2,1,0:T(8,128)(2,1)S(1)}, bf16[2,4,128,256]{3,2,1,0:T(8,128)(2,1)S(1)}, u32[]{:S(2)}, u32[]{:S(2)}) collective-permute-start(bf16[2,4,128,256]{3,2,1,0:T(8,128)(2,1)S(1)} %get-tuple-element.99), channel_id=1, source_target_pairs={{0,1},{1,0},{2,3},{3,2},{4,5},{5,4},{6,7},{7,6},{8,9},{9,8},{10,11... | collective-permute-start | bytes 1572872 | tf_op jit(solution)/shard_map/ppermute | solution.py:36
  51.9 2.1 %collective-permute-start.16 = (f32[8,128]{1,0:T(8,128)S(1)}, f32[8,128]{1,0:T(8,128)S(1)}, u32[]{:S(2)}, u32[]{:S(2)}) collective-permute-start(f32[8,128]{1,0:T(8,128)S(1)} %get-tuple-element.102.refs_0_), channel_id=1, source_target_pairs={{0,1},{1,0},{2,3},{3,2},{4,5},{5,4},{6,7},{7,6},{8,9},{9,8},{10,11... | collective-permute-start | bytes 12296 | tf_op jit(solution)/shard_map/ppermute | solution.py:36
  54.0 4.9 %collective-permute-start.20 = (f32[8,128]{1,0:T(8,128)S(1)}, f32[8,128]{1,0:T(8,128)S(1)}, u32[]{:S(2)}, u32[]{:S(2)}) collective-permute-start(f32[8,128]{1,0:T(8,128)S(1)} %shard_map.124), channel_id=1, source_target_pairs={{0,130},{1,131},{2,128},{3,129},{4,134},{5,135},{6,132},{7,133},{8... | collective-permute-start | bytes 12296 | tf_op jit(solution)/shard_map/ppermute | solution.py:42
  55.1 3.8 %collective-permute-start.19 = (f32[8,128]{1,0:T(8,128)S(1)}, f32[8,128]{1,0:T(8,128)S(1)}, u32[]{:S(2)}, u32[]{:S(2)}) collective-permute-start(f32[8,128]{1,0:T(8,128)S(1)} %shard_map.124), channel_id=1, source_target_pairs={{0,128},{1,129},{2,130},{3,131},{4,132},{5,133},{6,134},{7,135},{8... | collective-permute-start | bytes 12296 | tf_op jit(solution)/shard_map/ppermute | solution.py:42
  55.2 5.3 %collective-permute-start.18 = (f32[8,128]{1,0:T(8,128)S(1)}, f32[8,128]{1,0:T(8,128)S(1)}, u32[]{:S(2)}, u32[]{:S(2)}) collective-permute-start(f32[8,128]{1,0:T(8,128)S(1)} %shard_map.124), channel_id=1, source_target_pairs={{0,2},{1,3},{2,0},{3,1},{4,6},{5,7},{6,4},{7,5},{8,10},{9,11},{10,... | collective-permute-start | bytes 12296 | tf_op jit(solution)/shard_map/ppermute | solution.py:42
  58.8 9.1 %collective-permute-start.17 = (bf16[4,128,256]{2,1,0:T(8,128)(2,1)S(1)}, bf16[4,128,256]{2,1,0:T(8,128)(2,1)S(1)}, u32[]{:S(2)}, u32[]{:S(2)}) collective-permute-start(bf16[4,128,256]{2,1,0:T(8,128)(2,1)S(1)} %fusion.8), channel_id=1, source_target_pairs={{0,2},{1,3},{2,0},{3,1},{4,6},{5,7},{6,4},{7,5},{8,10},{9,11},{10,... | collective-permute-start | bytes 786440 | tf_op jit(solution)/shard_map/ppermute | solution.py:36
  60.4 3.6 %collective-permute-start.22 = (f32[8,128]{1,0:T(8,128)S(1)}, f32[8,128]{1,0:T(8,128)S(1)}, u32[]{:S(2)}, u32[]{:S(2)}) collective-permute-start(f32[8,128]{1,0:T(8,128)S(1)} %add_add_fusion), channel_id=1, source_target_pairs={{112,0},{0,16},{16,32},{32,48},{48,64},{64,80},{80,96},{96,112},{2... | collective-permute-start | bytes 12296 | tf_op jit(solution)/shard_map/ppermute | solution.py:53
  62.3 3.6 %collective-permute-start.21 = (f32[8,128]{1,0:T(8,128)S(1)}, f32[8,128]{1,0:T(8,128)S(1)}, u32[]{:S(2)}, u32[]{:S(2)}) collective-permute-start(f32[8,128]{1,0:T(8,128)S(1)} %add_add_fusion), channel_id=1, source_target_pairs={{16,0},{32,16},{48,32},{64,48},{80,64},{96,80},{112,96},{0,112},{1... | collective-permute-start | bytes 12296 | tf_op jit(solution)/shard_map/ppermute | solution.py:53
  68.2 8.6 %collective-permute-start.23 = (bf16[144,512]{1,0:T(8,128)(2,1)S(1)}, bf16[144,512]{1,0:T(8,128)(2,1)S(1)}, u32[]{:S(2)}, u32[]{:S(2)}) collective-permute-start(bf16[144,512]{1,0:T(8,128)(2,1)S(1)} %get-tuple-element.109), channel_id=1, source_target_pairs={{0,4},{1,5},{2,6},{3,7},{4,8},{5,9},{6,10},{7,11},{8,12},{9,13},{1... | collective-permute-start | bytes 442376 | tf_op jit(solution)/shard_map/ppermute | solution.py:36
  68.3 8.5 %collective-permute-start.24 = (bf16[144,512]{1,0:T(8,128)(2,1)S(1)}, bf16[144,512]{1,0:T(8,128)(2,1)S(1)}, u32[]{:S(2)}, u32[]{:S(2)}) collective-permute-start(bf16[144,512]{1,0:T(8,128)(2,1)S(1)} %get-tuple-element.110), channel_id=1, source_target_pairs={{0,8},{1,9},{2,10},{3,11},{4,12},{5,13},{6,14},{7,15},{8,0},{9,1},... | collective-permute-start | bytes 442376 | tf_op jit(solution)/shard_map/ppermute | solution.py:36
  70.3 7.1 %collective-permute-start.25 = (bf16[144,512]{1,0:T(8,128)(2,1)S(1)}, bf16[144,512]{1,0:T(8,128)(2,1)S(1)}, u32[]{:S(2)}, u32[]{:S(2)}) collective-permute-start(bf16[144,512]{1,0:T(8,128)(2,1)S(1)} %get-tuple-element.111), channel_id=1, source_target_pairs={{0,12},{1,13},{2,14},{3,15},{4,0},{5,1},{6,2},{7,3},{8,4},{9,5},{1... | collective-permute-start | bytes 442376 | tf_op jit(solution)/shard_map/ppermute | solution.py:36
  77.5 7.5 %collective-permute-start.27 = (f32[8,128]{1,0:T(8,128)S(1)}, f32[8,128]{1,0:T(8,128)S(1)}, u32[]{:S(2)}, u32[]{:S(2)}) collective-permute-start(f32[8,128]{1,0:T(8,128)S(1)} %shard_map.127.refs_0_), channel_id=1, source_target_pairs={{80,0},{96,16},{112,32},{0,48},{16,64},{32,80},{48,96},{64,112},{2... | collective-permute-start | bytes 12296 | tf_op jit(solution)/shard_map/ppermute | solution.py:53
  83.4 6.6 %collective-permute-start.26 = (f32[8,128]{1,0:T(8,128)S(1)}, f32[8,128]{1,0:T(8,128)S(1)}, u32[]{:S(2)}, u32[]{:S(2)}) collective-permute-start(f32[8,128]{1,0:T(8,128)S(1)} %shard_map.127.refs_0_), channel_id=1, source_target_pairs={{48,0},{64,16},{80,32},{96,48},{112,64},{0,80},{16,96},{32,112},{1... | collective-permute-start | bytes 12296 | tf_op jit(solution)/shard_map/ppermute | solution.py:53
